TPU v7x, 32 devices: a whole 2x2x4 slice. The times are simulated.
32 devices in a mesh: parts: 2 (over x), tensor: 16 (over z, y, core).
Axes of the slice: x: 2, y: 2, z: 4, core: 2. Of those that a mesh axis runs over, the one named last changes fastest.
Arguments:
- activations: bfloat16 [256, 8192], P(('parts', 'tensor')), parts along dimension 0, may hold values from -6 to 6
- out_grad: bfloat16 [256, 8192], P(('parts', 'tensor')), parts along dimension 0, may hold values from -6 to 6
- loss_mask: int32 [256], P(('parts', 'tensor')), parts along dimension 0, may hold values 0 or 1
- w_gate: bfloat16 [8192, 14336], P(None, 'tensor'), may hold values from -0.0625 to 0.0625
- w_down: bfloat16 [14336, 8192], P('tensor'), may hold values from -0.046875 to 0.046875
- basis_a: bfloat16 [8192, 8192], P('tensor'), may hold values from -0.0625 to 0.0625
- basis_g: bfloat16 [14336, 14336], P('tensor'), may hold values from -0.0625 to 0.0625
Outputs:
- eigenvalues: float32 [16384, 14336], P('parts', 'tensor'), parts along dimension 0
There are 2 independent parts, one for each index of `parts`. A program takes and returns all parts, laid end to end along the dimension named above; an argument that names none is the same for every part. Nothing has to cross between parts.
All inputs are finite; a program needn't handle non-finite values. No bound on the sum of `loss_mask` on one device may be relied on, other than what follows from the above.
Results may differ from a plain program's by a relative error of at most 0.0064.
Values may be sent and summed in bfloat16 or wider, within the bound.
No kernel may reach another device: no remote copies, remote signals or barrier semaphores. Data moves between devices by JAX's collectives and lax.ppermute only.
A program may use at most 256 MiB of HBM per device.

v0:
```python
import jax
import jax.numpy as jnp
from jax import lax
from jax.sharding import PartitionSpec as P

SEQS = 2
SEQ = 64


def on_device(activations, out_grad, loss_mask, w_gate, w_down, basis_a, basis_g):
    masked = out_grad * loss_mask.astype(out_grad.dtype)[:, None]
    whole_act, whole_grad = (
        lax.all_gather(activations, "tensor", axis=0, tiled=True),
        lax.all_gather(masked, "tensor", axis=0, tiled=True),
    )
    gate_pre = jnp.dot(whole_act, w_gate, preferred_element_type=jnp.float32)
    hid_grad = lax.dot_general(
        whole_grad, w_down, (((1,), (1,)), ((), ())), preferred_element_type=jnp.float32
    )
    up_grad = (hid_grad * jax.nn.silu(gate_pre)).astype(jnp.bfloat16)
    columns_a = lax.all_to_all(basis_a, "tensor", split_axis=1, concat_axis=0, tiled=True)
    share_a = jnp.dot(whole_act, columns_a, preferred_element_type=jnp.float32).astype(jnp.bfloat16)
    proj_a = lax.all_gather(share_a, "tensor", axis=1, tiled=True)
    own_units = basis_g.shape[0]
    proj_g_cols = lax.psum_scatter(
        lax.dot_general(
            basis_g, up_grad, (((0,), (1,)), ((), ())), preferred_element_type=jnp.float32
        ),
        "tensor",
        scatter_dimension=0,
        tiled=True,
    ).astype(jnp.bfloat16)
    total = jnp.zeros((proj_a.shape[1], own_units), jnp.float32)
    for which in range(SEQS):
        rows_a = proj_a[which * SEQ : (which + 1) * SEQ]
        rows_g = proj_g_cols[:, which * SEQ : (which + 1) * SEQ]
        product = lax.dot_general(
            rows_a, rows_g, (((0,), (1,)), ((), ())), preferred_element_type=jnp.float32
        )
        total = total + product * product
    return total / (SEQS * SEQ)


def solution(mesh):
    placed = (
        P(("parts", "tensor"), None),
        P(("parts", "tensor"), None),
        P(("parts", "tensor")),
        P(None, "tensor"),
        P("tensor", None),
        P("tensor", None),
        P("tensor", None),
    )
    return jax.shard_map(
        on_device, mesh=mesh, in_specs=placed, out_specs=P("parts", "tensor"), check_vma=False
    )
```

profile of v0, /device:TPU:0, one launch (start us, length us, event | category | flops | bytes accessed | tf_op | source)
XLA Modules:
  0.0 413.9 jit_solution(13197686959470194800)
XLA Ops:
  6.5 0.0 all-gather.4.cloned.1.call-start
  6.5 0.7 all-gather.4.cloned.1.call-update
  7.3 0.0 all-gather.8.cloned.1.call-start
  7.3 0.7 convert_element_type.13
  8.0 1.6 broadcast_multiply_fusion
  9.6 0.0 all-gather.8.cloned.1.call-update
  9.6 11.9 %copy.8 = bf16[512,8192]{0,1:T(8,128)(2,1)} copy(bf16[512,8192]{1,0:T(8,128)(2,1)} %param.12) | data formatting | bytes 16777216 | tf_op args[5]
  21.6 7.4 %all-to-all-start = ((bf16[512,16,512]{0,2,1:T(8,128)(2,1)}), bf16[512,16,512]{0,2,1:T(8,128)(2,1)}, u32[]{:S(2)}, u32[]{:S(2)}) async-start(bf16[512,16,512]{0,2,1:T(8,128)(2,1)} %bitcast.14), calls=%async_computation | async-start | bytes 16777216 | tf_op jit(solution)/shard_map/all_to_all | solution.py:21
  29.0 0.0 reduce-scatter.2.cloned.1.call-start
  29.1 64.3 %all-gather.4.cloned.1.call-done = bf16[128,8192]{1,0:T(8,128)(2,1)} async-done(((bf16[8,8192]{1,0:T(8,128)(2,1)}), bf16[128,8192]{1,0:T(8,128)(2,1)}) %all-gather.4.cloned.1.call-update) | async-done | bytes 2097168 | tf_op jit(solution)/shard_map/all_gather | solution.py:13
  93.4 8.2 %fusion.6 = f32[128,896]{1,0:T(8,128)S(1)} fusion(bf16[128,8192]{1,0:T(8,128)(2,1)} %all-gather.4.cloned.1.call-done, bf16[8192,896]{1,0:T(8,128)(2,1)} %param.10), kind=kOutput, calls=%fused_computation.11 | convolution fusion | flops 1879048192 | bytes 17235968 | tf_op jit(solution)/shard_map/dot_general | solution.py:16
  101.5 112.1 %all-gather.8.cloned.1.call-done = bf16[128,8192]{1,0:T(8,128)(2,1)} async-done(((bf16[8,8192]{1,0:T(8,128)(2,1)}), bf16[128,8192]{1,0:T(8,128)(2,1)}) %all-gather.8.cloned.1.call-update) | async-done | bytes 2097168 | tf_op jit(solution)/shard_map/all_gather | solution.py:14
  213.7 10.5 %fusion = bf16[128,896]{1,0:T(8,128)(2,1)S(1)} fusion(bf16[128,8192]{1,0:T(8,128)(2,1)} %all-gather.8.cloned.1.call-done, bf16[896,8192]{1,0:T(8,128)(2,1)} %param.11, f32[128,896]{1,0:T(8,128)S(1)} %fusion.6), kind=kOutput, calls=%fused_computation.3 | convolution fusion | flops 1879736320 | bytes 17465344 | tf_op jit(solution)/shard_map/dot_general | solution.py:17
  224.2 15.5 %convolution_bitcast_fusion = f32[14336,128]{0,1:T(8,128)} fusion(bf16[128,896]{1,0:T(8,128)(2,1)S(1)} %fusion, bf16[896,14336]{1,0:T(8,128)(2,1)} %param.13), kind=kOutput, calls=%fused_computation.1 | convolution fusion | flops 3288334336 | bytes 33259520 | tf_op jit(solution)/shard_map/dot_general | solution.py:26
  239.7 0.0 reduce-scatter.2.cloned.1.call-update
  239.8 0.2 all-gather.6.cloned.1.call-start
  240.0 0.0 all-to-all-done
  240.0 0.0 copy-start
  240.0 12.7 %copy.9 = bf16[16,512,512]{2,1,0:T(8,128)(2,1)} copy(bf16[16,512,512]{1,2,0:T(8,128)(2,1)} %bitcast.1) | data formatting | bytes 16777216 | tf_op jit(solution)/shard_map/all_to_all | solution.py:21
  252.7 0.0 copy-done
  252.7 6.0 %convolution_convert_fusion = bf16[128,512]{1,0:T(8,128)(2,1)} fusion(bf16[128,8192]{1,0:T(8,128)(2,1)S(1)} %copy-done, bf16[8192,512]{1,0:T(8,128)(2,1)} %bitcast.13), kind=kOutput, calls=%fused_computation.4 | convolution fusion | flops 1073807360 | bytes 10616832 | tf_op jit(solution)/shard_map/dot_general | solution.py:22
  258.7 0.0 all-gather.6.cloned.1.call-update
  258.7 70.5 %reduce-scatter.2.cloned.1.call-done = f32[896,128]{0,1:T(8,128)} async-done(((f32[14336,128]{0,1:T(8,128)}), f32[896,128]{0,1:T(8,128)}) %reduce-scatter.2.cloned.1.call-update) | async-done | bytes 458768 | tf_op jit(solution)/shard_map/reduce_scatter | solution.py:25
  329.2 1.0 convert_element_type.15
  330.3 41.9 %all-gather.6.cloned.1.call-done = bf16[128,8192]{1,0:T(8,128)(2,1)} async-done(((bf16[128,512]{1,0:T(8,128)(2,1)}), bf16[128,8192]{1,0:T(8,128)(2,1)}) %all-gather.6.cloned.1.call-update) | async-done | bytes 2097168 | tf_op jit(solution)/shard_map/all_gather | solution.py:23
  372.2 0.0 copy-start.1
  372.2 15.7 %fusion.2 = f32[8192,896]{1,0:T(8,128)} fusion(bf16[128,8192]{1,0:T(8,128)(2,1)} %all-gather.6.cloned.1.call-done, bf16[896,128]{0,1:T(8,128)(2,1)S(1)} %convert_element_type.15), kind=kOutput, calls=%fused_computation.6 | convolution fusion | flops 939524096 | bytes 30523392 | tf_op jit(solution)/shard_map/dot_general | solution.py:37
  387.9 0.0 copy-done.1
  387.9 19.5 %add_multiply_fusion = f32[8192,896]{1,0:T(8,128)} fusion(f32[8192,896]{1,0:T(8,128)} %fusion.2, bf16[128,8192]{1,0:T(8,128)(2,1)S(1)} %copy-done.1, bf16[896,128]{0,1:T(8,128)(2,1)S(1)} %convert_element_type.15), kind=kOutput, calls=%fused_computation | convolution fusion | flops 968884224 | bytes 59883520 | tf_op jit(solution)/shard_map/dot_general | solution.py:37
Async XLA Ops:
  6.5 86.8 %all-gather.4.cloned.1.call-start = ((), (), s32[]{:S(2)}) async-start(), calls=%async_computation.2 | async-start | bytes 2228224 | tf_op jit(solution)/shard_map/all_gather | solution.py:13
  7.3 206.4 %all-gather.8.cloned.1.call-start = ((), (), s32[]{:S(2)}) async-start(), calls=%async_computation.4 | async-start | bytes 2228224 | tf_op jit(solution)/shard_map/all_gather | solution.py:14
  21.6 218.4 %all-to-all-start = ((bf16[512,16,512]{0,2,1:T(8,128)(2,1)}), bf16[512,16,512]{0,2,1:T(8,128)(2,1)}, u32[]{:S(2)}, u32[]{:S(2)}) async-start(bf16[512,16,512]{0,2,1:T(8,128)(2,1)} %bitcast.14), calls=%async_computation | async-start | bytes 16777216 | tf_op jit(solution)/shard_map/all_to_all | solution.py:21
  29.0 300.2 %reduce-scatter.2.cloned.1.call-start = ((), (), s32[]{:S(2)}) async-start(), calls=%async_computation.5 | async-start | bytes 7798784 | tf_op jit(solution)/shard_map/reduce_scatter | solution.py:25
  239.8 132.4 %all-gather.6.cloned.1.call-start = ((), (), s32[]{:S(2)}) async-start(), calls=%async_computation.3 | async-start | bytes 2228224 | tf_op jit(solution)/shard_map/all_gather | solution.py:23
  240.0 12.7 %copy-start = (bf16[128,8192]{1,0:T(8,128)(2,1)S(1)}, bf16[128,8192]{1,0:T(8,128)(2,1)}, u32[]{:S(2)}) copy-start(bf16[128,8192]{1,0:T(8,128)(2,1)} %all-gather.4.cloned.1.call-done) | copy-start | bytes 6291460
  372.2 15.7 %copy-start.1 = (bf16[128,8192]{1,0:T(8,128)(2,1)S(1)}, bf16[128,8192]{1,0:T(8,128)(2,1)}, u32[]{:S(2)}) copy-start(bf16[128,8192]{1,0:T(8,128)(2,1)} %all-gather.6.cloned.1.call-done) | copy-start | bytes 6291460
Sparse Core Ops, SparseCore 0:
  9.5 83.7 all-gather.3
  95.5 118.0 all-gather.7
  239.9 89.2 reduce-scatter.1
  331.2 40.8 all-gather.5
where the time goes:
time: 415 us; the launch traced here: 414 us
  waiting for transfers between devices  290 us (70%)
  matrix products  75.5 us (18%)
  local copies, waits for them, and re-layouts  24.6 us (6%)
  between operations  13.2 us (3%)
  starting transfers between devices  7.74 us (2%)
    all_gather x1, waiting for transfers between devices, on_device(): lax.all_gather(masked, 'tensor', axis=0, tiled=True)  112 us
    reduce_scatter x1, waiting for transfers between devices, on_device(): lax.psum_scatter(lax.dot_general(basis_g, up_grad, (((0,), (1,)), ((), ()...  70.5 us
    all_gather x1, waiting for transfers between devices, on_device(): lax.all_gather(activations, 'tensor', axis=0, tiled=True)  64.3 us
    all_gather x1, waiting for transfers between devices, on_device(): proj_a = lax.all_gather(share_a, 'tensor', axis=1, tiled=True)  41.9 us
    dot_general x2, matrix products, on_device(): lax.dot_general(rows_a, rows_g, (((0,), (1,)), ((), ())), preferred_eleme...  35.2 us
    dot_general x1, matrix products, on_device(): lax.dot_general(basis_g, up_grad, (((0,), (1,)), ((), ())), preferred_ele...  15.5 us
    all_to_all x1, local copies, waits for them, and re-layouts, on_device(): lax.all_to_all(basis_a, 'tensor', split_axis=1, concat_axis=0, tiled=True)  12.7 us
    unnamed x5, local copies, waits for them, and re-layouts  12 us
  transfers between devices with their start and end apart: 5, of which 4 were waited for; matrix products, arithmetic and copies ran while one was open for 16% of the time, Pallas kernels for 0%

commit v1 on v0

v1 whole, which is shorter than its diff:
```python
import functools

import jax
import jax.numpy as jnp
from jax import lax
from jax.experimental import pallas as pl
from jax.experimental.pallas import tpu as pltpu
from jax.sharding import Mesh
from jax.sharding import PartitionSpec as P

SEQS = 2
F32 = jnp.float32
BF16 = jnp.bfloat16
VMEM_LIMIT = 48 * 1024 * 1024


def params():
    return pltpu.CompilerParams(vmem_limit_bytes=VMEM_LIMIT)


def plain(activations, out_grad, loss_mask, w_gate, w_down, basis_a, basis_g):
    axes = ("z", "y", "core")
    masked = out_grad * loss_mask.astype(out_grad.dtype)[:, None]
    whole_act = lax.all_gather(activations, axes, axis=0, tiled=True)
    whole_grad = lax.all_gather(masked, axes, axis=0, tiled=True)
    gate_pre = jnp.dot(whole_act, w_gate, preferred_element_type=F32)
    hid_grad = lax.dot_general(
        whole_grad, w_down, (((1,), (1,)), ((), ())), preferred_element_type=F32
    )
    up_grad = (hid_grad * jax.nn.silu(gate_pre)).astype(BF16)
    depth = basis_a.shape[0]
    own_act = lax.dynamic_slice_in_dim(whole_act, lax.axis_index(axes) * depth, depth, axis=1)
    share_a = lax.psum_scatter(
        jnp.dot(own_act, basis_a, preferred_element_type=F32),
        axes,
        scatter_dimension=1,
        tiled=True,
    ).astype(BF16)
    proj_a = lax.all_gather(share_a, axes, axis=1, tiled=True)
    proj_g_cols = lax.psum_scatter(
        lax.dot_general(basis_g, up_grad, (((0,), (1,)), ((), ())), preferred_element_type=F32),
        axes,
        scatter_dimension=0,
        tiled=True,
    ).astype(BF16)
    tokens = proj_a.shape[0]
    seq = tokens // SEQS
    total = 0.0
    for which in range(SEQS):
        rows = slice(which * seq, (which + 1) * seq)
        product = lax.dot_general(
            proj_a[rows],
            proj_g_cols[:, rows],
            (((0,), (1,)), ((), ())),
            preferred_element_type=F32,
        )
        total = total + product * product
    return total / tokens


def assemble(place, pieces, whole):
    part = pieces[0].shape[0] // SEQS
    for other in range(2):
        for across in range(2):
            core = (place[2] + other) % 2
            y = (place[1] + across) % 2
            for which in range(SEQS):
                start = ((which * 2 + core) * 2 + y) * part
                whole[pl.ds(pl.multiple_of(start, part), part), :] = pieces[other * 2 + across][
                    which * part : (which + 1) * part, :
                ]


def gate_kernel(place, p0, p1, p2, p3, weight, out, whole):
    assemble(place, (p0, p1, p2, p3), whole)
    product = jnp.dot(whole[...], weight[...], preferred_element_type=F32)

    @pl.when(pl.program_id(0) == 0)
    def _():
        out[...] = product

    @pl.when(pl.program_id(0) > 0)
    def _():
        out[...] += product


def gate_product(place, pieces, weight, step):
    rows, depth = pieces[0].shape
    width = weight.shape[1]
    return pl.pallas_call(
        gate_kernel,
        grid_spec=pltpu.PrefetchScalarGridSpec(
            num_scalar_prefetch=1,
            grid=(depth // step,),
            in_specs=[pl.BlockSpec((rows, step), lambda k, s: (0, k))] * 4
            + [pl.BlockSpec((step, width), lambda k, s: (k, 0))],
            out_specs=pl.BlockSpec((4 * rows, width), lambda k, s: (0, 0)),
            scratch_shapes=[pltpu.VMEM((4 * rows, step), BF16)],
        ),
        out_shape=jax.ShapeDtypeStruct((4 * rows, width), F32),
        compiler_params=params(),
        name="gate",
    )(place, *pieces, weight)


def down_kernel(place, p0, p1, p2, p3, weight, gate, out, whole, total):
    assemble(place, (p0, p1, p2, p3), whole)
    product = lax.dot_general(
        whole[...], weight[...], (((1,), (1,)), ((), ())), preferred_element_type=F32
    )

    @pl.when(pl.program_id(0) == 0)
    def _():
        total[...] = product

    @pl.when(pl.program_id(0) > 0)
    def _():
        total[...] += product

    @pl.when(pl.program_id(0) == pl.num_programs(0) - 1)
    def _():
        pre = gate[...]
        out[...] = (total[...] * (pre / (1.0 + jnp.exp(-pre)))).astype(out.dtype)


def down_product(place, pieces, weight, gate, step):
    rows, depth = pieces[0].shape
    width = weight.shape[0]
    return pl.pallas_call(
        down_kernel,
        grid_spec=pltpu.PrefetchScalarGridSpec(
            num_scalar_prefetch=1,
            grid=(depth // step,),
            in_specs=[pl.BlockSpec((rows, step), lambda k, s: (0, k))] * 4
            + [
                pl.BlockSpec((width, step), lambda k, s: (0, k)),
                pl.BlockSpec((4 * rows, width), lambda k, s: (0, 0)),
            ],
            out_specs=pl.BlockSpec((4 * rows, width), lambda k, s: (0, 0)),
            scratch_shapes=[
                pltpu.VMEM((4 * rows, step), BF16),
                pltpu.VMEM((4 * rows, width), F32),
            ],
        ),
        out_shape=jax.ShapeDtypeStruct((4 * rows, width), BF16),
        compiler_params=params(),
        name="down",
    )(place, *pieces, weight, gate)


def share_a_kernel(place, p0, p1, p2, p3, basis, out, whole):
    @pl.when(pl.program_id(0) == 0)
    def _():
        assemble(place, (p0, p1, p2, p3), whole)

    out[0] = jnp.dot(whole[...], basis[...], preferred_element_type=F32).astype(out.dtype)


def share_a(place, pieces, basis, chips, flip, kind):
    rows = pieces[0].shape[0]
    depth, columns = basis.shape
    block = columns // (2 * chips)
    return pl.pallas_call(
        share_a_kernel,
        grid_spec=pltpu.PrefetchScalarGridSpec(
            num_scalar_prefetch=1,
            grid=(chips,),
            in_specs=[pl.BlockSpec((rows, depth), lambda j, s: (0, s[3]))] * 4
            + [pl.BlockSpec((depth, block), lambda j, s: (0, (s[2] + flip) % 2 * chips + j))],
            out_specs=pl.BlockSpec((1, 4 * rows, block), lambda j, s: (j, 0, 0)),
            scratch_shapes=[pltpu.VMEM((4 * rows, depth), BF16)],
        ),
        out_shape=jax.ShapeDtypeStruct((chips, 4 * rows, block), kind),
        compiler_params=params(),
        name="share_a",
    )(place, *pieces, basis)


def share_g_kernel(place, up, basis, out):
    out[0] = jnp.dot(up[...], basis[...], preferred_element_type=F32).astype(out.dtype)


def share_g(place, up, basis, chips, flip, kind):
    tokens, depth = up.shape
    block = basis.shape[1] // (2 * chips)
    return pl.pallas_call(
        share_g_kernel,
        grid_spec=pltpu.PrefetchScalarGridSpec(
            num_scalar_prefetch=1,
            grid=(chips,),
            in_specs=[
                pl.BlockSpec((tokens, depth), lambda j, s: (0, 0)),
                pl.BlockSpec((depth, block), lambda j, s: (0, 2 * j + (s[2] + flip) % 2)),
            ],
            out_specs=pl.BlockSpec((1, tokens, block), lambda j, s: (j, 0, 0)),
        ),
        out_shape=jax.ShapeDtypeStruct((chips, tokens, block), kind),
        compiler_params=params(),
        name="share_g",
    )(place, up, basis)


def final_kernel(layers, place, a0, a1, a2, a3, g, out):
    step = pl.program_id(0)
    tokens = g.shape[0]
    seq = tokens // SEQS
    for which, ref in enumerate((a0, a1, a2, a3)):

        @pl.when(step // layers == which)
        def _(ref=ref):
            block = ref[lax.rem(step, layers)]
            total = None
            for s in range(SEQS):
                rows = slice(s * seq, (s + 1) * seq)
                product = lax.dot_general(
                    block[rows],
                    g[rows, :],
                    (((0,), (0,)), ((), ())),
                    preferred_element_type=F32,
                )
                total = product * product if total is None else total + product * product
            out[...] = total * (1.0 / tokens)


def final_product(place, pieces, g):
    layers, tokens, block = pieces[0].shape
    width = g.shape[1]

    def where(j, s):
        piece = j // layers
        core = (s[2] + piece // 2) % 2
        y = (s[1] + piece) % 2
        return ((core * layers + j % layers) * 2 + y, 0)

    return pl.pallas_call(
        functools.partial(final_kernel, layers),
        grid_spec=pltpu.PrefetchScalarGridSpec(
            num_scalar_prefetch=1,
            grid=(4 * layers,),
            in_specs=[pl.BlockSpec((layers, tokens, block), lambda j, s: (0, 0, 0))] * 4
            + [pl.BlockSpec((tokens, width), lambda j, s: (0, 0))],
            out_specs=pl.BlockSpec((block, width), where),
        ),
        out_shape=jax.ShapeDtypeStruct((4 * layers * block, width), F32),
        compiler_params=params(),
        name="final",
    )(place, *pieces, g)


def turn(value, axis, size, by):
    return lax.ppermute(value, axis, [(i, (i + by) % size) for i in range(size)])


def gather(value, z, layers):
    pieces = [value] + [turn(value, "z", layers, by) for by in range(1, layers)]
    mine = jnp.stack([lax.select_n((z - i) % layers, *pieces) for i in range(layers)])
    across = turn(mine, "y", 2, 1)
    return mine, across, turn(mine, "core", 2, 1), turn(across, "core", 2, 1)


def pick(value, which):
    return lax.dynamic_index_in_dim(value, which, 0, keepdims=False)


def reduce_blocks(kept, got, z, y, layers):
    shape = (layers, 2) + kept.shape[1:]
    kept, got = kept.reshape(shape), got.reshape(shape)

    def both(which):
        return lax.dynamic_index_in_dim(kept, which, 1, keepdims=False) + (
            lax.dynamic_index_in_dim(got, which, 1, keepdims=False).astype(F32)
        )

    total = both(y) + turn(both(1 - y).astype(BF16), "y", 2, 1).astype(F32)
    own = pick(total, z)
    for by in range(1, layers):
        own = own + turn(pick(total, (z + by) % layers).astype(BF16), "z", layers, by).astype(F32)
    return own.astype(BF16)


def on_device(layers, activations, out_grad, loss_mask, w_gate, w_down, basis_a, basis_g):
    z, y, core = (lax.axis_index(name) for name in ("z", "y", "core"))
    chips = 2 * layers
    place = jnp.stack([z, y, core, lax.axis_index(("z", "y", "core"))]).astype(jnp.int32)
    masked = out_grad * loss_mask.astype(out_grad.dtype)[:, None]

    def flat(stacks):
        return [s.reshape(-1, s.shape[-1]) for s in stacks]

    act = flat(gather(activations, z, layers))
    grad = flat(gather(masked, z, layers))
    sent_a = share_a(place, act, basis_a, chips, 1, BF16)
    kept_a = share_a(place, act, basis_a, chips, 0, F32)
    own_a = reduce_blocks(kept_a, turn(sent_a, "core", 2, 1), z, y, layers)
    proj_a = gather(own_a, z, layers)
    gate = gate_product(place, act, w_gate, 1024)
    up = down_product(place, grad, w_down, gate, 1024)
    sent_g = share_g(place, up, basis_g, chips, 1, BF16)
    kept_g = share_g(place, up, basis_g, chips, 0, F32)
    own_g = reduce_blocks(kept_g, turn(sent_g, "core", 2, 1), z, y, layers)
    return final_product(place, proj_a, own_g)


def solution(mesh):
    tensor = mesh.shape["tensor"]
    chips = tensor // 2
    across = max(d for d in range(1, chips + 1) if chips % d == 0 and d * d <= chips)
    layers = chips // across
    fine = Mesh(
        mesh.devices.reshape(mesh.shape["parts"], layers, across, 2), ("parts", "z", "y", "core")
    )
    t = ("z", "y", "core")
    placed = (
        P(("parts",) + t, None),
        P(("parts",) + t, None),
        P(("parts",) + t),
        P(None, t),
        P(t, None),
        P(t, None),
        P(t, None),
    )

    def step(*args):
        rows = args[0].shape[0] // (mesh.shape["parts"] * tensor)
        small = across == 2 and layers * rows // SEQS == 16
        body = functools.partial(on_device, layers) if small else plain
        return jax.shard_map(
            body, mesh=fine, in_specs=placed, out_specs=P("parts", t), check_vma=False
        )(*args)

    return step
```

time: 415 us -> 202 us (0.49)
  waiting for transfers between devices: 290 us -> 75.2 us
  matrix products: 75.5 us -> 0 us
  Pallas kernels: 0 us -> 69.7 us
  starting transfers between devices: 7.74 us -> 43.7 us
  local copies, waits for them, and re-layouts: 24.6 us -> 2.24 us
  between operations: 13.2 us -> 0.21 us
  other arithmetic: 3.33 us -> 9.6 us
    all_gather x3 -> x0, waiting for transfers between devices: 218 us -> none  [the longest x1 112 us: on_device(): lax.all_gather(masked, 'tensor', axis=0, tiled=True)]
    dot_general x6 -> x0, matrix products: 75.5 us -> none  [the longest x2 35.2 us: on_device(): lax.dot_general(rows_a, rows_g, (((0,), (1,)), ((), ())), preferred_eleme...]
    ppermute x0 -> x28, waiting for transfers between devices: none -> 75.2 us  [turn(): lax.ppermute(value, axis, [(i, (i + by) % size) for i in range(size)])]
    reduce_scatter x1 -> x0, waiting for transfers between devices: 70.5 us -> none  [on_device(): lax.psum_scatter(lax.dot_general(basis_g, up_grad, (((0,), (1,)), ((), ()...]
    pallas_call x0 -> x7, Pallas kernels: none -> 69.7 us  [the longest x2 18.9 us: share_g(): pl.pallas_call(share_g_kernel, grid_spec=pltpu.PrefetchScalarGridSpec(num...]
    ppermute x0 -> x28, starting transfers between devices: none -> 43.7 us  [turn(): lax.ppermute(value, axis, [(i, (i + by) % size) for i in range(size)])]
    all_to_all x1 -> x0, local copies, waits for them, and re-layouts: 12.7 us -> none  [on_device(): lax.all_to_all(basis_a, 'tensor', split_axis=1, concat_axis=0, tiled=True)]
    unnamed x5 -> x10, local copies, waits for them, and re-layouts: 12 us -> 2.09 us
  transfers between devices with their start and end apart: 5 -> 28, of which waited for: 4 -> 11; matrix products, arithmetic and copies ran while one was open for 16% -> 5% of each run, Pallas kernels for 0% -> 26%
where the time goes in v1:
time: 202 us; the launch traced here: 201 us
  waiting for transfers between devices  75.2 us (37%)
  Pallas kernels  69.7 us (35%)
  starting transfers between devices  43.7 us (22%)
  other arithmetic  9.6 us (5%)
  local copies, waits for them, and re-layouts  2.24 us (1%)
    ppermute x28, waiting for transfers between devices, turn(): lax.ppermute(value, axis, [(i, (i + by) % size) for i in range(size)])  75.2 us
    ppermute x28, starting transfers between devices, turn(): lax.ppermute(value, axis, [(i, (i + by) % size) for i in range(size)])  43.7 us
    pallas_call x2, Pallas kernels, share_g(): pl.pallas_call(share_g_kernel, grid_spec=pltpu.PrefetchScalarGridSpec(num...  18.9 us
    pallas_call x1, Pallas kernels, final_product(): pl.pallas_call(functools.partial(final_kernel, layers), grid_spec=pltpu.P...  16.7 us
    pallas_call x2, Pallas kernels, share_a(): pl.pallas_call(share_a_kernel, grid_spec=pltpu.PrefetchScalarGridSpec(num...  13.4 us
    pallas_call x1, Pallas kernels, down_product(): pl.pallas_call(down_kernel, grid_spec=pltpu.PrefetchScalarGridSpec(num_sc...  11 us
    pallas_call x1, Pallas kernels, gate_product(): pl.pallas_call(gate_kernel, grid_spec=pltpu.PrefetchScalarGridSpec(num_sc...  9.65 us
  transfers between devices with their start and end apart: 28, of which 11 were waited for; matrix products, arithmetic and copies ran while one was open for 5% of the time, Pallas kernels for 26%

profile of v1, /device:TPU:0, one launch (start us, length us, event | category | flops | bytes accessed | tf_op | source)
XLA Modules:
  0.0 200.6 jit_solution(11990032363301090093)
XLA Ops:
  0.0 3.0 %collective-permute-start = (bf16[8,8192]{1,0:T(8,128)(2,1)}, bf16[8,8192]{1,0:T(8,128)(2,1)S(1)}, u32[]{:S(2)}, u32[]{:S(2)}) collective-permute-start(bf16[8,8192]{1,0:T(8,128)(2,1)} %param.7), channel_id=1, source_target_pairs={{0,4},{4,8},{8,12},{12,0},{1,5},{5,9},{9,13},{13,1},{2,6},{6,10},{... | collective-permute-start | bytes 393224 | tf_op jit(solution)/shard_map/ppermute | solution.py:251
  3.0 2.6 %collective-permute-start.1 = (bf16[8,8192]{1,0:T(8,128)(2,1)}, bf16[8,8192]{1,0:T(8,128)(2,1)S(1)}, u32[]{:S(2)}, u32[]{:S(2)}) collective-permute-start(bf16[8,8192]{1,0:T(8,128)(2,1)} %param.7), channel_id=1, source_target_pairs={{0,8},{4,12},{8,0},{12,4},{1,9},{5,13},{9,1},{13,5},{2,10},{6,14},... | collective-permute-start | bytes 393224 | tf_op jit(solution)/shard_map/ppermute | solution.py:251
  8.9 2.9 %collective-permute-start.19 = (bf16[8,8192]{1,0:T(8,128)(2,1)S(1)}, bf16[8,8192]{1,0:T(8,128)(2,1)S(1)}, u32[]{:S(2)}, u32[]{:S(2)}) collective-permute-start(bf16[8,8192]{1,0:T(8,128)(2,1)S(1)} %broadcast_multiply_fusion), channel_id=1, source_target_pairs={{0,12},{4,0},{8,4},{12,8},{1,13},{5,1},{9,5},{13,9},{2,14},{6,2},{... | collective-permute-start | bytes 393224 | tf_op jit(solution)/shard_map/ppermute | solution.py:251
  11.7 8.1 %collective-permute-start.17 = (bf16[8,8192]{1,0:T(8,128)(2,1)S(1)}, bf16[8,8192]{1,0:T(8,128)(2,1)S(1)}, u32[]{:S(2)}, u32[]{:S(2)}) collective-permute-start(bf16[8,8192]{1,0:T(8,128)(2,1)S(1)} %broadcast_multiply_fusion), channel_id=1, source_target_pairs={{0,4},{4,8},{8,12},{12,0},{1,5},{5,9},{9,13},{13,1},{2,6},{6,10},{... | collective-permute-start | bytes 393224 | tf_op jit(solution)/shard_map/ppermute | solution.py:251
  20.9 1.6 collective-permute-start.3
  22.5 3.3 %collective-permute-done.18 = bf16[8,8192]{1,0:T(8,128)(2,1)S(1)} collective-permute-done((bf16[8,8192]{1,0:T(8,128)(2,1)S(1)}, bf16[8,8192]{1,0:T(8,128)(2,1)S(1)}, u32[]{:S(2)}, u32[]{:S(2)}) %collective-permute-start.18) | collective-permute-done | bytes 131104 | tf_op jit(solution)/shard_map/ppermute | solution.py:251
  25.9 4.2 %collective-permute-done.3 = bf16[4,8,8192]{2,1,0:T(8,128)(2,1)S(1)} collective-permute-done((bf16[4,8,8192]{2,1,0:T(8,128)(2,1)S(1)}, bf16[4,8,8192]{2,1,0:T(8,128)(2,1)S(1)}, u32[]{:S(2)}, u32[]{:S(2)}) %collective-permute-start.3) | collective-permute-done | bytes 524320 | tf_op jit(solution)/shard_map/ppermute | solution.py:251
  31.0 1.7 collective-permute-start.20
  32.8 7.2 %share_a.3 = bf16[8,128,512]{2,1,0:T(8,128)(2,1)} custom-call(s32[4]{0:T(128)S(1)} %pad_add_fusion.place, bf16[32,8192]{1,0:T(8,128)(2,1)S(1)} %get-tuple-element.22.p0, bf16[32,8192]{1,0:T(8,128)(2,1)S(1)} %bitcast.118, bf16[32,8192]{1,0:T(8,128)(2,1)S(1)} %bitcast.121, bf16[32,8192]{1,0:T(8,128)(2,1)S(1)} %bitcast.124, bf16[512,8192]{1,0:T(8,128)(2,1)} %basis.5), custom_call_target="tpu_custom_call" | custom-call | tf_op jit(solution)/shard_map/share_a/pallas_call | solution.py:163
  40.5 5.1 %collective-permute-done.20 = bf16[4,8,8192]{2,1,0:T(8,128)(2,1)} collective-permute-done((bf16[4,8,8192]{2,1,0:T(8,128)(2,1)}, bf16[4,8,8192]{2,1,0:T(8,128)(2,1)}, u32[]{:S(2)}, u32[]{:S(2)}) %collective-permute-start.20) | collective-permute-done | bytes 524320 | tf_op jit(solution)/shard_map/ppermute | solution.py:251
  45.7 9.6 %gate.1 = f32[128,896]{1,0:T(8,128)S(1)} custom-call(s32[4]{0:T(128)S(1)} %pad_add_fusion.place, bf16[32,8192]{1,0:T(8,128)(2,1)S(1)} %get-tuple-element.22.p0, bf16[32,8192]{1,0:T(8,128)(2,1)S(1)} %bitcast.119, bf16[32,8192]{1,0:T(8,128)(2,1)S(1)} %bitcast.122, bf16[32,8192]{1,0:T(8,128)(2,1)S(1)} %bitcast.125, bf16[8192,896]{1,0:T(8,128)(2,1)} %weight.2), custom_call_target="tpu_custom_call" | custom-call | tf_op jit(solution)/shard_map/gate/pallas_call | solution.py:90
  55.4 11.0 %down.1.up = bf16[128,896]{1,0:T(8,128)(2,1)S(1)} custom-call(s32[4]{0:T(128)S(1)} %pad_add_fusion.place, bf16[32,8192]{1,0:T(8,128)(2,1)S(1)} %get-tuple-element.12.p0, bf16[32,8192]{1,0:T(8,128)(2,1)} %bitcast.29.p1, bf16[32,8192]{1,0:T(8,128)(2,1)S(1)} %bitcast.127, bf16[32,8192]{1,0:T(8,128)(2,1)S(1)} %bitcast.128, bf16[896,8192]{1,0:T(8,128)(2,1)} %weight.3, ...), custom_call_target="tpu_custom_call" | custom-call | tf_op jit(solution)/shard_map/down/pallas_call | solution.py:129
  66.4 10.0 %share_g.3 = bf16[8,128,896]{2,1,0:T(8,128)(2,1)} custom-call(s32[4]{0:T(128)S(1)} %pad_add_fusion.place, bf16[128,896]{1,0:T(8,128)(2,1)S(1)} %down.1.up, bf16[896,14336]{1,0:T(8,128)(2,1)} %basis.7), custom_call_target="tpu_custom_call" | custom-call | tf_op jit(solution)/shard_map/share_g/pallas_call | solution.py:186
  78.9 6.2 %share_a.2 = f32[8,128,512]{2,1,0:T(8,128)S(1)} custom-call(s32[4]{0:T(128)S(1)} %pad_add_fusion.place, bf16[32,8192]{1,0:T(8,128)(2,1)S(1)} %get-tuple-element.22.p0, bf16[32,8192]{1,0:T(8,128)(2,1)S(1)} %bitcast.120, bf16[32,8192]{1,0:T(8,128)(2,1)S(1)} %bitcast.123, bf16[32,8192]{1,0:T(8,128)(2,1)S(1)} %bitcast.126, bf16[512,8192]{1,0:T(8,128)(2,1)} %basis.5), custom_call_target="tpu_custom_call" | custom-call | tf_op jit(solution)/shard_map/share_a/pallas_call | solution.py:163
  86.3 1.7 collective-permute-start.7
  88.1 12.3 %collective-permute-done.7 = bf16[4,128,512]{2,1,0:T(8,128)(2,1)} collective-permute-done((bf16[4,128,512]{2,1,0:T(8,128)(2,1)S(1)}, bf16[4,128,512]{2,1,0:T(8,128)(2,1)}, u32[]{:S(2)}, u32[]{:S(2)}) %collective-permute-start.7) | collective-permute-done | bytes 524320 | tf_op jit(solution)/shard_map/ppermute | solution.py:251
  100.4 1.4 fusion.5
  101.9 6.2 %collective-permute-start.8 = (bf16[128,512]{1,0:T(8,128)(2,1)S(1)}, bf16[128,512]{1,0:T(8,128)(2,1)S(1)}, u32[]{:S(2)}, u32[]{:S(2)}) collective-permute-start(bf16[128,512]{1,0:T(8,128)(2,1)S(1)} %get-tuple-element.8), channel_id=1, source_target_pairs={{0,4},{4,8},{8,12},{12,0},{1,5},{5,9},{9,13},{13,1},{2,6},{6,10},{... | collective-permute-start | bytes 393224 | tf_op jit(solution)/shard_map/ppermute | solution.py:251
  108.0 2.2 %collective-permute-start.10 = (bf16[128,512]{1,0:T(8,128)(2,1)S(1)}, bf16[128,512]{1,0:T(8,128)(2,1)S(1)}, u32[]{:S(2)}, u32[]{:S(2)}) collective-permute-start(bf16[128,512]{1,0:T(8,128)(2,1)S(1)} %get-tuple-element.9), channel_id=1, source_target_pairs={{0,12},{4,0},{8,4},{12,8},{1,13},{5,1},{9,5},{13,9},{2,14},{6,2},{... | collective-permute-start | bytes 393224 | tf_op jit(solution)/shard_map/ppermute | solution.py:251
  110.7 8.9 %share_g.2 = f32[8,128,896]{2,1,0:T(8,128)S(1)} custom-call(s32[4]{0:T(128)S(1)} %pad_add_fusion.place, bf16[128,896]{1,0:T(8,128)(2,1)S(1)} %down.1.up, bf16[896,14336]{1,0:T(8,128)(2,1)} %basis.7), custom_call_target="tpu_custom_call" | custom-call | tf_op jit(solution)/shard_map/share_g/pallas_call | solution.py:186
  119.7 1.7 collective-permute-done.9
  125.6 1.6 collective-permute-start.24
  127.4 7.2 %collective-permute-done.12 = bf16[128,512]{1,0:T(8,128)(2,1)S(1)} collective-permute-done((bf16[128,512]{1,0:T(8,128)(2,1)S(1)}, bf16[128,512]{1,0:T(8,128)(2,1)S(1)}, u32[]{:S(2)}, u32[]{:S(2)}) %collective-permute-start.12) | collective-permute-done | bytes 131104 | tf_op jit(solution)/shard_map/ppermute | solution.py:251
  134.8 1.6 collective-permute-start.14
  136.4 21.2 %collective-permute-done.14.a1 = bf16[4,128,512]{2,1,0:T(8,128)(2,1)S(1)} collective-permute-done((bf16[4,128,512]{2,1,0:T(8,128)(2,1)S(1)}, bf16[4,128,512]{2,1,0:T(8,128)(2,1)S(1)}, u32[]{:S(2)}, u32[]{:S(2)}) %collective-permute-start.14) | collective-permute-done | bytes 524320 | tf_op jit(solution)/shard_map/ppermute | solution.py:251
  157.6 1.5 fusion.2
  159.1 1.7 collective-permute-start.25
  160.8 2.2 %collective-permute-start.27 = (bf16[128,896]{1,0:T(8,128)(2,1)S(1)}, bf16[128,896]{1,0:T(8,128)(2,1)S(1)}, u32[]{:S(2)}, u32[]{:S(2)}) collective-permute-start(bf16[128,896]{1,0:T(8,128)(2,1)S(1)} %get-tuple-element.6), channel_id=1, source_target_pairs={{0,12},{4,0},{8,4},{12,8},{1,13},{5,1},{9,5},{13,9},{2,14},{6,2},{... | collective-permute-start | bytes 688136 | tf_op jit(solution)/shard_map/ppermute | solution.py:251
  163.9 5.6 %collective-permute-done.25 = bf16[128,896]{1,0:T(8,128)(2,1)S(1)} collective-permute-done((bf16[128,896]{1,0:T(8,128)(2,1)S(1)}, bf16[128,896]{1,0:T(8,128)(2,1)S(1)}, u32[]{:S(2)}, u32[]{:S(2)}) %collective-permute-start.25) | collective-permute-done | bytes 229408 | tf_op jit(solution)/shard_map/ppermute | solution.py:251
  169.4 4.0 %collective-permute-done.27 = bf16[128,896]{1,0:T(8,128)(2,1)S(1)} collective-permute-done((bf16[128,896]{1,0:T(8,128)(2,1)S(1)}, bf16[128,896]{1,0:T(8,128)(2,1)S(1)}, u32[]{:S(2)}, u32[]{:S(2)}) %collective-permute-start.27) | collective-permute-done | bytes 229408 | tf_op jit(solution)/shard_map/ppermute | solution.py:251
  173.5 10.3 %collective-permute-done.26 = bf16[128,896]{1,0:T(8,128)(2,1)S(1)} collective-permute-done((bf16[128,896]{1,0:T(8,128)(2,1)S(1)}, bf16[128,896]{1,0:T(8,128)(2,1)S(1)}, u32[]{:S(2)}, u32[]{:S(2)}) %collective-permute-start.26) | collective-permute-done | bytes 229408 | tf_op jit(solution)/shard_map/ppermute | solution.py:251
  183.9 16.7 %final.1 = f32[8192,896]{1,0:T(8,128)} custom-call(s32[4]{0:T(128)S(1)} %pad_add_fusion.place, bf16[4,128,512]{2,1,0:T(8,128)(2,1)S(1)} %pad_maximum_fusion.1.a0, bf16[4,128,512]{2,1,0:T(8,128)(2,1)S(1)} %collective-permute-done.14.a1, bf16[4,128,512]{2,1,0:T(8,128)(2,1)S(1)} %collective-permute-done.15.a2, ...), custom_call_target="tpu_custom_call" | custom-call | tf_op jit(solution)/shard_map/final/pallas_call | solution.py:235
  (58 shorter events, 15.9 us)
Async XLA Ops:
  0.0 25.8 %copy-start.4 = (bf16[8,8192]{1,0:T(8,128)(2,1)S(1)}, bf16[8,8192]{1,0:T(8,128)(2,1)}, u32[]{:S(2)}) copy-start(bf16[8,8192]{1,0:T(8,128)(2,1)} %param.8) | copy-start | bytes 393220
  0.0 11.7 %collective-permute-start = (bf16[8,8192]{1,0:T(8,128)(2,1)}, bf16[8,8192]{1,0:T(8,128)(2,1)S(1)}, u32[]{:S(2)}, u32[]{:S(2)}) collective-permute-start(bf16[8,8192]{1,0:T(8,128)(2,1)} %param.7), channel_id=1, source_target_pairs={{0,4},{4,8},{8,12},{12,0},{1,5},{5,9},{9,13},{13,1},{2,6},{6,10},{... | collective-permute-start | bytes 393224 | tf_op jit(solution)/shard_map/ppermute | solution.py:251
  3.0 16.8 %collective-permute-start.1 = (bf16[8,8192]{1,0:T(8,128)(2,1)}, bf16[8,8192]{1,0:T(8,128)(2,1)S(1)}, u32[]{:S(2)}, u32[]{:S(2)}) collective-permute-start(bf16[8,8192]{1,0:T(8,128)(2,1)} %param.7), channel_id=1, source_target_pairs={{0,8},{4,12},{8,0},{12,4},{1,9},{5,13},{9,1},{13,5},{2,10},{6,14},... | collective-permute-start | bytes 393224 | tf_op jit(solution)/shard_map/ppermute | solution.py:251
  5.6 14.2 %collective-permute-start.2 = (bf16[8,8192]{1,0:T(8,128)(2,1)}, bf16[8,8192]{1,0:T(8,128)(2,1)S(1)}, u32[]{:S(2)}, u32[]{:S(2)}) collective-permute-start(bf16[8,8192]{1,0:T(8,128)(2,1)} %param.7), channel_id=1, source_target_pairs={{0,12},{4,0},{8,4},{12,8},{1,13},{5,1},{9,5},{13,9},{2,14},{6,2},{... | collective-permute-start | bytes 393224 | tf_op jit(solution)/shard_map/ppermute | solution.py:251
  8.6 17.1 %collective-permute-start.18 = (bf16[8,8192]{1,0:T(8,128)(2,1)S(1)}, bf16[8,8192]{1,0:T(8,128)(2,1)S(1)}, u32[]{:S(2)}, u32[]{:S(2)}) collective-permute-start(bf16[8,8192]{1,0:T(8,128)(2,1)S(1)} %broadcast_multiply_fusion), channel_id=1, source_target_pairs={{0,8},{4,12},{8,0},{12,4},{1,9},{5,13},{9,1},{13,5},{2,10},{6,14},... | collective-permute-start | bytes 393224 | tf_op jit(solution)/shard_map/ppermute | solution.py:251
  8.9 16.9 %collective-permute-start.19 = (bf16[8,8192]{1,0:T(8,128)(2,1)S(1)}, bf16[8,8192]{1,0:T(8,128)(2,1)S(1)}, u32[]{:S(2)}, u32[]{:S(2)}) collective-permute-start(bf16[8,8192]{1,0:T(8,128)(2,1)S(1)} %broadcast_multiply_fusion), channel_id=1, source_target_pairs={{0,12},{4,0},{8,4},{12,8},{1,13},{5,1},{9,5},{13,9},{2,14},{6,2},{... | collective-permute-start | bytes 393224 | tf_op jit(solution)/shard_map/ppermute | solution.py:251
  11.7 14.0 %collective-permute-start.17 = (bf16[8,8192]{1,0:T(8,128)(2,1)S(1)}, bf16[8,8192]{1,0:T(8,128)(2,1)S(1)}, u32[]{:S(2)}, u32[]{:S(2)}) collective-permute-start(bf16[8,8192]{1,0:T(8,128)(2,1)S(1)} %broadcast_multiply_fusion), channel_id=1, source_target_pairs={{0,4},{4,8},{8,12},{12,0},{1,5},{5,9},{9,13},{13,1},{2,6},{6,10},{... | collective-permute-start | bytes 393224 | tf_op jit(solution)/shard_map/ppermute | solution.py:251
  20.9 9.2 %collective-permute-start.3 = (bf16[4,8,8192]{2,1,0:T(8,128)(2,1)S(1)}, bf16[4,8,8192]{2,1,0:T(8,128)(2,1)S(1)}, u32[]{:S(2)}, u32[]{:S(2)}) collective-permute-start(bf16[4,8,8192]{2,1,0:T(8,128)(2,1)S(1)} %get-tuple-element.21), channel_id=1, source_target_pairs={{0,2},{2,0},{1,3},{3,1},{4,6},{6,4},{5,7},{7,5},{8,10},{10,8},{9,1... | collective-permute-start | bytes 1572872 | tf_op jit(solution)/shard_map/ppermute | solution.py:251
  22.5 10.3 %collective-permute-start.4 = (bf16[4,8,8192]{2,1,0:T(8,128)(2,1)S(1)}, bf16[4,8,8192]{2,1,0:T(8,128)(2,1)S(1)}, u32[]{:S(2)}, u32[]{:S(2)}) collective-permute-start(bf16[4,8,8192]{2,1,0:T(8,128)(2,1)S(1)} %get-tuple-element.21), channel_id=1, source_target_pairs={{0,1},{1,0},{2,3},{3,2},{4,5},{5,4},{6,7},{7,6},{8,9},{9,8},{10,11... | collective-permute-start | bytes 1572872 | tf_op jit(solution)/shard_map/ppermute | solution.py:251
  30.1 2.6 %collective-permute-start.5 = (bf16[4,8,8192]{2,1,0:T(8,128)(2,1)S(1)}, bf16[4,8,8192]{2,1,0:T(8,128)(2,1)S(1)}, u32[]{:S(2)}, u32[]{:S(2)}) collective-permute-start(bf16[4,8,8192]{2,1,0:T(8,128)(2,1)S(1)} %collective-permute-done.3), channel_id=1, source_target_pairs={{0,1},{1,0},{2,3},{3,2},{4,5},{5,4},{6,7},{7,6},{8,9},{9,8},{10,11... | collective-permute-start | bytes 1572872 | tf_op jit(solution)/shard_map/ppermute | solution.py:251
  31.0 14.7 %collective-permute-start.20 = (bf16[4,8,8192]{2,1,0:T(8,128)(2,1)}, bf16[4,8,8192]{2,1,0:T(8,128)(2,1)}, u32[]{:S(2)}, u32[]{:S(2)}) collective-permute-start(bf16[4,8,8192]{2,1,0:T(8,128)(2,1)} %get-tuple-element.11), channel_id=1, source_target_pairs={{0,2},{2,0},{1,3},{3,1},{4,6},{6,4},{5,7},{7,5},{8,10},{10,8},{9,1... | collective-permute-start | bytes 1572872 | tf_op jit(solution)/shard_map/ppermute | solution.py:251
  32.8 12.9 %copy-start = (bf16[4,8,8192]{2,1,0:T(8,128)(2,1)}, bf16[4,8,8192]{2,1,0:T(8,128)(2,1)S(1)}, u32[]{:S(2)}) copy-start(bf16[4,8,8192]{2,1,0:T(8,128)(2,1)S(1)} %collective-permute-done.4) | copy-start | bytes 1572868
  32.8 12.9 %copy-start.2 = (bf16[4,8,8192]{2,1,0:T(8,128)(2,1)}, bf16[4,8,8192]{2,1,0:T(8,128)(2,1)S(1)}, u32[]{:S(2)}) copy-start(bf16[4,8,8192]{2,1,0:T(8,128)(2,1)S(1)} %collective-permute-done.5) | copy-start | bytes 1572868
  40.0 45.1 %collective-permute-start.6 = (bf16[8,128,512]{2,1,0:T(8,128)(2,1)}, bf16[8,128,512]{2,1,0:T(8,128)(2,1)}, u32[]{:S(2)}, u32[]{:S(2)}) collective-permute-start(bf16[8,128,512]{2,1,0:T(8,128)(2,1)} %share_a.3), channel_id=1, source_target_pairs={{0,1},{1,0},{2,3},{3,2},{4,5},{5,4},{6,7},{7,6},{8,9},{9,8},{10,11... | collective-permute-start | bytes 3145736 | tf_op jit(solution)/shard_map/ppermute | solution.py:251
  40.3 15.1 %collective-permute-start.21 = (bf16[4,8,8192]{2,1,0:T(8,128)(2,1)}, bf16[4,8,8192]{2,1,0:T(8,128)(2,1)S(1)}, u32[]{:S(2)}, u32[]{:S(2)}) collective-permute-start(bf16[4,8,8192]{2,1,0:T(8,128)(2,1)} %get-tuple-element.11), channel_id=1, source_target_pairs={{0,1},{1,0},{2,3},{3,2},{4,5},{5,4},{6,7},{7,6},{8,9},{9,8},{10,11... | collective-permute-start | bytes 1572872 | tf_op jit(solution)/shard_map/ppermute | solution.py:251
  45.7 9.7 %collective-permute-start.22 = (bf16[4,8,8192]{2,1,0:T(8,128)(2,1)}, bf16[4,8,8192]{2,1,0:T(8,128)(2,1)S(1)}, u32[]{:S(2)}, u32[]{:S(2)}) collective-permute-start(bf16[4,8,8192]{2,1,0:T(8,128)(2,1)} %collective-permute-done.20), channel_id=1, source_target_pairs={{0,1},{1,0},{2,3},{3,2},{4,5},{5,4},{6,7},{7,6},{8,9},{9,8},{10,11... | collective-permute-start | bytes 1572872 | tf_op jit(solution)/shard_map/ppermute | solution.py:251
  76.3 47.9 %collective-permute-start.23 = (bf16[8,128,896]{2,1,0:T(8,128)(2,1)}, bf16[8,128,896]{2,1,0:T(8,128)(2,1)}, u32[]{:S(2)}, u32[]{:S(2)}) collective-permute-start(bf16[8,128,896]{2,1,0:T(8,128)(2,1)} %share_g.3), channel_id=1, source_target_pairs={{0,1},{1,0},{2,3},{3,2},{4,5},{5,4},{6,7},{7,6},{8,9},{9,8},{10,11... | collective-permute-start | bytes 5505032 | tf_op jit(solution)/shard_map/ppermute | solution.py:251
  76.8 1.0 copy-start.1
  86.3 14.0 %collective-permute-start.7 = (bf16[4,128,512]{2,1,0:T(8,128)(2,1)S(1)}, bf16[4,128,512]{2,1,0:T(8,128)(2,1)}, u32[]{:S(2)}, u32[]{:S(2)}) collective-permute-start(bf16[4,128,512]{2,1,0:T(8,128)(2,1)S(1)} %fusion.7), channel_id=1, source_target_pairs={{0,2},{2,0},{1,3},{3,1},{4,6},{6,4},{5,7},{7,5},{8,10},{10,8},{9,1... | collective-permute-start | bytes 1572872 | tf_op jit(solution)/shard_map/ppermute | solution.py:251
  101.9 17.8 %collective-permute-start.8 = (bf16[128,512]{1,0:T(8,128)(2,1)S(1)}, bf16[128,512]{1,0:T(8,128)(2,1)S(1)}, u32[]{:S(2)}, u32[]{:S(2)}) collective-permute-start(bf16[128,512]{1,0:T(8,128)(2,1)S(1)} %get-tuple-element.8), channel_id=1, source_target_pairs={{0,4},{4,8},{8,12},{12,0},{1,5},{5,9},{9,13},{13,1},{2,6},{6,10},{... | collective-permute-start | bytes 393224 | tf_op jit(solution)/shard_map/ppermute | solution.py:251
  108.0 11.6 %collective-permute-start.10 = (bf16[128,512]{1,0:T(8,128)(2,1)S(1)}, bf16[128,512]{1,0:T(8,128)(2,1)S(1)}, u32[]{:S(2)}, u32[]{:S(2)}) collective-permute-start(bf16[128,512]{1,0:T(8,128)(2,1)S(1)} %get-tuple-element.9), channel_id=1, source_target_pairs={{0,12},{4,0},{8,4},{12,8},{1,13},{5,1},{9,5},{13,9},{2,14},{6,2},{... | collective-permute-start | bytes 393224 | tf_op jit(solution)/shard_map/ppermute | solution.py:251
  110.2 11.2 %collective-permute-start.9 = (bf16[128,512]{1,0:T(8,128)(2,1)S(1)}, bf16[128,512]{1,0:T(8,128)(2,1)S(1)}, u32[]{:S(2)}, u32[]{:S(2)}) collective-permute-start(bf16[128,512]{1,0:T(8,128)(2,1)S(1)} %get-tuple-element.10), channel_id=1, source_target_pairs={{0,8},{4,12},{8,0},{12,4},{1,9},{5,13},{9,1},{13,5},{2,10},{6,14},... | collective-permute-start | bytes 393224 | tf_op jit(solution)/shard_map/ppermute | solution.py:251
  121.4 6.0 %collective-permute-start.13 = (bf16[128,512]{1,0:T(8,128)(2,1)S(1)}, bf16[128,512]{1,0:T(8,128)(2,1)S(1)}, u32[]{:S(2)}, u32[]{:S(2)}) collective-permute-start(bf16[128,512]{1,0:T(8,128)(2,1)S(1)} %fusion.13), channel_id=1, source_target_pairs={{0,12},{4,0},{8,4},{12,8},{1,13},{5,1},{9,5},{13,9},{2,14},{6,2},{... | collective-permute-start | bytes 393224 | tf_op jit(solution)/shard_map/ppermute | solution.py:251
  122.5 12.1 %collective-permute-start.12 = (bf16[128,512]{1,0:T(8,128)(2,1)S(1)}, bf16[128,512]{1,0:T(8,128)(2,1)S(1)}, u32[]{:S(2)}, u32[]{:S(2)}) collective-permute-start(bf16[128,512]{1,0:T(8,128)(2,1)S(1)} %fusion.13), channel_id=1, source_target_pairs={{0,8},{4,12},{8,0},{12,4},{1,9},{5,13},{9,1},{13,5},{2,10},{6,14},... | collective-permute-start | bytes 393224 | tf_op jit(solution)/shard_map/ppermute | solution.py:251
  123.3 11.4 %collective-permute-start.11 = (bf16[128,512]{1,0:T(8,128)(2,1)S(1)}, bf16[128,512]{1,0:T(8,128)(2,1)S(1)}, u32[]{:S(2)}, u32[]{:S(2)}) collective-permute-start(bf16[128,512]{1,0:T(8,128)(2,1)S(1)} %fusion.13), channel_id=1, source_target_pairs={{0,4},{4,8},{8,12},{12,0},{1,5},{5,9},{9,13},{13,1},{2,6},{6,10},{... | collective-permute-start | bytes 393224 | tf_op jit(solution)/shard_map/ppermute | solution.py:251
  125.6 31.9 %collective-permute-start.24 = (bf16[4,128,896]{2,1,0:T(8,128)(2,1)S(1)}, bf16[4,128,896]{2,1,0:T(8,128)(2,1)S(1)}, u32[]{:S(2)}, u32[]{:S(2)}) collective-permute-start(bf16[4,128,896]{2,1,0:T(8,128)(2,1)S(1)} %fusion.6), channel_id=1, source_target_pairs={{0,2},{2,0},{1,3},{3,1},{4,6},{6,4},{5,7},{7,5},{8,10},{10,8},{9,1... | collective-permute-start | bytes 2752520 | tf_op jit(solution)/shard_map/ppermute | solution.py:251
  134.8 22.8 %collective-permute-start.14 = (bf16[4,128,512]{2,1,0:T(8,128)(2,1)S(1)}, bf16[4,128,512]{2,1,0:T(8,128)(2,1)S(1)}, u32[]{:S(2)}, u32[]{:S(2)}) collective-permute-start(bf16[4,128,512]{2,1,0:T(8,128)(2,1)S(1)} %pad_maximum_fusion.1.a0), channel_id=1, source_target_pairs={{0,2},{2,0},{1,3},{3,1},{4,6},{6,4},{5,7},{7,5},{8,10},{10,8},{9,1... | collective-permute-start | bytes 1572872 | tf_op jit(solution)/shard_map/ppermute | solution.py:251
  136.4 47.5 %collective-permute-start.15 = (bf16[4,128,512]{2,1,0:T(8,128)(2,1)S(1)}, bf16[4,128,512]{2,1,0:T(8,128)(2,1)S(1)}, u32[]{:S(2)}, u32[]{:S(2)}) collective-permute-start(bf16[4,128,512]{2,1,0:T(8,128)(2,1)S(1)} %pad_maximum_fusion.1.a0), channel_id=1, source_target_pairs={{0,1},{1,0},{2,3},{3,2},{4,5},{5,4},{6,7},{7,6},{8,9},{9,8},{10,11... | collective-permute-start | bytes 1572872 | tf_op jit(solution)/shard_map/ppermute | solution.py:251
  157.6 26.3 %collective-permute-start.16 = (bf16[4,128,512]{2,1,0:T(8,128)(2,1)S(1)}, bf16[4,128,512]{2,1,0:T(8,128)(2,1)S(1)}, u32[]{:S(2)}, u32[]{:S(2)}) collective-permute-start(bf16[4,128,512]{2,1,0:T(8,128)(2,1)S(1)} %collective-permute-done.14.a1), channel_id=1, source_target_pairs={{0,1},{1,0},{2,3},{3,2},{4,5},{5,4},{6,7},{7,6},{8,9},{9,8},{10,11... | collective-permute-start | bytes 1572872 | tf_op jit(solution)/shard_map/ppermute | solution.py:251
  159.1 10.3 %collective-permute-start.25 = (bf16[128,896]{1,0:T(8,128)(2,1)S(1)}, bf16[128,896]{1,0:T(8,128)(2,1)S(1)}, u32[]{:S(2)}, u32[]{:S(2)}) collective-permute-start(bf16[128,896]{1,0:T(8,128)(2,1)S(1)} %get-tuple-element.5), channel_id=1, source_target_pairs={{0,4},{4,8},{8,12},{12,0},{1,5},{5,9},{9,13},{13,1},{2,6},{6,10},{... | collective-permute-start | bytes 688136 | tf_op jit(solution)/shard_map/ppermute | solution.py:251
  160.8 12.7 %collective-permute-start.27 = (bf16[128,896]{1,0:T(8,128)(2,1)S(1)}, bf16[128,896]{1,0:T(8,128)(2,1)S(1)}, u32[]{:S(2)}, u32[]{:S(2)}) collective-permute-start(bf16[128,896]{1,0:T(8,128)(2,1)S(1)} %get-tuple-element.6), channel_id=1, source_target_pairs={{0,12},{4,0},{8,4},{12,8},{1,13},{5,1},{9,5},{13,9},{2,14},{6,2},{... | collective-permute-start | bytes 688136 | tf_op jit(solution)/shard_map/ppermute | solution.py:251
  163.0 20.7 %collective-permute-start.26 = (bf16[128,896]{1,0:T(8,128)(2,1)S(1)}, bf16[128,896]{1,0:T(8,128)(2,1)S(1)}, u32[]{:S(2)}, u32[]{:S(2)}) collective-permute-start(bf16[128,896]{1,0:T(8,128)(2,1)S(1)} %get-tuple-element.7), channel_id=1, source_target_pairs={{0,8},{4,12},{8,0},{12,4},{1,9},{5,13},{9,1},{13,5},{2,10},{6,14},... | collective-permute-start | bytes 688136 | tf_op jit(solution)/shard_map/ppermute | solution.py:251
  (1 other events, 1.0 us)

commit v2 on v0

v2 whole, which is shorter than its diff:
```python
import functools

import jax
import jax.numpy as jnp
from jax import lax
from jax.experimental import pallas as pl
from jax.experimental.pallas import tpu as pltpu
from jax.sharding import Mesh
from jax.sharding import PartitionSpec as P

SEQS = 2
F32 = jnp.float32
BF16 = jnp.bfloat16
VMEM_LIMIT = 52 * 1024 * 1024


def plain(activations, out_grad, loss_mask, w_gate, w_down, basis_a, basis_g):
    axes = ("z", "y", "core")
    masked = out_grad * loss_mask.astype(out_grad.dtype)[:, None]
    whole_act = lax.all_gather(activations, axes, axis=0, tiled=True)
    whole_grad = lax.all_gather(masked, axes, axis=0, tiled=True)
    gate_pre = jnp.dot(whole_act, w_gate, preferred_element_type=F32)
    hid_grad = lax.dot_general(
        whole_grad, w_down, (((1,), (1,)), ((), ())), preferred_element_type=F32
    )
    up_grad = (hid_grad * jax.nn.silu(gate_pre)).astype(BF16)
    depth = basis_a.shape[0]
    own_act = lax.dynamic_slice_in_dim(whole_act, lax.axis_index(axes) * depth, depth, axis=1)
    share_a = lax.psum_scatter(
        jnp.dot(own_act, basis_a, preferred_element_type=F32),
        axes,
        scatter_dimension=1,
        tiled=True,
    ).astype(BF16)
    proj_a = lax.all_gather(share_a, axes, axis=1, tiled=True)
    proj_g_cols = lax.psum_scatter(
        lax.dot_general(basis_g, up_grad, (((0,), (1,)), ((), ())), preferred_element_type=F32),
        axes,
        scatter_dimension=0,
        tiled=True,
    ).astype(BF16)
    tokens = proj_a.shape[0]
    seq = tokens // SEQS
    total = 0.0
    for which in range(SEQS):
        rows = slice(which * seq, (which + 1) * seq)
        product = lax.dot_general(
            proj_a[rows],
            proj_g_cols[:, rows],
            (((0,), (1,)), ((), ())),
            preferred_element_type=F32,
        )
        total = total + product * product
    return total / tokens


def in_hbm():
    return pl.BlockSpec(memory_space=pltpu.HBM)


def anywhere():
    return pl.BlockSpec(memory_space=pl.ANY)


def same(shape):
    return pl.BlockSpec(shape, lambda i, s: (0,) * len(shape))


def call(kernel, place, operands, in_specs, outs, out_specs, scratch, flops, moved, name, after=(), through=()):
    n_in, n_out, n_after, n_through = len(operands), len(outs), len(after), len(through)
    skip = n_in + n_after + n_through

    def body(place, *refs):
        rest = refs[skip : skip + n_out] + refs[skip + n_out + n_through :]
        kernel(place, *refs[:n_in], *rest)

    return pl.pallas_call(
        body,
        grid_spec=pltpu.PrefetchScalarGridSpec(
            num_scalar_prefetch=1,
            grid=(1,),
            in_specs=list(in_specs) + [anywhere()] * (n_after + n_through),
            out_specs=list(out_specs) + [anywhere()] * n_through,
            scratch_shapes=scratch,
        ),
        out_shape=list(outs) + [jax.ShapeDtypeStruct(t.shape, t.dtype) for t in through],
        input_output_aliases={1 + n_in + n_after + i: n_out + i for i in range(n_through)},
        compiler_params=pltpu.CompilerParams(vmem_limit_bytes=VMEM_LIMIT),
        cost_estimate=pl.CostEstimate(flops=flops, transcendentals=0, bytes_accessed=moved),
        name=name,
    )(place, *operands, *after, *through)


def hold(place, value, *after):
    return call(lambda place: None, place, (), [], [], [], [], 0, 0, "hold", after, (value,))[0]


def row_copies(place, pieces, start_column, columns, whole, sems):
    part = pieces[0].shape[0] // SEQS
    copies = []
    for other in range(2):
        for across in range(2):
            core = (place[2] + other) % 2
            y = (place[1] + across) % 2
            for which in range(SEQS):
                start = pl.multiple_of(((which * 2 + core) * 2 + y) * part, part)
                copies.append(
                    pltpu.make_async_copy(
                        pieces[other * 2 + across].at[
                            pl.ds(which * part, part), pl.ds(start_column, columns)
                        ],
                        whole.at[pl.ds(start, part), :],
                        sems.at[len(copies)],
                    )
                )
    return copies


def start_all(copies):
    for copy in copies:
        copy.start()


def wait_all(copies):
    for copy in copies:
        copy.wait()


def gate_kernel(steps, place, p0, p1, p2, p3, weight, out, whole, buffer, sems, row_sems):
    rows_in = row_copies(place, (p0, p1, p2, p3), 0, whole.shape[1], whole, row_sems)
    start_all(rows_in)
    depth = weight.shape[0] // steps
    copies = []
    for i in range(steps):
        rows = pl.ds(i * depth, depth)
        copies.append(pltpu.make_async_copy(weight.at[rows], buffer.at[rows], sems.at[i]))
    start_all(copies)
    wait_all(rows_in)
    total = None
    for i in range(steps):
        copies[i].wait()
        part = slice(i * depth, (i + 1) * depth)
        product = jnp.dot(whole[:, part], buffer[part, :], preferred_element_type=F32)
        total = product if total is None else total + product
    out[...] = total


def gate_product(place, pieces, weight, after, through, steps=8):
    rows, depth = pieces[0].shape
    width = weight.shape[1]
    return call(
        functools.partial(gate_kernel, steps),
        place,
        (*pieces, weight),
        [in_hbm()] * 5,
        [jax.ShapeDtypeStruct((4 * rows, width), F32)],
        [same((4 * rows, width))],
        [
            pltpu.VMEM((4 * rows, depth), BF16),
            pltpu.VMEM((depth, width), BF16),
            pltpu.SemaphoreType.DMA((steps,)),
            pltpu.SemaphoreType.DMA((4 * SEQS,)),
        ],
        8 * rows * depth * width,
        2 * depth * width,
        "gate",
        after=after,
        through=through,
    )


def down_kernel(steps, place, p0, p1, p2, p3, weight, gate, out, whole, buffer, sems, row_sems):
    rows_in = row_copies(place, (p0, p1, p2, p3), 0, whole.shape[1], whole, row_sems)
    start_all(rows_in)
    depth = weight.shape[1] // steps
    copies = []
    for i in range(steps):
        columns = pl.ds(i * depth, depth)
        copies.append(pltpu.make_async_copy(weight.at[:, columns], buffer.at[:, columns], sems.at[i]))
    start_all(copies)
    wait_all(rows_in)
    total = None
    for i in range(steps):
        copies[i].wait()
        part = slice(i * depth, (i + 1) * depth)
        product = lax.dot_general(
            whole[:, part], buffer[:, part], (((1,), (1,)), ((), ())), preferred_element_type=F32
        )
        total = product if total is None else total + product
    pre = gate[...]
    out[...] = (total * (pre / (1.0 + jnp.exp(-pre)))).astype(out.dtype)


def down_product(place, pieces, weight, gate, after, through, steps=8):
    rows, depth = pieces[0].shape
    width = weight.shape[0]
    return call(
        functools.partial(down_kernel, steps),
        place,
        (*pieces, weight, gate),
        [in_hbm()] * 5 + [same((4 * rows, width))],
        [jax.ShapeDtypeStruct((4 * rows, width), BF16)],
        [same((4 * rows, width))],
        [
            pltpu.VMEM((4 * rows, depth), BF16),
            pltpu.VMEM((width, depth), BF16),
            pltpu.SemaphoreType.DMA((steps,)),
            pltpu.SemaphoreType.DMA((4 * SEQS,)),
        ],
        8 * rows * depth * width,
        2 * depth * width,
        "down",
        after=after,
        through=through,
    )


def share_copies(place, basis, flip, block, buffer, sems):
    copies = []
    for chip in range(buffer.shape[0]):
        start = pl.multiple_of((2 * chip + (place[2] + flip) % 2) * block, block)
        copies.append(
            pltpu.make_async_copy(basis.at[:, pl.ds(start, block)], buffer.at[chip], sems.at[chip])
        )
    return copies


def share_products(left, copies, buffer, out):
    for chip, copy in enumerate(copies):
        copy.wait()
        out[chip] = jnp.dot(left[...], buffer[chip], preferred_element_type=F32).astype(out.dtype)


def share_a_kernel(block, place, p0, p1, p2, p3, basis, send, keep, left, buf0, buf1, sems, row_sems):
    depth = left.shape[1]
    start = pl.multiple_of(place[3] * depth, depth)
    rows_in = row_copies(place, (p0, p1, p2, p3), start, depth, left, row_sems)
    start_all(rows_in)
    sent = share_copies(place, basis, 1, block, buf0, sems.at[0])
    kept = share_copies(place, basis, 0, block, buf1, sems.at[1])
    start_all(sent)
    start_all(kept)
    wait_all(rows_in)
    share_products(left, sent, buf0, send)
    share_products(left, kept, buf1, keep)


def share_a(place, pieces, basis, chips, after):
    rows = pieces[0].shape[0]
    depth, columns = basis.shape
    block = columns // (2 * chips)
    shape = (chips, 4 * rows, block)
    return call(
        functools.partial(share_a_kernel, block),
        place,
        (*pieces, basis),
        [in_hbm()] * 5,
        [jax.ShapeDtypeStruct(shape, BF16), jax.ShapeDtypeStruct(shape, F32)],
        [same(shape), same(shape)],
        [pltpu.VMEM((4 * rows, depth), BF16)]
        + [pltpu.VMEM((chips, depth, block), BF16)] * 2
        + [pltpu.SemaphoreType.DMA((2, chips)), pltpu.SemaphoreType.DMA((4 * SEQS,))],
        8 * rows * depth * columns,
        2 * depth * columns,
        "share_a",
        after=after,
    )


def share_g_kernel(flip, block, place, up, basis, out, buffer, sems):
    copies = share_copies(place, basis, flip, block, buffer, sems)
    start_all(copies)
    share_products(up, copies, buffer, out)


def share_g(place, up, basis, chips, flip, kind, after, through):
    tokens, depth = up.shape
    block = basis.shape[1] // (2 * chips)
    shape = (chips, tokens, block)
    return call(
        functools.partial(share_g_kernel, flip, block),
        place,
        (up, basis),
        [same((tokens, depth)), in_hbm()],
        [jax.ShapeDtypeStruct(shape, kind)],
        [same(shape)],
        [pltpu.VMEM((chips, depth, block), BF16), pltpu.SemaphoreType.DMA((chips,))],
        2 * tokens * depth * chips * block,
        2 * depth * chips * block,
        "share_g",
        after=after,
        through=through,
    )


SLOTS = 8


def final_kernel(layers, first, place, a0, a1, a2, a3, g, out, pair, left, stage, sems, in_sems):
    pieces = (a0, a1, a2, a3)
    tokens, width = g.shape
    seq = tokens // SEQS
    block = stage.shape[1]
    loads = [
        pltpu.make_async_copy(pieces[which].at[z], left.at[which * layers + z], in_sems.at[which * layers + z])
        for which in range(4)
        for z in range(layers)
    ]
    start_all(loads)
    pair[...] = jnp.zeros_like(pair)
    for s in range(SEQS):
        rows = slice(s * seq, (s + 1) * seq)
        pair[rows, s * width : (s + 1) * width] = g[rows, :]
    copies = []
    for step in range(4 * layers):
        which, z = divmod(step, layers)
        core = (place[2] + which // 2) % 2
        y = (place[1] + which) % 2
        slot = step % SLOTS
        loads[step].wait()
        if step >= SLOTS:
            copies[step - SLOTS].wait()
        product = lax.dot_general(
            left[step], pair[...], (((0,), (0,)), ((), ())), preferred_element_type=F32
        )
        total = None
        for s in range(SEQS):
            one = product[:, s * width : (s + 1) * width]
            total = one * one if total is None else total + one * one
        stage[slot] = total * (1.0 / tokens)
        start = pl.multiple_of(((z * 2 + y) * 2 + core) * block, block)
        copies.append(
            pltpu.make_async_copy(
                stage.at[slot],
                out.at[pl.ds(start, block), pl.ds(first, width)],
                sems.at[slot],
            )
        )
        copies[step].start()
    wait_all(copies[-SLOTS:])


def final_product(place, pieces, g, first, columns, before):
    layers, tokens, block = pieces[0].shape
    width = g.shape[1]
    shape = jax.ShapeDtypeStruct((4 * layers * block, columns), F32)

    def kernel(place, a0, a1, a2, a3, g, *rest):
        final_kernel(layers, first, place, a0, a1, a2, a3, g, *rest[-6:])

    filled = () if before is None else (before,)
    return pl.pallas_call(
        kernel,
        grid_spec=pltpu.PrefetchScalarGridSpec(
            num_scalar_prefetch=1,
            grid=(1,),
            in_specs=[in_hbm()] * 4 + [same((tokens, width))] + [in_hbm()] * len(filled),
            out_specs=in_hbm(),
            scratch_shapes=[
                pltpu.VMEM((tokens, SEQS * width), BF16),
                pltpu.VMEM((4 * layers, tokens, block), BF16),
                pltpu.VMEM((SLOTS, block, width), F32),
                pltpu.SemaphoreType.DMA((SLOTS,)),
                pltpu.SemaphoreType.DMA((4 * layers,)),
            ],
        ),
        out_shape=shape,
        input_output_aliases={6: 0} if filled else {},
        compiler_params=pltpu.CompilerParams(vmem_limit_bytes=VMEM_LIMIT),
        cost_estimate=pl.CostEstimate(
            flops=8 * layers * block * width * tokens,
            transcendentals=0,
            bytes_accessed=16 * layers * block * width,
        ),
        name="final",
    )(place, *pieces, g, *filled)


def turn(value, axis, size, by):
    return lax.ppermute(value, axis, [(i, (i + by) % size) for i in range(size)])


def from_z(value, layers):
    return [value] + [turn(value, "z", layers, by) for by in range(1, layers)]


def in_order(pieces, z):
    layers = len(pieces)
    return jnp.stack([lax.select_n((z - i) % layers, *pieces) for i in range(layers)])


def over_chip(mine):
    across = turn(mine, "y", 2, 1)
    return mine, across, turn(mine, "core", 2, 1), turn(across, "core", 2, 1)


def pick(value, which):
    return lax.dynamic_index_in_dim(value, which, 0, keepdims=False)


def for_y(keep, got, y, layers):
    shape = (layers, 2) + keep.shape[1:]
    keep, got = keep.reshape(shape), got.reshape(shape)

    def total(which):
        return lax.dynamic_index_in_dim(keep, which, 1, keepdims=False) + (
            lax.dynamic_index_in_dim(got, which, 1, keepdims=False).astype(F32)
        )

    return total(1 - y).astype(BF16), total(y)


def for_z(keep, got, z, layers):
    total = keep + got.astype(F32)
    return [pick(total, (z + by) % layers).astype(BF16) for by in range(1, layers)], pick(total, z)


def reduce_z(sends, keep, layers):
    for by, send in enumerate(sends, 1):
        keep = keep + turn(send, "z", layers, by).astype(F32)
    return keep.astype(BF16)


def on_device(layers, activations, out_grad, loss_mask, w_gate, w_down, basis_a, basis_g):
    z, y, core = (lax.axis_index(name) for name in ("z", "y", "core"))
    chips = 2 * layers
    place = jnp.stack([z, y, core, lax.axis_index(("z", "y", "core"))]).astype(jnp.int32)
    masked = out_grad * loss_mask.astype(out_grad.dtype)[:, None]

    def flat(stacks):
        return [s.reshape(-1, s.shape[-1]) for s in stacks]

    act_z = in_order(from_z(activations, layers), z)
    grad_z = in_order(from_z(masked, layers), z)
    act = flat(over_chip(act_z))
    across = turn(grad_z, "y", 2, 1)
    send_a, keep_a = share_a(place, act, basis_a, chips, (grad_z,))
    gate, keep_a = gate_product(place, act, w_gate, (send_a,), (keep_a,))
    across = hold(place, across, gate)
    grad = flat((grad_z, across, turn(grad_z, "core", 2, 1), turn(across, "core", 2, 1)))
    send_a, keep_a = for_y(keep_a, turn(send_a, "core", 2, 1), y, layers)
    up, keep_a = down_product(place, grad, w_down, gate, (send_a,), (keep_a,))
    send_g, keep_a = share_g(place, up, basis_g, chips, 1, BF16, (send_a,), (keep_a,))
    sends_a, own_a = for_z(keep_a, turn(send_a, "y", 2, 1), z, layers)
    send_g = hold(place, send_g, sends_a[0])
    keep_g, own_a = share_g(place, up, basis_g, chips, 0, F32, (send_g,), (own_a,))
    send_g, keep_g = for_y(keep_g, turn(send_g, "core", 2, 1), y, layers)
    own_a = reduce_z(sends_a, hold(place, own_a, send_g), layers)
    pieces_a = from_z(own_a, layers)
    sends_g, own_g = for_z(keep_g, turn(send_g, "y", 2, 1), z, layers)
    pieces_a[0] = hold(place, own_a, sends_g[0])
    proj_a = over_chip(in_order(pieces_a, z))
    own_g = reduce_z(sends_g, own_g, layers)
    return final_product(place, proj_a, own_g, 0, own_g.shape[1], None)


def solution(mesh):
    tensor = mesh.shape["tensor"]
    chips = tensor // 2
    across = max(d for d in range(1, chips + 1) if chips % d == 0 and d * d <= chips)
    layers = chips // across
    fine = Mesh(
        mesh.devices.reshape(mesh.shape["parts"], layers, across, 2), ("parts", "z", "y", "core")
    )
    t = ("z", "y", "core")
    placed = (
        P(("parts",) + t, None),
        P(("parts",) + t, None),
        P(("parts",) + t),
        P(None, t),
        P(t, None),
        P(t, None),
        P(t, None),
    )

    def step(*args):
        rows = args[0].shape[0] // (mesh.shape["parts"] * tensor)
        small = across == 2 and layers * rows // SEQS == 16
        body = functools.partial(on_device, layers) if small else plain
        return jax.shard_map(
            body, mesh=fine, in_specs=placed, out_specs=P("parts", t), check_vma=False
        )(*args)

    return step
```

time: 415 us -> 183 us (0.44)
  waiting for transfers between devices: 290 us -> 55.5 us
  matrix products: 75.5 us -> 0 us
  Pallas kernels: 0 us -> 62.8 us
  starting transfers between devices: 7.74 us -> 44.3 us
  local copies, waits for them, and re-layouts: 24.6 us -> 5.53 us
  between operations: 13.2 us -> 0.48 us
  other arithmetic: 3.33 us -> 12.2 us
    all_gather x3 -> x0, waiting for transfers between devices: 218 us -> none  [the longest x1 112 us: on_device(): lax.all_gather(masked, 'tensor', axis=0, tiled=True)]
    dot_general x6 -> x0, matrix products: 75.5 us -> none  [the longest x2 35.2 us: on_device(): lax.dot_general(rows_a, rows_g, (((0,), (1,)), ((), ())), preferred_eleme...]
    reduce_scatter x1 -> x0, waiting for transfers between devices: 70.5 us -> none  [on_device(): lax.psum_scatter(lax.dot_general(basis_g, up_grad, (((0,), (1,)), ((), ()...]
    pallas_call x0 -> x10, Pallas kernels: none -> 62.8 us  [the longest x9 46.8 us: call(): pl.pallas_call(body, grid_spec=pltpu.PrefetchScalarGridSpec(num_scalar_pr...]
    ppermute x0 -> x28, waiting for transfers between devices: none -> 55.5 us  [turn(): lax.ppermute(value, axis, [(i, (i + by) % size) for i in range(size)])]
    ppermute x0 -> x28, starting transfers between devices: none -> 44.3 us  [turn(): lax.ppermute(value, axis, [(i, (i + by) % size) for i in range(size)])]
    all_to_all x1 -> x0, local copies, waits for them, and re-layouts: 12.7 us -> none  [on_device(): lax.all_to_all(basis_a, 'tensor', split_axis=1, concat_axis=0, tiled=True)]
    unnamed x5 -> x24, local copies, waits for them, and re-layouts: 12 us -> 4.22 us
  transfers between devices with their start and end apart: 5 -> 28, of which waited for: 4 -> 10; matrix products, arithmetic and copies ran while one was open for 16% -> 5% of each run, Pallas kernels for 0% -> 20%
where the time goes in v2:
time: 183 us; the launch traced here: 181 us
  Pallas kernels  62.8 us (34%)
  waiting for transfers between devices  55.5 us (30%)
  starting transfers between devices  44.3 us (24%)
  other arithmetic  12.2 us (7%)
  local copies, waits for them, and re-layouts  5.53 us (3%)
    ppermute x28, waiting for transfers between devices, turn(): lax.ppermute(value, axis, [(i, (i + by) % size) for i in range(size)])  55.5 us
    pallas_call x9, Pallas kernels, call(): pl.pallas_call(body, grid_spec=pltpu.PrefetchScalarGridSpec(num_scalar_pr...  46.8 us
    ppermute x28, starting transfers between devices, turn(): lax.ppermute(value, axis, [(i, (i + by) % size) for i in range(size)])  44.3 us
    pallas_call x1, Pallas kernels, final_product(): pl.pallas_call(kernel, grid_spec=pltpu.PrefetchScalarGridSpec(num_scalar_...  16 us
    unnamed x24, local copies, waits for them, and re-layouts  4.22 us
  transfers between devices with their start and end apart: 28, of which 10 were waited for; matrix products, arithmetic and copies ran while one was open for 5% of the time, Pallas kernels for 20%

profile of v2, /device:TPU:0, one launch (start us, length us, event | category | flops | bytes accessed | tf_op | source)
XLA Modules:
  0.0 180.8 jit_solution(15833621509934788904)
XLA Ops:
  0.0 3.0 %collective-permute-start.3 = (bf16[8,8192]{1,0:T(8,128)(2,1)}, bf16[8,8192]{1,0:T(8,128)(2,1)S(1)}, u32[]{:S(2)}, u32[]{:S(2)}) collective-permute-start(bf16[8,8192]{1,0:T(8,128)(2,1)} %param.7), channel_id=1, source_target_pairs={{0,4},{4,8},{8,12},{12,0},{1,5},{5,9},{9,13},{13,1},{2,6},{6,10},{... | collective-permute-start | bytes 393224 | tf_op jit(solution)/shard_map/ppermute | solution.py:380
  3.0 2.6 %collective-permute-start.4 = (bf16[8,8192]{1,0:T(8,128)(2,1)}, bf16[8,8192]{1,0:T(8,128)(2,1)S(1)}, u32[]{:S(2)}, u32[]{:S(2)}) collective-permute-start(bf16[8,8192]{1,0:T(8,128)(2,1)} %param.7), channel_id=1, source_target_pairs={{0,8},{4,12},{8,0},{12,4},{1,9},{5,13},{9,1},{13,5},{2,10},{6,14},... | collective-permute-start | bytes 393224 | tf_op jit(solution)/shard_map/ppermute | solution.py:380
  5.6 1.3 collective-permute-start.5
  8.9 2.9 %collective-permute-start.2 = (bf16[8,8192]{1,0:T(8,128)(2,1)S(1)}, bf16[8,8192]{1,0:T(8,128)(2,1)S(1)}, u32[]{:S(2)}, u32[]{:S(2)}) collective-permute-start(bf16[8,8192]{1,0:T(8,128)(2,1)S(1)} %broadcast_multiply_fusion), channel_id=1, source_target_pairs={{0,12},{4,0},{8,4},{12,8},{1,13},{5,1},{9,5},{13,9},{2,14},{6,2},{... | collective-permute-start | bytes 393224 | tf_op jit(solution)/shard_map/ppermute | solution.py:380
  11.8 8.0 %collective-permute-start = (bf16[8,8192]{1,0:T(8,128)(2,1)S(1)}, bf16[8,8192]{1,0:T(8,128)(2,1)S(1)}, u32[]{:S(2)}, u32[]{:S(2)}) collective-permute-start(bf16[8,8192]{1,0:T(8,128)(2,1)S(1)} %broadcast_multiply_fusion), channel_id=1, source_target_pairs={{0,4},{4,8},{8,12},{12,0},{1,5},{5,9},{9,13},{13,1},{2,6},{6,10},{... | collective-permute-start | bytes 393224 | tf_op jit(solution)/shard_map/ppermute | solution.py:380
  20.9 1.6 collective-permute-start.6
  22.5 3.3 %collective-permute-done.1 = bf16[8,8192]{1,0:T(8,128)(2,1)S(1)} collective-permute-done((bf16[8,8192]{1,0:T(8,128)(2,1)S(1)}, bf16[8,8192]{1,0:T(8,128)(2,1)S(1)}, u32[]{:S(2)}, u32[]{:S(2)}) %collective-permute-start.1) | collective-permute-done | bytes 131104 | tf_op jit(solution)/shard_map/ppermute | solution.py:380
  25.9 4.2 %collective-permute-done.6 = bf16[4,8,8192]{2,1,0:T(8,128)(2,1)S(1)} collective-permute-done((bf16[4,8,8192]{2,1,0:T(8,128)(2,1)S(1)}, bf16[4,8,8192]{2,1,0:T(8,128)(2,1)S(1)}, u32[]{:S(2)}, u32[]{:S(2)}) %collective-permute-start.6) | collective-permute-done | bytes 524320 | tf_op jit(solution)/shard_map/ppermute | solution.py:380
  32.8 9.2 %share_a.1 = (bf16[8,128,512]{2,1,0:T(8,128)(2,1)}, f32[8,128,512]{2,1,0:T(8,128)}) custom-call(s32[4]{0:T(128)S(1)} %pad_add_fusion.place, bf16[32,8192]{1,0:T(8,128)(2,1)S(1)} %get-tuple-element.40.refs_0_, bf16[32,8192]{1,0:T(8,128)(2,1)S(1)} %bitcast.104, bf16[32,8192]{1,0:T(8,128)(2,1)S(1)} %bitcast.106, bf16[32,8192]{1,0:T(8,128)(2,1)} %bitcast.112, ...), custom_call_target="tpu_custom_call" | custom-call | flops 1073741824 | bytes 8388608 | tf_op jit(solution)/shard_map/share_a/pallas_call | solution.py:77
  42.2 1.7 collective-permute-start.9
  44.0 9.1 %gate.1 = (f32[128,896]{1,0:T(8,128)S(1)}, f32[8,128,512]{2,1,0:T(8,128)}) custom-call(s32[4]{0:T(128)S(1)} %pad_add_fusion.place, bf16[32,8192]{1,0:T(8,128)(2,1)S(1)} %get-tuple-element.40.refs_0_, bf16[32,8192]{1,0:T(8,128)(2,1)S(1)} %bitcast.105, bf16[32,8192]{1,0:T(8,128)(2,1)} %bitcast.107, ...), custom_call_target="tpu_custom_call", output_to_operand_aliasing={{1}: (7, {})} | custom-call | flops 1879048192 | bytes 14680064 | tf_op jit(solution)/shard_map/gate/pallas_call | solution.py:77
  53.2 3.3 %collective-permute-done.9.refs_1_ = bf16[4,8,8192]{2,1,0:T(8,128)(2,1)S(1)} collective-permute-done((bf16[4,8,8192]{2,1,0:T(8,128)(2,1)S(1)}, bf16[4,8,8192]{2,1,0:T(8,128)(2,1)S(1)}, u32[]{:S(2)}, u32[]{:S(2)}) %collective-permute-start.9) | collective-permute-done | bytes 524320 | tf_op jit(solution)/shard_map/ppermute | solution.py:380
  57.1 3.2 %fusion.3 = (f32[4,128,512]{2,1,0:T(8,128)}, bf16[4,128,512]{2,1,0:T(8,128)(2,1)S(1)}) fusion(f32[4,2,128,512]{3,2,1,0:T(8,128)} %bitcast.109, s32[]{:T(128)S(6)} %select_n.394, bf16[4,2,128,512]{3,2,1,0:T(8,128)(2,1)} %bitcast.21, s32[]{:T(128)S(6)} %select_n.393), kind=kLoop, calls=%fused_computation.6 | loop fusion | flops 1310720 | bytes 4718600 | tf_op jit(solution)/shard_map/add | solution.py:406
  60.3 1.7 collective-permute-start.13
  62.0 11.4 %down.1 = (bf16[128,896]{1,0:T(8,128)(2,1)S(1)}, f32[4,128,512]{2,1,0:T(8,128)}) custom-call(s32[4]{0:T(128)S(1)} %pad_add_fusion.place, bf16[32,8192]{1,0:T(8,128)(2,1)S(1)} %get-tuple-element.38.refs_0_, bf16[32,8192]{1,0:T(8,128)(2,1)S(1)} %bitcast.108, bf16[32,8192]{1,0:T(8,128)(2,1)} %bitcast.18.refs_2_, ...), custom_call_target="tpu_custom_call", output_to_operand_aliasing={{1}: (8, {})} | custom-call | flops 1879048192 | bytes 14680064 | tf_op jit(solution)/shard_map/down/pallas_call | solution.py:77
  75.7 7.1 %share_g.2 = (bf16[8,128,896]{2,1,0:T(8,128)(2,1)}, f32[4,128,512]{2,1,0:T(8,128)S(1)}) custom-call(s32[4]{0:T(128)S(1)} %pad_add_fusion.place, bf16[128,896]{1,0:T(8,128)(2,1)S(1)} %get-tuple-element.19.refs_0_, bf16[896,14336]{1,0:T(8,128)(2,1)} %refs_1_.3, bf16[4,128,512]{2,1,0:T(8,128)(2,1)S(1)} %copy-done.4, ...), custom_call_target="tpu_custom_call", output_to_operand_aliasing={{1}: (4, {})} | custom-call | flops 1644167168 | bytes 12845056 | tf_op jit(solution)/shard_map/share_g/pallas_call | solution.py:77
  82.8 1.4 convert_add_fusion
  86.6 7.8 %share_g.3 = (f32[8,128,896]{2,1,0:T(8,128)}, f32[128,512]{1,0:T(8,128)S(1)}) custom-call(s32[4]{0:T(128)S(1)} %pad_add_fusion.place, bf16[128,896]{1,0:T(8,128)(2,1)S(1)} %get-tuple-element.19.refs_0_, bf16[896,14336]{1,0:T(8,128)(2,1)} %refs_1_.3, bf16[8,128,896]{2,1,0:T(8,128)(2,1)} %copy-done.2, ...), custom_call_target="tpu_custom_call", output_to_operand_aliasing={{1}: (4, {})} | custom-call | flops 1644167168 | bytes 12845056 | tf_op jit(solution)/shard_map/share_g/pallas_call | solution.py:77
  94.4 2.1 %fusion.5.refs_0_ = bf16[4,128,896]{2,1,0:T(8,128)(2,1)S(1)} fusion(f32[4,2,128,896]{3,2,1,0:T(8,128)} %bitcast.110, s32[]{:T(128)S(6)} %select_n.393, bf16[4,2,128,896]{3,2,1,0:T(8,128)(2,1)} %bitcast.27), kind=kLoop, calls=%fused_computation.10 | loop fusion | flops 1376256 | bytes 3670020 | tf_op jit(solution)/shard_map/convert_element_type | solution.py:410
  97.5 8.1 %collective-permute-start.18 = (bf16[128,512]{1,0:T(8,128)(2,1)S(1)}, bf16[128,512]{1,0:T(8,128)(2,1)S(1)}, u32[]{:S(2)}, u32[]{:S(2)}) collective-permute-start(bf16[128,512]{1,0:T(8,128)(2,1)S(1)} %get-tuple-element.31), channel_id=1, source_target_pairs={{0,12},{4,0},{8,4},{12,8},{1,13},{5,1},{9,5},{13,9},{2,14},{6,2},{... | collective-permute-start | bytes 393224 | tf_op jit(solution)/shard_map/ppermute | solution.py:380
  106.7 2.8 %collective-permute-done.18 = bf16[128,512]{1,0:T(8,128)(2,1)S(1)} collective-permute-done((bf16[128,512]{1,0:T(8,128)(2,1)S(1)}, bf16[128,512]{1,0:T(8,128)(2,1)S(1)}, u32[]{:S(2)}, u32[]{:S(2)}) %collective-permute-start.18) | collective-permute-done | bytes 131104 | tf_op jit(solution)/shard_map/ppermute | solution.py:380
  109.5 7.4 %collective-permute-done.17 = bf16[128,512]{1,0:T(8,128)(2,1)S(1)} collective-permute-done((bf16[128,512]{1,0:T(8,128)(2,1)S(1)}, bf16[128,512]{1,0:T(8,128)(2,1)S(1)}, u32[]{:S(2)}, u32[]{:S(2)}) %collective-permute-start.17) | collective-permute-done | bytes 131104 | tf_op jit(solution)/shard_map/ppermute | solution.py:380
  116.9 1.5 collective-permute-start.21
  119.5 1.9 %collective-permute-start.19 = (bf16[128,512]{1,0:T(8,128)(2,1)S(1)}, bf16[128,512]{1,0:T(8,128)(2,1)S(1)}, u32[]{:S(2)}, u32[]{:S(2)}) collective-permute-start(bf16[128,512]{1,0:T(8,128)(2,1)S(1)} %add_convert_fusion.refs_1_), channel_id=1, source_target_pairs={{0,4},{4,8},{8,12},{12,0},{1,5},{5,9},{9,13},{13,1},{2,6},{6,10},{... | collective-permute-start | bytes 393224 | tf_op jit(solution)/shard_map/ppermute | solution.py:380
  121.4 1.5 fusion.2
  123.0 7.6 %collective-permute-done.20 = bf16[128,512]{1,0:T(8,128)(2,1)S(1)} collective-permute-done((bf16[128,512]{1,0:T(8,128)(2,1)S(1)}, bf16[128,512]{1,0:T(8,128)(2,1)S(1)}, u32[]{:S(2)}, u32[]{:S(2)}) %collective-permute-start.20) | collective-permute-done | bytes 131104 | tf_op jit(solution)/shard_map/ppermute | solution.py:380
  132.6 10.6 %collective-permute-done.22.a1 = bf16[4,128,512]{2,1,0:T(8,128)(2,1)S(1)} collective-permute-done((bf16[4,128,512]{2,1,0:T(8,128)(2,1)S(1)}, bf16[4,128,512]{2,1,0:T(8,128)(2,1)S(1)}, u32[]{:S(2)}, u32[]{:S(2)}) %collective-permute-start.22) | collective-permute-done | bytes 524320 | tf_op jit(solution)/shard_map/ppermute | solution.py:380
  143.2 3.2 %collective-permute-start.26 = (bf16[128,896]{1,0:T(8,128)(2,1)S(1)}, bf16[128,896]{1,0:T(8,128)(2,1)S(1)}, u32[]{:S(2)}, u32[]{:S(2)}) collective-permute-start(bf16[128,896]{1,0:T(8,128)(2,1)S(1)} %get-tuple-element.27), channel_id=1, source_target_pairs={{0,8},{4,12},{8,0},{12,4},{1,9},{5,13},{9,1},{13,5},{2,10},{6,14},... | collective-permute-start | bytes 688136 | tf_op jit(solution)/shard_map/ppermute | solution.py:380
  146.8 1.6 collective-permute-start.25
  148.4 9.8 %collective-permute-done.26 = bf16[128,896]{1,0:T(8,128)(2,1)S(1)} collective-permute-done((bf16[128,896]{1,0:T(8,128)(2,1)S(1)}, bf16[128,896]{1,0:T(8,128)(2,1)S(1)}, u32[]{:S(2)}, u32[]{:S(2)}) %collective-permute-start.26) | collective-permute-done | bytes 229408 | tf_op jit(solution)/shard_map/ppermute | solution.py:380
  158.2 5.5 %collective-permute-done.27 = bf16[128,896]{1,0:T(8,128)(2,1)S(1)} collective-permute-done((bf16[128,896]{1,0:T(8,128)(2,1)S(1)}, bf16[128,896]{1,0:T(8,128)(2,1)S(1)}, u32[]{:S(2)}, u32[]{:S(2)}) %collective-permute-start.27) | collective-permute-done | bytes 229408 | tf_op jit(solution)/shard_map/ppermute | solution.py:380
  164.6 16.0 %final.1 = f32[8192,896]{1,0:T(8,128)} custom-call(s32[4]{0:T(128)S(1)} %pad_add_fusion.place, bf16[4,128,512]{2,1,0:T(8,128)(2,1)S(1)} %pad_maximum_fusion.2.a0, bf16[4,128,512]{2,1,0:T(8,128)(2,1)S(1)} %collective-permute-done.22.a1, bf16[4,128,512]{2,1,0:T(8,128)(2,1)S(1)} %collective-permute-done.23.a2, bf16[4,128,512]{2,1,0:T(8,128)(2,1)} %copy-done.10, ...), custom_call_target="tpu_custom_call" | custom-call | flops 1879048192 | bytes 29360128 | tf_op jit(solution)/shard_map/final/pallas_call | solution.py:352
  (76 shorter events, 18.1 us)
Async XLA Ops:
  0.0 25.8 %copy-start.11 = (bf16[8,8192]{1,0:T(8,128)(2,1)S(1)}, bf16[8,8192]{1,0:T(8,128)(2,1)}, u32[]{:S(2)}) copy-start(bf16[8,8192]{1,0:T(8,128)(2,1)} %param.8) | copy-start | bytes 393220
  0.0 11.8 %collective-permute-start.3 = (bf16[8,8192]{1,0:T(8,128)(2,1)}, bf16[8,8192]{1,0:T(8,128)(2,1)S(1)}, u32[]{:S(2)}, u32[]{:S(2)}) collective-permute-start(bf16[8,8192]{1,0:T(8,128)(2,1)} %param.7), channel_id=1, source_target_pairs={{0,4},{4,8},{8,12},{12,0},{1,5},{5,9},{9,13},{13,1},{2,6},{6,10},{... | collective-permute-start | bytes 393224 | tf_op jit(solution)/shard_map/ppermute | solution.py:380
  3.0 16.8 %collective-permute-start.4 = (bf16[8,8192]{1,0:T(8,128)(2,1)}, bf16[8,8192]{1,0:T(8,128)(2,1)S(1)}, u32[]{:S(2)}, u32[]{:S(2)}) collective-permute-start(bf16[8,8192]{1,0:T(8,128)(2,1)} %param.7), channel_id=1, source_target_pairs={{0,8},{4,12},{8,0},{12,4},{1,9},{5,13},{9,1},{13,5},{2,10},{6,14},... | collective-permute-start | bytes 393224 | tf_op jit(solution)/shard_map/ppermute | solution.py:380
  5.6 14.2 %collective-permute-start.5 = (bf16[8,8192]{1,0:T(8,128)(2,1)}, bf16[8,8192]{1,0:T(8,128)(2,1)S(1)}, u32[]{:S(2)}, u32[]{:S(2)}) collective-permute-start(bf16[8,8192]{1,0:T(8,128)(2,1)} %param.7), channel_id=1, source_target_pairs={{0,12},{4,0},{8,4},{12,8},{1,13},{5,1},{9,5},{13,9},{2,14},{6,2},{... | collective-permute-start | bytes 393224 | tf_op jit(solution)/shard_map/ppermute | solution.py:380
  8.6 17.1 %collective-permute-start.1 = (bf16[8,8192]{1,0:T(8,128)(2,1)S(1)}, bf16[8,8192]{1,0:T(8,128)(2,1)S(1)}, u32[]{:S(2)}, u32[]{:S(2)}) collective-permute-start(bf16[8,8192]{1,0:T(8,128)(2,1)S(1)} %broadcast_multiply_fusion), channel_id=1, source_target_pairs={{0,8},{4,12},{8,0},{12,4},{1,9},{5,13},{9,1},{13,5},{2,10},{6,14},... | collective-permute-start | bytes 393224 | tf_op jit(solution)/shard_map/ppermute | solution.py:380
  8.9 16.9 %collective-permute-start.2 = (bf16[8,8192]{1,0:T(8,128)(2,1)S(1)}, bf16[8,8192]{1,0:T(8,128)(2,1)S(1)}, u32[]{:S(2)}, u32[]{:S(2)}) collective-permute-start(bf16[8,8192]{1,0:T(8,128)(2,1)S(1)} %broadcast_multiply_fusion), channel_id=1, source_target_pairs={{0,12},{4,0},{8,4},{12,8},{1,13},{5,1},{9,5},{13,9},{2,14},{6,2},{... | collective-permute-start | bytes 393224 | tf_op jit(solution)/shard_map/ppermute | solution.py:380
  11.8 14.0 %collective-permute-start = (bf16[8,8192]{1,0:T(8,128)(2,1)S(1)}, bf16[8,8192]{1,0:T(8,128)(2,1)S(1)}, u32[]{:S(2)}, u32[]{:S(2)}) collective-permute-start(bf16[8,8192]{1,0:T(8,128)(2,1)S(1)} %broadcast_multiply_fusion), channel_id=1, source_target_pairs={{0,4},{4,8},{8,12},{12,0},{1,5},{5,9},{9,13},{13,1},{2,6},{6,10},{... | collective-permute-start | bytes 393224 | tf_op jit(solution)/shard_map/ppermute | solution.py:380
  20.9 9.2 %collective-permute-start.6 = (bf16[4,8,8192]{2,1,0:T(8,128)(2,1)S(1)}, bf16[4,8,8192]{2,1,0:T(8,128)(2,1)S(1)}, u32[]{:S(2)}, u32[]{:S(2)}) collective-permute-start(bf16[4,8,8192]{2,1,0:T(8,128)(2,1)S(1)} %get-tuple-element.39), channel_id=1, source_target_pairs={{0,2},{2,0},{1,3},{3,1},{4,6},{6,4},{5,7},{7,5},{8,10},{10,8},{9,1... | collective-permute-start | bytes 1572872 | tf_op jit(solution)/shard_map/ppermute | solution.py:380
  22.5 8.6 %collective-permute-start.7 = (bf16[4,8,8192]{2,1,0:T(8,128)(2,1)S(1)}, bf16[4,8,8192]{2,1,0:T(8,128)(2,1)S(1)}, u32[]{:S(2)}, u32[]{:S(2)}) collective-permute-start(bf16[4,8,8192]{2,1,0:T(8,128)(2,1)S(1)} %get-tuple-element.39), channel_id=1, source_target_pairs={{0,1},{1,0},{2,3},{3,2},{4,5},{5,4},{6,7},{7,6},{8,9},{9,8},{10,11... | collective-permute-start | bytes 1572872 | tf_op jit(solution)/shard_map/ppermute | solution.py:380
  30.1 1.9 %collective-permute-start.8 = (bf16[4,8,8192]{2,1,0:T(8,128)(2,1)S(1)}, bf16[4,8,8192]{2,1,0:T(8,128)(2,1)S(1)}, u32[]{:S(2)}, u32[]{:S(2)}) collective-permute-start(bf16[4,8,8192]{2,1,0:T(8,128)(2,1)S(1)} %collective-permute-done.6), channel_id=1, source_target_pairs={{0,1},{1,0},{2,3},{3,2},{4,5},{5,4},{6,7},{7,6},{8,9},{9,8},{10,11... | collective-permute-start | bytes 1572872 | tf_op jit(solution)/shard_map/ppermute | solution.py:380
  31.0 11.0 %copy-start.5 = (bf16[4,8,8192]{2,1,0:T(8,128)(2,1)}, bf16[4,8,8192]{2,1,0:T(8,128)(2,1)S(1)}, u32[]{:S(2)}) copy-start(bf16[4,8,8192]{2,1,0:T(8,128)(2,1)S(1)} %collective-permute-done.7) | copy-start | bytes 1572868
  32.8 9.4 %copy-start.8 = (bf16[4,8,8192]{2,1,0:T(8,128)(2,1)S(1)}, bf16[4,8,8192]{2,1,0:T(8,128)(2,1)}, u32[]{:S(2)}) copy-start(bf16[4,8,8192]{2,1,0:T(8,128)(2,1)} %get-tuple-element.37.refs_5_) | copy-start | bytes 1572868
  42.0 15.0 %collective-permute-start.12 = (bf16[8,128,512]{2,1,0:T(8,128)(2,1)}, bf16[8,128,512]{2,1,0:T(8,128)(2,1)}, u32[]{:S(2)}, u32[]{:S(2)}) collective-permute-start(bf16[8,128,512]{2,1,0:T(8,128)(2,1)} %get-tuple-element.15.refs_5_), channel_id=1, source_target_pairs={{0,1},{1,0},{2,3},{3,2},{4,5},{5,4},{6,7},{7,6},{8,9},{9,8},{10,11... | collective-permute-start | bytes 3145736 | tf_op jit(solution)/shard_map/ppermute | solution.py:380
  42.2 14.2 %collective-permute-start.9 = (bf16[4,8,8192]{2,1,0:T(8,128)(2,1)S(1)}, bf16[4,8,8192]{2,1,0:T(8,128)(2,1)S(1)}, u32[]{:S(2)}, u32[]{:S(2)}) collective-permute-start(bf16[4,8,8192]{2,1,0:T(8,128)(2,1)S(1)} %copy-done.8), channel_id=1, source_target_pairs={{0,2},{2,0},{1,3},{3,1},{4,6},{6,4},{5,7},{7,5},{8,10},{10,8},{9,1... | collective-permute-start | bytes 1572872 | tf_op jit(solution)/shard_map/ppermute | solution.py:380
  43.9 18.0 %collective-permute-start.10 = (bf16[4,8,8192]{2,1,0:T(8,128)(2,1)S(1)}, bf16[4,8,8192]{2,1,0:T(8,128)(2,1)}, u32[]{:S(2)}, u32[]{:S(2)}) collective-permute-start(bf16[4,8,8192]{2,1,0:T(8,128)(2,1)S(1)} %copy-done.8), channel_id=1, source_target_pairs={{0,1},{1,0},{2,3},{3,2},{4,5},{5,4},{6,7},{7,6},{8,9},{9,8},{10,11... | collective-permute-start | bytes 1572872 | tf_op jit(solution)/shard_map/ppermute | solution.py:380
  57.0 5.0 %collective-permute-start.11 = (bf16[4,8,8192]{2,1,0:T(8,128)(2,1)S(1)}, bf16[4,8,8192]{2,1,0:T(8,128)(2,1)}, u32[]{:S(2)}, u32[]{:S(2)}) collective-permute-start(bf16[4,8,8192]{2,1,0:T(8,128)(2,1)S(1)} %hold.4), channel_id=1, source_target_pairs={{0,1},{1,0},{2,3},{3,2},{4,5},{5,4},{6,7},{7,6},{8,9},{9,8},{10,11... | collective-permute-start | bytes 1572872 | tf_op jit(solution)/shard_map/ppermute | solution.py:380
  60.3 22.6 %collective-permute-start.13 = (bf16[4,128,512]{2,1,0:T(8,128)(2,1)S(1)}, bf16[4,128,512]{2,1,0:T(8,128)(2,1)}, u32[]{:S(2)}, u32[]{:S(2)}) collective-permute-start(bf16[4,128,512]{2,1,0:T(8,128)(2,1)S(1)} %get-tuple-element.26.refs_6_.refs_2_), channel_id=1, source_target_pairs={{0,2},{2,0},{1,3},{3,1},{4,6},{6,4},{5,7},{7,5},{8,10},{10,8},{9,1... | collective-permute-start | bytes 1572872 | tf_op jit(solution)/shard_map/ppermute | solution.py:380
  85.2 9.2 %collective-permute-start.14 = (bf16[8,128,896]{2,1,0:T(8,128)(2,1)S(1)}, bf16[8,128,896]{2,1,0:T(8,128)(2,1)}, u32[]{:S(2)}, u32[]{:S(2)}) collective-permute-start(bf16[8,128,896]{2,1,0:T(8,128)(2,1)S(1)} %hold.5.refs_2_), channel_id=1, source_target_pairs={{0,1},{1,0},{2,3},{3,2},{4,5},{5,4},{6,7},{7,6},{8,9},{9,8},{10,11... | collective-permute-start | bytes 5505032 | tf_op jit(solution)/shard_map/ppermute | solution.py:380
  94.4 27.0 %copy-start.6 = (f32[8,128,896]{2,1,0:T(8,128)S(1)}, f32[8,128,896]{2,1,0:T(8,128)}, u32[]{:S(2)}) copy-start(f32[8,128,896]{2,1,0:T(8,128)} %get-tuple-element.23) | copy-start | bytes 11010052
  96.5 24.9 %collective-permute-start.15 = (bf16[4,128,896]{2,1,0:T(8,128)(2,1)S(1)}, bf16[4,128,896]{2,1,0:T(8,128)(2,1)S(1)}, u32[]{:S(2)}, u32[]{:S(2)}) collective-permute-start(bf16[4,128,896]{2,1,0:T(8,128)(2,1)S(1)} %fusion.5.refs_0_), channel_id=1, source_target_pairs={{0,2},{2,0},{1,3},{3,1},{4,6},{6,4},{5,7},{7,5},{8,10},{10,8},{9,1... | collective-permute-start | bytes 2752520 | tf_op jit(solution)/shard_map/ppermute | solution.py:380
  97.5 12.0 %collective-permute-start.18 = (bf16[128,512]{1,0:T(8,128)(2,1)S(1)}, bf16[128,512]{1,0:T(8,128)(2,1)S(1)}, u32[]{:S(2)}, u32[]{:S(2)}) collective-permute-start(bf16[128,512]{1,0:T(8,128)(2,1)S(1)} %get-tuple-element.31), channel_id=1, source_target_pairs={{0,12},{4,0},{8,4},{12,8},{1,13},{5,1},{9,5},{13,9},{2,14},{6,2},{... | collective-permute-start | bytes 393224 | tf_op jit(solution)/shard_map/ppermute | solution.py:380
  105.6 11.3 %collective-permute-start.17 = (bf16[128,512]{1,0:T(8,128)(2,1)S(1)}, bf16[128,512]{1,0:T(8,128)(2,1)S(1)}, u32[]{:S(2)}, u32[]{:S(2)}) collective-permute-start(bf16[128,512]{1,0:T(8,128)(2,1)S(1)} %get-tuple-element.32), channel_id=1, source_target_pairs={{0,8},{4,12},{8,0},{12,4},{1,9},{5,13},{9,1},{13,5},{2,10},{6,14},... | collective-permute-start | bytes 393224 | tf_op jit(solution)/shard_map/ppermute | solution.py:380
  105.6 11.3 %collective-permute-start.16 = (bf16[128,512]{1,0:T(8,128)(2,1)S(1)}, bf16[128,512]{1,0:T(8,128)(2,1)S(1)}, u32[]{:S(2)}, u32[]{:S(2)}) collective-permute-start(bf16[128,512]{1,0:T(8,128)(2,1)S(1)} %get-tuple-element.30.refs_0_), channel_id=1, source_target_pairs={{0,4},{4,8},{8,12},{12,0},{1,5},{5,9},{9,13},{13,1},{2,6},{6,10},{... | collective-permute-start | bytes 393224 | tf_op jit(solution)/shard_map/ppermute | solution.py:380
  116.9 6.0 %collective-permute-start.21 = (bf16[128,512]{1,0:T(8,128)(2,1)S(1)}, bf16[128,512]{1,0:T(8,128)(2,1)S(1)}, u32[]{:S(2)}, u32[]{:S(2)}) collective-permute-start(bf16[128,512]{1,0:T(8,128)(2,1)S(1)} %add_convert_fusion.refs_1_), channel_id=1, source_target_pairs={{0,12},{4,0},{8,4},{12,8},{1,13},{5,1},{9,5},{13,9},{2,14},{6,2},{... | collective-permute-start | bytes 393224 | tf_op jit(solution)/shard_map/ppermute | solution.py:380
  118.5 12.1 %collective-permute-start.20 = (bf16[128,512]{1,0:T(8,128)(2,1)S(1)}, bf16[128,512]{1,0:T(8,128)(2,1)S(1)}, u32[]{:S(2)}, u32[]{:S(2)}) collective-permute-start(bf16[128,512]{1,0:T(8,128)(2,1)S(1)} %add_convert_fusion.refs_1_), channel_id=1, source_target_pairs={{0,8},{4,12},{8,0},{12,4},{1,9},{5,13},{9,1},{13,5},{2,10},{6,14},... | collective-permute-start | bytes 393224 | tf_op jit(solution)/shard_map/ppermute | solution.py:380
  119.5 11.1 %collective-permute-start.19 = (bf16[128,512]{1,0:T(8,128)(2,1)S(1)}, bf16[128,512]{1,0:T(8,128)(2,1)S(1)}, u32[]{:S(2)}, u32[]{:S(2)}) collective-permute-start(bf16[128,512]{1,0:T(8,128)(2,1)S(1)} %add_convert_fusion.refs_1_), channel_id=1, source_target_pairs={{0,4},{4,8},{8,12},{12,0},{1,5},{5,9},{9,13},{13,1},{2,6},{6,10},{... | collective-permute-start | bytes 393224 | tf_op jit(solution)/shard_map/ppermute | solution.py:380
  131.3 11.9 %collective-permute-start.22 = (bf16[4,128,512]{2,1,0:T(8,128)(2,1)S(1)}, bf16[4,128,512]{2,1,0:T(8,128)(2,1)S(1)}, u32[]{:S(2)}, u32[]{:S(2)}) collective-permute-start(bf16[4,128,512]{2,1,0:T(8,128)(2,1)S(1)} %pad_maximum_fusion.2.a0), channel_id=1, source_target_pairs={{0,2},{2,0},{1,3},{3,1},{4,6},{6,4},{5,7},{7,5},{8,10},{10,8},{9,1... | collective-permute-start | bytes 1572872 | tf_op jit(solution)/shard_map/ppermute | solution.py:380
  132.6 31.2 %collective-permute-start.23 = (bf16[4,128,512]{2,1,0:T(8,128)(2,1)S(1)}, bf16[4,128,512]{2,1,0:T(8,128)(2,1)S(1)}, u32[]{:S(2)}, u32[]{:S(2)}) collective-permute-start(bf16[4,128,512]{2,1,0:T(8,128)(2,1)S(1)} %pad_maximum_fusion.2.a0), channel_id=1, source_target_pairs={{0,1},{1,0},{2,3},{3,2},{4,5},{5,4},{6,7},{7,6},{8,9},{9,8},{10,11... | collective-permute-start | bytes 1572872 | tf_op jit(solution)/shard_map/ppermute | solution.py:380
  143.2 20.6 %collective-permute-start.24 = (bf16[4,128,512]{2,1,0:T(8,128)(2,1)S(1)}, bf16[4,128,512]{2,1,0:T(8,128)(2,1)S(1)}, u32[]{:S(2)}, u32[]{:S(2)}) collective-permute-start(bf16[4,128,512]{2,1,0:T(8,128)(2,1)S(1)} %collective-permute-done.22.a1), channel_id=1, source_target_pairs={{0,1},{1,0},{2,3},{3,2},{4,5},{5,4},{6,7},{7,6},{8,9},{9,8},{10,11... | collective-permute-start | bytes 1572872 | tf_op jit(solution)/shard_map/ppermute | solution.py:380
  143.2 15.0 %collective-permute-start.26 = (bf16[128,896]{1,0:T(8,128)(2,1)S(1)}, bf16[128,896]{1,0:T(8,128)(2,1)S(1)}, u32[]{:S(2)}, u32[]{:S(2)}) collective-permute-start(bf16[128,896]{1,0:T(8,128)(2,1)S(1)} %get-tuple-element.27), channel_id=1, source_target_pairs={{0,8},{4,12},{8,0},{12,4},{1,9},{5,13},{9,1},{13,5},{2,10},{6,14},... | collective-permute-start | bytes 688136 | tf_op jit(solution)/shard_map/ppermute | solution.py:380
  146.4 17.3 %collective-permute-start.27 = (bf16[128,896]{1,0:T(8,128)(2,1)S(1)}, bf16[128,896]{1,0:T(8,128)(2,1)S(1)}, u32[]{:S(2)}, u32[]{:S(2)}) collective-permute-start(bf16[128,896]{1,0:T(8,128)(2,1)S(1)} %get-tuple-element.28), channel_id=1, source_target_pairs={{0,12},{4,0},{8,4},{12,8},{1,13},{5,1},{9,5},{13,9},{2,14},{6,2},{... | collective-permute-start | bytes 688136 | tf_op jit(solution)/shard_map/ppermute | solution.py:380
  146.8 16.9 %collective-permute-start.25 = (bf16[128,896]{1,0:T(8,128)(2,1)S(1)}, bf16[128,896]{1,0:T(8,128)(2,1)S(1)}, u32[]{:S(2)}, u32[]{:S(2)}) collective-permute-start(bf16[128,896]{1,0:T(8,128)(2,1)S(1)} %get-tuple-element.29.refs_0_), channel_id=1, source_target_pairs={{0,4},{4,8},{8,12},{12,0},{1,5},{5,9},{9,13},{13,1},{2,6},{6,10},{... | collective-permute-start | bytes 688136 | tf_op jit(solution)/shard_map/ppermute | solution.py:380
  (8 other events, 9.6 us)

commit v3 on v2

--- a/solution.py
+++ b/solution.py
@@ -126,49 +126,6 @@
         copy.wait()
 
 
-def gate_kernel(steps, place, p0, p1, p2, p3, weight, out, whole, buffer, sems, row_sems):
-    rows_in = row_copies(place, (p0, p1, p2, p3), 0, whole.shape[1], whole, row_sems)
-    start_all(rows_in)
-    depth = weight.shape[0] // steps
-    copies = []
-    for i in range(steps):
-        rows = pl.ds(i * depth, depth)
-        copies.append(pltpu.make_async_copy(weight.at[rows], buffer.at[rows], sems.at[i]))
-    start_all(copies)
-    wait_all(rows_in)
-    total = None
-    for i in range(steps):
-        copies[i].wait()
-        part = slice(i * depth, (i + 1) * depth)
-        product = jnp.dot(whole[:, part], buffer[part, :], preferred_element_type=F32)
-        total = product if total is None else total + product
-    out[...] = total
-
-
-def gate_product(place, pieces, weight, after, through, steps=8):
-    rows, depth = pieces[0].shape
-    width = weight.shape[1]
-    return call(
-        functools.partial(gate_kernel, steps),
-        place,
-        (*pieces, weight),
-        [in_hbm()] * 5,
-        [jax.ShapeDtypeStruct((4 * rows, width), F32)],
-        [same((4 * rows, width))],
-        [
-            pltpu.VMEM((4 * rows, depth), BF16),
-            pltpu.VMEM((depth, width), BF16),
-            pltpu.SemaphoreType.DMA((steps,)),
-            pltpu.SemaphoreType.DMA((4 * SEQS,)),
-        ],
-        8 * rows * depth * width,
-        2 * depth * width,
-        "gate",
-        after=after,
-        through=through,
-    )
-
-
 def down_kernel(steps, place, p0, p1, p2, p3, weight, gate, out, whole, buffer, sems, row_sems):
     rows_in = row_copies(place, (p0, p1, p2, p3), 0, whole.shape[1], whole, row_sems)
     start_all(rows_in)
@@ -231,62 +188,92 @@
         out[chip] = jnp.dot(left[...], buffer[chip], preferred_element_type=F32).astype(out.dtype)
 
 
-def share_a_kernel(block, place, p0, p1, p2, p3, basis, send, keep, left, buf0, buf1, sems, row_sems):
-    depth = left.shape[1]
-    start = pl.multiple_of(place[3] * depth, depth)
-    rows_in = row_copies(place, (p0, p1, p2, p3), start, depth, left, row_sems)
-    start_all(rows_in)
+def front_kernel(steps, block, place, p0, p1, p2, p3, weight, basis, gate, send, keep, whole, left, buffer, buf0, buf1, sems, row_sems, left_sems, share_sems):
+    pieces = (p0, p1, p2, p3)
+    depth_a = left.shape[1]
+    start = pl.multiple_of(place[3] * depth_a, depth_a)
+    rows_in = row_copies(place, pieces, start, depth_a, left, left_sems)
+    whole_in = row_copies(place, pieces, 0, whole.shape[1], whole, row_sems)
+    sent = share_copies(place, basis, 1, block, buf0, share_sems.at[0])
+    kept = share_copies(place, basis, 0, block, buf1, share_sems.at[1])
+    depth = weight.shape[0] // steps
+    copies = []
+    for i in range(steps):
+        rows = pl.ds(i * depth, depth)
+        copies.append(pltpu.make_async_copy(weight.at[rows], buffer.at[rows], sems.at[i]))
+    for some in (rows_in, sent, kept, whole_in, copies):
+        start_all(some)
+    wait_all(rows_in)
+    share_products(left, sent, buf0, send)
+    share_products(left, kept, buf1, keep)
+    wait_all(whole_in)
+    total = None
+    for i in range(steps):
+        copies[i].wait()
+        part = slice(i * depth, (i + 1) * depth)
+        product = jnp.dot(whole[:, part], buffer[part, :], preferred_element_type=F32)
+        total = product if total is None else total + product
+    gate[...] = total
+
+
+def front(place, pieces, weight, basis, chips, after, steps=8):
+    rows, depth = pieces[0].shape
+    width = weight.shape[1]
+    depth_a, columns = basis.shape
+    block = columns // (2 * chips)
+    shape = (chips, 4 * rows, block)
+    return call(
+        functools.partial(front_kernel, steps, block),
+        place,
+        (*pieces, weight, basis),
+        [in_hbm()] * 6,
+        [
+            jax.ShapeDtypeStruct((4 * rows, width), F32),
+            jax.ShapeDtypeStruct(shape, BF16),
+            jax.ShapeDtypeStruct(shape, F32),
+        ],
+        [same((4 * rows, width)), same(shape), same(shape)],
+        [
+            pltpu.VMEM((4 * rows, depth), BF16),
+            pltpu.VMEM((4 * rows, depth_a), BF16),
+            pltpu.VMEM((depth, width), BF16),
+            pltpu.VMEM((chips, depth_a, block), BF16),
+            pltpu.VMEM((chips, depth_a, block), BF16),
+            pltpu.SemaphoreType.DMA((steps,)),
+            pltpu.SemaphoreType.DMA((4 * SEQS,)),
+            pltpu.SemaphoreType.DMA((4 * SEQS,)),
+            pltpu.SemaphoreType.DMA((2, chips)),
+        ],
+        8 * rows * (depth * width + depth_a * columns),
+        2 * (depth * width + depth_a * columns),
+        "front",
+        after=after,
+    )
+
+
+def share_g_kernel(block, place, up, basis, send, keep, buf0, buf1, sems):
     sent = share_copies(place, basis, 1, block, buf0, sems.at[0])
     kept = share_copies(place, basis, 0, block, buf1, sems.at[1])
     start_all(sent)
     start_all(kept)
-    wait_all(rows_in)
-    share_products(left, sent, buf0, send)
-    share_products(left, kept, buf1, keep)
-
-
-def share_a(place, pieces, basis, chips, after):
-    rows = pieces[0].shape[0]
-    depth, columns = basis.shape
-    block = columns // (2 * chips)
-    shape = (chips, 4 * rows, block)
-    return call(
-        functools.partial(share_a_kernel, block),
-        place,
-        (*pieces, basis),
-        [in_hbm()] * 5,
-        [jax.ShapeDtypeStruct(shape, BF16), jax.ShapeDtypeStruct(shape, F32)],
-        [same(shape), same(shape)],
-        [pltpu.VMEM((4 * rows, depth), BF16)]
-        + [pltpu.VMEM((chips, depth, block), BF16)] * 2
-        + [pltpu.SemaphoreType.DMA((2, chips)), pltpu.SemaphoreType.DMA((4 * SEQS,))],
-        8 * rows * depth * columns,
-        2 * depth * columns,
-        "share_a",
-        after=after,
-    )
-
-
-def share_g_kernel(flip, block, place, up, basis, out, buffer, sems):
-    copies = share_copies(place, basis, flip, block, buffer, sems)
-    start_all(copies)
-    share_products(up, copies, buffer, out)
-
-
-def share_g(place, up, basis, chips, flip, kind, after, through):
+    share_products(up, sent, buf0, send)
+    share_products(up, kept, buf1, keep)
+
+
+def share_g(place, up, basis, chips, after, through):
     tokens, depth = up.shape
     block = basis.shape[1] // (2 * chips)
     shape = (chips, tokens, block)
     return call(
-        functools.partial(share_g_kernel, flip, block),
+        functools.partial(share_g_kernel, block),
         place,
         (up, basis),
         [same((tokens, depth)), in_hbm()],
-        [jax.ShapeDtypeStruct(shape, kind)],
-        [same(shape)],
-        [pltpu.VMEM((chips, depth, block), BF16), pltpu.SemaphoreType.DMA((chips,))],
-        2 * tokens * depth * chips * block,
-        2 * depth * chips * block,
+        [jax.ShapeDtypeStruct(shape, BF16), jax.ShapeDtypeStruct(shape, F32)],
+        [same(shape), same(shape)],
+        [pltpu.VMEM((chips, depth, block), BF16)] * 2 + [pltpu.SemaphoreType.DMA((2, chips))],
+        4 * tokens * depth * chips * block,
+        4 * depth * chips * block,
         "share_g",
         after=after,
         through=through,
@@ -415,9 +402,13 @@
     return [pick(total, (z + by) % layers).astype(BF16) for by in range(1, layers)], pick(total, z)
 
 
-def reduce_z(sends, keep, layers):
-    for by, send in enumerate(sends, 1):
-        keep = keep + turn(send, "z", layers, by).astype(F32)
+def from_others(sends, layers):
+    return [turn(send, "z", layers, by) for by, send in enumerate(sends, 1)]
+
+
+def summed(keep, got):
+    for one in got:
+        keep = keep + one.astype(F32)
     return keep.astype(BF16)
 
 
@@ -434,23 +425,24 @@
     grad_z = in_order(from_z(masked, layers), z)
     act = flat(over_chip(act_z))
     across = turn(grad_z, "y", 2, 1)
-    send_a, keep_a = share_a(place, act, basis_a, chips, (grad_z,))
-    gate, keep_a = gate_product(place, act, w_gate, (send_a,), (keep_a,))
+    gate, send_a, keep_a = front(place, act, w_gate, basis_a, chips, (grad_z,))
     across = hold(place, across, gate)
+    send_a = hold(place, send_a, across)
     grad = flat((grad_z, across, turn(grad_z, "core", 2, 1), turn(across, "core", 2, 1)))
     send_a, keep_a = for_y(keep_a, turn(send_a, "core", 2, 1), y, layers)
     up, keep_a = down_product(place, grad, w_down, gate, (send_a,), (keep_a,))
-    send_g, keep_a = share_g(place, up, basis_g, chips, 1, BF16, (send_a,), (keep_a,))
     sends_a, own_a = for_z(keep_a, turn(send_a, "y", 2, 1), z, layers)
-    send_g = hold(place, send_g, sends_a[0])
-    keep_g, own_a = share_g(place, up, basis_g, chips, 0, F32, (send_g,), (own_a,))
+    send_g, keep_g, own_a = share_g(place, up, basis_g, chips, (sends_a[0],), (own_a,))
+    own_a = summed(own_a, from_others(sends_a, layers))
+    send_g = hold(place, send_g, own_a)
     send_g, keep_g = for_y(keep_g, turn(send_g, "core", 2, 1), y, layers)
-    own_a = reduce_z(sends_a, hold(place, own_a, send_g), layers)
     pieces_a = from_z(own_a, layers)
     sends_g, own_g = for_z(keep_g, turn(send_g, "y", 2, 1), z, layers)
+    own_g = summed(own_g, from_others(sends_g, layers))
     pieces_a[0] = hold(place, own_a, sends_g[0])
-    proj_a = over_chip(in_order(pieces_a, z))
-    own_g = reduce_z(sends_g, own_g, layers)
+    mine = in_order(pieces_a, z)
+    across = hold(place, turn(mine, "y", 2, 1), own_g)
+    proj_a = mine, across, turn(mine, "core", 2, 1), turn(across, "core", 2, 1)
     return final_product(place, proj_a, own_g, 0, own_g.shape[1], None)
 
 

time: 183 us -> 161 us (0.88)
  Pallas kernels: 62.8 us -> 54.7 us
  waiting for transfers between devices: 55.5 us -> 47.6 us
  other arithmetic: 12.2 us -> 9.13 us
    ppermute x28, waiting for transfers between devices: 55.5 us -> 47.6 us  [turn(): lax.ppermute(value, axis, [(i, (i + by) % size) for i in range(size)])]
    pallas_call x9 -> x8, Pallas kernels: 46.8 us -> 38.9 us  [call(): pl.pallas_call(body, grid_spec=pltpu.PrefetchScalarGridSpec(num_scalar_pr...]
    convert_element_type x1, other arithmetic: 2.07 us -> 0.17 us  [for_y(): return (total(1 - y).astype(BF16), total(y))]
    unnamed x24 -> x14, local copies, waits for them, and re-layouts: 4.22 us -> 3.73 us
  transfers between devices with their start and end apart: 28 -> 28, of which waited for: 10 -> 9; matrix products, arithmetic and copies ran while one was open for 5% -> 5% of each run, Pallas kernels for 20% -> 23%
where the time goes in v3:
time: 161 us; the launch traced here: 160 us
  Pallas kernels  54.7 us (34%)
  waiting for transfers between devices  47.6 us (30%)
  starting transfers between devices  44.2 us (27%)
  other arithmetic  9.13 us (6%)
  local copies, waits for them, and re-layouts  3.9 us (2%)
    ppermute x28, waiting for transfers between devices, turn(): lax.ppermute(value, axis, [(i, (i + by) % size) for i in range(size)])  47.6 us
    ppermute x28, starting transfers between devices, turn(): lax.ppermute(value, axis, [(i, (i + by) % size) for i in range(size)])  44.2 us
    pallas_call x8, Pallas kernels, call(): pl.pallas_call(body, grid_spec=pltpu.PrefetchScalarGridSpec(num_scalar_pr...  38.9 us
    pallas_call x1, Pallas kernels, final_product(): pl.pallas_call(kernel, grid_spec=pltpu.PrefetchScalarGridSpec(num_scalar_...  15.8 us
    unnamed x14, local copies, waits for them, and re-layouts  3.73 us
  transfers between devices with their start and end apart: 28, of which 9 were waited for; matrix products, arithmetic and copies ran while one was open for 5% of the time, Pallas kernels for 23%

profile of v3, /device:TPU:0, one launch (start us, length us, event | category | flops | bytes accessed | tf_op | source)
XLA Modules:
  0.0 160.0 jit_solution(7046127062199228049)
XLA Ops:
  0.0 3.0 %collective-permute-start.3 = (bf16[8,8192]{1,0:T(8,128)(2,1)}, bf16[8,8192]{1,0:T(8,128)(2,1)S(1)}, u32[]{:S(2)}, u32[]{:S(2)}) collective-permute-start(bf16[8,8192]{1,0:T(8,128)(2,1)} %param.7), channel_id=1, source_target_pairs={{0,4},{4,8},{8,12},{12,0},{1,5},{5,9},{9,13},{13,1},{2,6},{6,10},{... | collective-permute-start | bytes 393224 | tf_op jit(solution)/shard_map/ppermute | solution.py:367
  3.0 2.6 %collective-permute-start.4 = (bf16[8,8192]{1,0:T(8,128)(2,1)}, bf16[8,8192]{1,0:T(8,128)(2,1)S(1)}, u32[]{:S(2)}, u32[]{:S(2)}) collective-permute-start(bf16[8,8192]{1,0:T(8,128)(2,1)} %param.7), channel_id=1, source_target_pairs={{0,8},{4,12},{8,0},{12,4},{1,9},{5,13},{9,1},{13,5},{2,10},{6,14},... | collective-permute-start | bytes 393224 | tf_op jit(solution)/shard_map/ppermute | solution.py:367
  5.6 1.3 collective-permute-start.5
  7.6 1.0 broadcast_multiply_fusion
  8.9 2.9 %collective-permute-start.2 = (bf16[8,8192]{1,0:T(8,128)(2,1)S(1)}, bf16[8,8192]{1,0:T(8,128)(2,1)S(1)}, u32[]{:S(2)}, u32[]{:S(2)}) collective-permute-start(bf16[8,8192]{1,0:T(8,128)(2,1)S(1)} %broadcast_multiply_fusion), channel_id=1, source_target_pairs={{0,12},{4,0},{8,4},{12,8},{1,13},{5,1},{9,5},{13,9},{2,14},{6,2},{... | collective-permute-start | bytes 393224 | tf_op jit(solution)/shard_map/ppermute | solution.py:367
  11.7 8.1 %collective-permute-start = (bf16[8,8192]{1,0:T(8,128)(2,1)S(1)}, bf16[8,8192]{1,0:T(8,128)(2,1)S(1)}, u32[]{:S(2)}, u32[]{:S(2)}) collective-permute-start(bf16[8,8192]{1,0:T(8,128)(2,1)S(1)} %broadcast_multiply_fusion), channel_id=1, source_target_pairs={{0,4},{4,8},{8,12},{12,0},{1,5},{5,9},{9,13},{13,1},{2,6},{6,10},{... | collective-permute-start | bytes 393224 | tf_op jit(solution)/shard_map/ppermute | solution.py:367
  19.8 1.0 select_bitcast_fusion.7
  20.9 1.6 collective-permute-start.6
  22.5 3.3 %collective-permute-done.1 = bf16[8,8192]{1,0:T(8,128)(2,1)S(1)} collective-permute-done((bf16[8,8192]{1,0:T(8,128)(2,1)S(1)}, bf16[8,8192]{1,0:T(8,128)(2,1)S(1)}, u32[]{:S(2)}, u32[]{:S(2)}) %collective-permute-start.1) | collective-permute-done | bytes 131104 | tf_op jit(solution)/shard_map/ppermute | solution.py:367
  25.9 4.3 %collective-permute-done.6 = bf16[4,8,8192]{2,1,0:T(8,128)(2,1)S(1)} collective-permute-done((bf16[4,8,8192]{2,1,0:T(8,128)(2,1)S(1)}, bf16[4,8,8192]{2,1,0:T(8,128)(2,1)S(1)}, u32[]{:S(2)}, u32[]{:S(2)}) %collective-permute-start.6) | collective-permute-done | bytes 524320 | tf_op jit(solution)/shard_map/ppermute | solution.py:367
  31.0 1.7 %collective-permute-start.9 = (bf16[4,8,8192]{2,1,0:T(8,128)(2,1)}, bf16[4,8,8192]{2,1,0:T(8,128)(2,1)S(1)}, u32[]{:S(2)}, u32[]{:S(2)}) collective-permute-start(bf16[4,8,8192]{2,1,0:T(8,128)(2,1)} %get-tuple-element.33.refs_6_), channel_id=1, source_target_pairs={{0,2},{2,0},{1,3},{3,1},{4,6},{6,4},{5,7},{7,5},{8,10},{10,8},{9,1... | collective-permute-start | bytes 1572872 | tf_op jit(solution)/shard_map/ppermute | solution.py:367
  32.8 13.1 %front.1 = (f32[128,896]{1,0:T(8,128)S(1)}, bf16[8,128,512]{2,1,0:T(8,128)(2,1)}, f32[8,128,512]{2,1,0:T(8,128)}) custom-call(s32[4]{0:T(128)S(1)} %pad_add_fusion.place, bf16[32,8192]{1,0:T(8,128)(2,1)S(1)} %get-tuple-element.36.refs_0_, bf16[32,8192]{1,0:T(8,128)(2,1)S(1)} %bitcast.105, bf16[32,8192]{1,0:T(8,128)(2,1)} %bitcast.15.refs_2_, ...), custom_call_target="tpu_custom_call" | custom-call | flops 2952790016 | bytes 23068672 | tf_op jit(solution)/shard_map/front/pallas_call | solution.py:77
  48.4 2.1 %collective-permute-done.12 = bf16[8,128,512]{2,1,0:T(8,128)(2,1)} collective-permute-done((bf16[8,128,512]{2,1,0:T(8,128)(2,1)S(1)}, bf16[8,128,512]{2,1,0:T(8,128)(2,1)}, u32[]{:S(2)}, u32[]{:S(2)}) %collective-permute-start.12) | collective-permute-done | bytes 1048608 | tf_op jit(solution)/shard_map/ppermute | solution.py:367
  50.5 3.2 %fusion.3 = (f32[4,128,512]{2,1,0:T(8,128)}, bf16[4,128,512]{2,1,0:T(8,128)(2,1)S(1)}) fusion(f32[4,2,128,512]{3,2,1,0:T(8,128)} %bitcast.108, s32[]{:T(128)S(6)} %select_n.394, bf16[4,2,128,512]{3,2,1,0:T(8,128)(2,1)} %bitcast.21, s32[]{:T(128)S(6)} %select_n.393), kind=kLoop, calls=%fused_computation.6 | loop fusion | flops 1310720 | bytes 4718600 | tf_op jit(solution)/shard_map/add | solution.py:393
  53.7 1.2 collective-permute-start.13
  55.7 11.2 %down.1 = (bf16[128,896]{1,0:T(8,128)(2,1)S(1)}, f32[4,128,512]{2,1,0:T(8,128)}) custom-call(s32[4]{0:T(128)S(1)} %pad_add_fusion.place, bf16[32,8192]{1,0:T(8,128)(2,1)S(1)} %get-tuple-element.34.refs_0_, bf16[32,8192]{1,0:T(8,128)(2,1)S(1)} %bitcast.104, bf16[32,8192]{1,0:T(8,128)(2,1)} %bitcast.111, ...), custom_call_target="tpu_custom_call", output_to_operand_aliasing={{1}: (8, {})} | custom-call | flops 1879048192 | bytes 14680064 | tf_op jit(solution)/shard_map/down/pallas_call | solution.py:77
  67.8 1.4 convert_add_fusion
  69.3 8.1 %collective-permute-start.16 = (bf16[128,512]{1,0:T(8,128)(2,1)S(1)}, bf16[128,512]{1,0:T(8,128)(2,1)S(1)}, u32[]{:S(2)}, u32[]{:S(2)}) collective-permute-start(bf16[128,512]{1,0:T(8,128)(2,1)S(1)} %get-tuple-element.27), channel_id=1, source_target_pairs={{0,12},{4,0},{8,4},{12,8},{1,13},{5,1},{9,5},{13,9},{2,14},{6,2},{... | collective-permute-start | bytes 393224 | tf_op jit(solution)/shard_map/ppermute | solution.py:367
  78.0 11.9 %share_g.1 = (bf16[8,128,896]{2,1,0:T(8,128)(2,1)}, f32[8,128,896]{2,1,0:T(8,128)}, f32[128,512]{1,0:T(8,128)S(1)}) custom-call(s32[4]{0:T(128)S(1)} %pad_add_fusion.place, bf16[128,896]{1,0:T(8,128)(2,1)S(1)} %get-tuple-element.16.refs_0_, bf16[896,14336]{1,0:T(8,128)(2,1)} %refs_1_.1, ...), custom_call_target="tpu_custom_call", output_to_operand_aliasing={{2}: (4, {})} | custom-call | flops 3288334336 | bytes 25690112 | tf_op jit(solution)/shard_map/share_g/pallas_call | solution.py:77
  90.1 1.5 copy-done
  92.2 3.8 %collective-permute-done.17 = bf16[8,128,896]{2,1,0:T(8,128)(2,1)S(1)} collective-permute-done((bf16[8,128,896]{2,1,0:T(8,128)(2,1)S(1)}, bf16[8,128,896]{2,1,0:T(8,128)(2,1)S(1)}, u32[]{:S(2)}, u32[]{:S(2)}) %collective-permute-start.17) | collective-permute-done | bytes 1835040 | tf_op jit(solution)/shard_map/ppermute | solution.py:367
  96.1 1.2 collective-permute-start.18
  97.3 3.2 %collective-permute-start.21 = (bf16[128,512]{1,0:T(8,128)(2,1)S(1)}, bf16[128,512]{1,0:T(8,128)(2,1)S(1)}, u32[]{:S(2)}, u32[]{:S(2)}) collective-permute-start(bf16[128,512]{1,0:T(8,128)(2,1)S(1)} %add_convert_fusion.refs_0_.refs_1_), channel_id=1, source_target_pairs={{0,12},{4,0},{8,4},{12,8},{1,13},{5,1},{9,5},{13,9},{2,14},{6,2},{... | collective-permute-start | bytes 393224 | tf_op jit(solution)/shard_map/ppermute | solution.py:367
  100.5 1.1 collective-permute-start.20
  101.6 17.0 %collective-permute-done.18 = bf16[4,128,896]{2,1,0:T(8,128)(2,1)S(1)} collective-permute-done((bf16[4,128,896]{2,1,0:T(8,128)(2,1)S(1)}, bf16[4,128,896]{2,1,0:T(8,128)(2,1)S(1)}, u32[]{:S(2)}, u32[]{:S(2)}) %collective-permute-start.18) | collective-permute-done | bytes 917536 | tf_op jit(solution)/shard_map/ppermute | solution.py:367
  119.7 1.2 collective-permute-start.25
  120.8 2.3 %collective-permute-start.23 = (bf16[128,896]{1,0:T(8,128)(2,1)S(1)}, bf16[128,896]{1,0:T(8,128)(2,1)S(1)}, u32[]{:S(2)}, u32[]{:S(2)}) collective-permute-start(bf16[128,896]{1,0:T(8,128)(2,1)S(1)} %get-tuple-element.23), channel_id=1, source_target_pairs={{0,8},{4,12},{8,0},{12,4},{1,9},{5,13},{9,1},{13,5},{2,10},{6,14},... | collective-permute-start | bytes 688136 | tf_op jit(solution)/shard_map/ppermute | solution.py:367
  123.1 2.9 %collective-permute-start.24 = (bf16[128,896]{1,0:T(8,128)(2,1)S(1)}, bf16[128,896]{1,0:T(8,128)(2,1)S(1)}, u32[]{:S(2)}, u32[]{:S(2)}) collective-permute-start(bf16[128,896]{1,0:T(8,128)(2,1)S(1)} %get-tuple-element.24), channel_id=1, source_target_pairs={{0,12},{4,0},{8,4},{12,8},{1,13},{5,1},{9,5},{13,9},{2,14},{6,2},{... | collective-permute-start | bytes 688136 | tf_op jit(solution)/shard_map/ppermute | solution.py:367
  126.0 10.8 %collective-permute-done.23 = bf16[128,896]{1,0:T(8,128)(2,1)S(1)} collective-permute-done((bf16[128,896]{1,0:T(8,128)(2,1)S(1)}, bf16[128,896]{1,0:T(8,128)(2,1)S(1)}, u32[]{:S(2)}, u32[]{:S(2)}) %collective-permute-start.23) | collective-permute-done | bytes 229408 | tf_op jit(solution)/shard_map/ppermute | solution.py:367
  136.8 3.7 %collective-permute-done.22 = bf16[128,896]{1,0:T(8,128)(2,1)S(1)} collective-permute-done((bf16[128,896]{1,0:T(8,128)(2,1)S(1)}, bf16[128,896]{1,0:T(8,128)(2,1)S(1)}, u32[]{:S(2)}, u32[]{:S(2)}) %collective-permute-start.22) | collective-permute-done | bytes 229408 | tf_op jit(solution)/shard_map/ppermute | solution.py:367
  141.3 1.9 %collective-permute-done.27.a3 = bf16[4,128,512]{2,1,0:T(8,128)(2,1)S(1)} collective-permute-done((bf16[4,128,512]{2,1,0:T(8,128)(2,1)S(1)}, bf16[4,128,512]{2,1,0:T(8,128)(2,1)S(1)}, u32[]{:S(2)}, u32[]{:S(2)}) %collective-permute-start.27) | collective-permute-done | bytes 524320 | tf_op jit(solution)/shard_map/ppermute | solution.py:367
  144.0 15.8 %final.1 = f32[8192,896]{1,0:T(8,128)} custom-call(s32[4]{0:T(128)S(1)} %pad_add_fusion.place, bf16[4,128,512]{2,1,0:T(8,128)(2,1)S(1)} %pad_maximum_fusion.2.a0, bf16[4,128,512]{2,1,0:T(8,128)(2,1)S(1)} %hold.9.a1, bf16[4,128,512]{2,1,0:T(8,128)(2,1)S(1)} %collective-permute-done.26.a2, bf16[4,128,512]{2,1,0:T(8,128)(2,1)} %copy-done.4, ...), custom_call_target="tpu_custom_call" | custom-call | flops 1879048192 | bytes 29360128 | tf_op jit(solution)/shard_map/final/pallas_call | solution.py:339
  (65 shorter events, 10.4 us)
Async XLA Ops:
  0.0 25.8 %copy-start.6 = (bf16[8,8192]{1,0:T(8,128)(2,1)S(1)}, bf16[8,8192]{1,0:T(8,128)(2,1)}, u32[]{:S(2)}) copy-start(bf16[8,8192]{1,0:T(8,128)(2,1)} %param.8) | copy-start | bytes 393220
  0.0 11.7 %collective-permute-start.3 = (bf16[8,8192]{1,0:T(8,128)(2,1)}, bf16[8,8192]{1,0:T(8,128)(2,1)S(1)}, u32[]{:S(2)}, u32[]{:S(2)}) collective-permute-start(bf16[8,8192]{1,0:T(8,128)(2,1)} %param.7), channel_id=1, source_target_pairs={{0,4},{4,8},{8,12},{12,0},{1,5},{5,9},{9,13},{13,1},{2,6},{6,10},{... | collective-permute-start | bytes 393224 | tf_op jit(solution)/shard_map/ppermute | solution.py:367
  3.0 16.8 %collective-permute-start.4 = (bf16[8,8192]{1,0:T(8,128)(2,1)}, bf16[8,8192]{1,0:T(8,128)(2,1)S(1)}, u32[]{:S(2)}, u32[]{:S(2)}) collective-permute-start(bf16[8,8192]{1,0:T(8,128)(2,1)} %param.7), channel_id=1, source_target_pairs={{0,8},{4,12},{8,0},{12,4},{1,9},{5,13},{9,1},{13,5},{2,10},{6,14},... | collective-permute-start | bytes 393224 | tf_op jit(solution)/shard_map/ppermute | solution.py:367
  5.6 14.2 %collective-permute-start.5 = (bf16[8,8192]{1,0:T(8,128)(2,1)}, bf16[8,8192]{1,0:T(8,128)(2,1)S(1)}, u32[]{:S(2)}, u32[]{:S(2)}) collective-permute-start(bf16[8,8192]{1,0:T(8,128)(2,1)} %param.7), channel_id=1, source_target_pairs={{0,12},{4,0},{8,4},{12,8},{1,13},{5,1},{9,5},{13,9},{2,14},{6,2},{... | collective-permute-start | bytes 393224 | tf_op jit(solution)/shard_map/ppermute | solution.py:367
  8.6 17.1 %collective-permute-start.1 = (bf16[8,8192]{1,0:T(8,128)(2,1)S(1)}, bf16[8,8192]{1,0:T(8,128)(2,1)S(1)}, u32[]{:S(2)}, u32[]{:S(2)}) collective-permute-start(bf16[8,8192]{1,0:T(8,128)(2,1)S(1)} %broadcast_multiply_fusion), channel_id=1, source_target_pairs={{0,8},{4,12},{8,0},{12,4},{1,9},{5,13},{9,1},{13,5},{2,10},{6,14},... | collective-permute-start | bytes 393224 | tf_op jit(solution)/shard_map/ppermute | solution.py:367
  8.9 16.9 %collective-permute-start.2 = (bf16[8,8192]{1,0:T(8,128)(2,1)S(1)}, bf16[8,8192]{1,0:T(8,128)(2,1)S(1)}, u32[]{:S(2)}, u32[]{:S(2)}) collective-permute-start(bf16[8,8192]{1,0:T(8,128)(2,1)S(1)} %broadcast_multiply_fusion), channel_id=1, source_target_pairs={{0,12},{4,0},{8,4},{12,8},{1,13},{5,1},{9,5},{13,9},{2,14},{6,2},{... | collective-permute-start | bytes 393224 | tf_op jit(solution)/shard_map/ppermute | solution.py:367
  11.7 14.0 %collective-permute-start = (bf16[8,8192]{1,0:T(8,128)(2,1)S(1)}, bf16[8,8192]{1,0:T(8,128)(2,1)S(1)}, u32[]{:S(2)}, u32[]{:S(2)}) collective-permute-start(bf16[8,8192]{1,0:T(8,128)(2,1)S(1)} %broadcast_multiply_fusion), channel_id=1, source_target_pairs={{0,4},{4,8},{8,12},{12,0},{1,5},{5,9},{9,13},{13,1},{2,6},{6,10},{... | collective-permute-start | bytes 393224 | tf_op jit(solution)/shard_map/ppermute | solution.py:367
  20.9 9.2 %collective-permute-start.6 = (bf16[4,8,8192]{2,1,0:T(8,128)(2,1)S(1)}, bf16[4,8,8192]{2,1,0:T(8,128)(2,1)S(1)}, u32[]{:S(2)}, u32[]{:S(2)}) collective-permute-start(bf16[4,8,8192]{2,1,0:T(8,128)(2,1)S(1)} %get-tuple-element.35), channel_id=1, source_target_pairs={{0,2},{2,0},{1,3},{3,1},{4,6},{6,4},{5,7},{7,5},{8,10},{10,8},{9,1... | collective-permute-start | bytes 1572872 | tf_op jit(solution)/shard_map/ppermute | solution.py:367
  22.5 10.3 %collective-permute-start.7 = (bf16[4,8,8192]{2,1,0:T(8,128)(2,1)S(1)}, bf16[4,8,8192]{2,1,0:T(8,128)(2,1)}, u32[]{:S(2)}, u32[]{:S(2)}) collective-permute-start(bf16[4,8,8192]{2,1,0:T(8,128)(2,1)S(1)} %get-tuple-element.35), channel_id=1, source_target_pairs={{0,1},{1,0},{2,3},{3,2},{4,5},{5,4},{6,7},{7,6},{8,9},{9,8},{10,11... | collective-permute-start | bytes 1572872 | tf_op jit(solution)/shard_map/ppermute | solution.py:367
  30.1 2.7 %collective-permute-start.8 = (bf16[4,8,8192]{2,1,0:T(8,128)(2,1)S(1)}, bf16[4,8,8192]{2,1,0:T(8,128)(2,1)}, u32[]{:S(2)}, u32[]{:S(2)}) collective-permute-start(bf16[4,8,8192]{2,1,0:T(8,128)(2,1)S(1)} %collective-permute-done.6), channel_id=1, source_target_pairs={{0,1},{1,0},{2,3},{3,2},{4,5},{5,4},{6,7},{7,6},{8,9},{9,8},{10,11... | collective-permute-start | bytes 1572872 | tf_op jit(solution)/shard_map/ppermute | solution.py:367
  31.0 14.8 %collective-permute-start.9 = (bf16[4,8,8192]{2,1,0:T(8,128)(2,1)}, bf16[4,8,8192]{2,1,0:T(8,128)(2,1)S(1)}, u32[]{:S(2)}, u32[]{:S(2)}) collective-permute-start(bf16[4,8,8192]{2,1,0:T(8,128)(2,1)} %get-tuple-element.33.refs_6_), channel_id=1, source_target_pairs={{0,2},{2,0},{1,3},{3,1},{4,6},{6,4},{5,7},{7,5},{8,10},{10,8},{9,1... | collective-permute-start | bytes 1572872 | tf_op jit(solution)/shard_map/ppermute | solution.py:367
  45.9 1.2 copy-start.1
  47.6 2.9 %collective-permute-start.12 = (bf16[8,128,512]{2,1,0:T(8,128)(2,1)S(1)}, bf16[8,128,512]{2,1,0:T(8,128)(2,1)}, u32[]{:S(2)}, u32[]{:S(2)}) collective-permute-start(bf16[8,128,512]{2,1,0:T(8,128)(2,1)S(1)} %hold.6), channel_id=1, source_target_pairs={{0,1},{1,0},{2,3},{3,2},{4,5},{5,4},{6,7},{7,6},{8,9},{9,8},{10,11... | collective-permute-start | bytes 3145736 | tf_op jit(solution)/shard_map/ppermute | solution.py:367
  47.9 7.0 %collective-permute-start.10 = (bf16[4,8,8192]{2,1,0:T(8,128)(2,1)}, bf16[4,8,8192]{2,1,0:T(8,128)(2,1)S(1)}, u32[]{:S(2)}, u32[]{:S(2)}) collective-permute-start(bf16[4,8,8192]{2,1,0:T(8,128)(2,1)} %get-tuple-element.33.refs_6_), channel_id=1, source_target_pairs={{0,1},{1,0},{2,3},{3,2},{4,5},{5,4},{6,7},{7,6},{8,9},{9,8},{10,11... | collective-permute-start | bytes 1572872 | tf_op jit(solution)/shard_map/ppermute | solution.py:367
  48.2 6.7 %collective-permute-start.11 = (bf16[4,8,8192]{2,1,0:T(8,128)(2,1)S(1)}, bf16[4,8,8192]{2,1,0:T(8,128)(2,1)}, u32[]{:S(2)}, u32[]{:S(2)}) collective-permute-start(bf16[4,8,8192]{2,1,0:T(8,128)(2,1)S(1)} %hold.5.refs_0_), channel_id=1, source_target_pairs={{0,1},{1,0},{2,3},{3,2},{4,5},{5,4},{6,7},{7,6},{8,9},{9,8},{10,11... | collective-permute-start | bytes 1572872 | tf_op jit(solution)/shard_map/ppermute | solution.py:367
  53.7 14.1 %collective-permute-start.13 = (bf16[4,128,512]{2,1,0:T(8,128)(2,1)S(1)}, bf16[4,128,512]{2,1,0:T(8,128)(2,1)S(1)}, u32[]{:S(2)}, u32[]{:S(2)}) collective-permute-start(bf16[4,128,512]{2,1,0:T(8,128)(2,1)S(1)} %get-tuple-element.22.refs_6_), channel_id=1, source_target_pairs={{0,2},{2,0},{1,3},{3,1},{4,6},{6,4},{5,7},{7,5},{8,10},{10,8},{9,1... | collective-permute-start | bytes 1572872 | tf_op jit(solution)/shard_map/ppermute | solution.py:367
  69.3 20.7 %collective-permute-start.16 = (bf16[128,512]{1,0:T(8,128)(2,1)S(1)}, bf16[128,512]{1,0:T(8,128)(2,1)S(1)}, u32[]{:S(2)}, u32[]{:S(2)}) collective-permute-start(bf16[128,512]{1,0:T(8,128)(2,1)S(1)} %get-tuple-element.27), channel_id=1, source_target_pairs={{0,12},{4,0},{8,4},{12,8},{1,13},{5,1},{9,5},{13,9},{2,14},{6,2},{... | collective-permute-start | bytes 393224 | tf_op jit(solution)/shard_map/ppermute | solution.py:367
  77.4 12.6 %collective-permute-start.15 = (bf16[128,512]{1,0:T(8,128)(2,1)S(1)}, bf16[128,512]{1,0:T(8,128)(2,1)S(1)}, u32[]{:S(2)}, u32[]{:S(2)}) collective-permute-start(bf16[128,512]{1,0:T(8,128)(2,1)S(1)} %get-tuple-element.28), channel_id=1, source_target_pairs={{0,8},{4,12},{8,0},{12,4},{1,9},{5,13},{9,1},{13,5},{2,10},{6,14},... | collective-permute-start | bytes 393224 | tf_op jit(solution)/shard_map/ppermute | solution.py:367
  77.4 12.6 %collective-permute-start.14 = (bf16[128,512]{1,0:T(8,128)(2,1)S(1)}, bf16[128,512]{1,0:T(8,128)(2,1)S(1)}, u32[]{:S(2)}, u32[]{:S(2)}) collective-permute-start(bf16[128,512]{1,0:T(8,128)(2,1)S(1)} %get-tuple-element.26.refs_2_), channel_id=1, source_target_pairs={{0,4},{4,8},{8,12},{12,0},{1,5},{5,9},{9,13},{13,1},{2,6},{6,10},{... | collective-permute-start | bytes 393224 | tf_op jit(solution)/shard_map/ppermute | solution.py:367
  90.0 1.5 copy-start
  91.6 4.4 %copy-start.2 = (f32[8,128,896]{2,1,0:T(8,128)S(1)}, f32[8,128,896]{2,1,0:T(8,128)}, u32[]{:S(2)}) copy-start(f32[8,128,896]{2,1,0:T(8,128)} %get-tuple-element.18) | copy-start | bytes 11010052
  92.1 3.9 %collective-permute-start.17 = (bf16[8,128,896]{2,1,0:T(8,128)(2,1)S(1)}, bf16[8,128,896]{2,1,0:T(8,128)(2,1)S(1)}, u32[]{:S(2)}, u32[]{:S(2)}) collective-permute-start(bf16[8,128,896]{2,1,0:T(8,128)(2,1)S(1)} %hold.7), channel_id=1, source_target_pairs={{0,1},{1,0},{2,3},{3,2},{4,5},{5,4},{6,7},{7,6},{8,9},{9,8},{10,11... | collective-permute-start | bytes 5505032 | tf_op jit(solution)/shard_map/ppermute | solution.py:367
  96.1 22.5 %collective-permute-start.18 = (bf16[4,128,896]{2,1,0:T(8,128)(2,1)S(1)}, bf16[4,128,896]{2,1,0:T(8,128)(2,1)S(1)}, u32[]{:S(2)}, u32[]{:S(2)}) collective-permute-start(bf16[4,128,896]{2,1,0:T(8,128)(2,1)S(1)} %fusion.5), channel_id=1, source_target_pairs={{0,2},{2,0},{1,3},{3,1},{4,6},{6,4},{5,7},{7,5},{8,10},{10,8},{9,1... | collective-permute-start | bytes 2752520 | tf_op jit(solution)/shard_map/ppermute | solution.py:367
  97.3 21.6 %collective-permute-start.21 = (bf16[128,512]{1,0:T(8,128)(2,1)S(1)}, bf16[128,512]{1,0:T(8,128)(2,1)S(1)}, u32[]{:S(2)}, u32[]{:S(2)}) collective-permute-start(bf16[128,512]{1,0:T(8,128)(2,1)S(1)} %add_convert_fusion.refs_0_.refs_1_), channel_id=1, source_target_pairs={{0,12},{4,0},{8,4},{12,8},{1,13},{5,1},{9,5},{13,9},{2,14},{6,2},{... | collective-permute-start | bytes 393224 | tf_op jit(solution)/shard_map/ppermute | solution.py:367
  100.5 18.5 %collective-permute-start.20 = (bf16[128,512]{1,0:T(8,128)(2,1)S(1)}, bf16[128,512]{1,0:T(8,128)(2,1)S(1)}, u32[]{:S(2)}, u32[]{:S(2)}) collective-permute-start(bf16[128,512]{1,0:T(8,128)(2,1)S(1)} %add_convert_fusion.refs_0_.refs_1_), channel_id=1, source_target_pairs={{0,8},{4,12},{8,0},{12,4},{1,9},{5,13},{9,1},{13,5},{2,10},{6,14},... | collective-permute-start | bytes 393224 | tf_op jit(solution)/shard_map/ppermute | solution.py:367
  101.6 17.4 %collective-permute-start.19 = (bf16[128,512]{1,0:T(8,128)(2,1)S(1)}, bf16[128,512]{1,0:T(8,128)(2,1)S(1)}, u32[]{:S(2)}, u32[]{:S(2)}) collective-permute-start(bf16[128,512]{1,0:T(8,128)(2,1)S(1)} %add_convert_fusion.refs_0_.refs_1_), channel_id=1, source_target_pairs={{0,4},{4,8},{8,12},{12,0},{1,5},{5,9},{9,13},{13,1},{2,6},{6,10},{... | collective-permute-start | bytes 393224 | tf_op jit(solution)/shard_map/ppermute | solution.py:367
  119.7 21.0 %collective-permute-start.25 = (bf16[4,128,512]{2,1,0:T(8,128)(2,1)S(1)}, bf16[4,128,512]{2,1,0:T(8,128)(2,1)S(1)}, u32[]{:S(2)}, u32[]{:S(2)}) collective-permute-start(bf16[4,128,512]{2,1,0:T(8,128)(2,1)S(1)} %pad_maximum_fusion.2.a0), channel_id=1, source_target_pairs={{0,2},{2,0},{1,3},{3,1},{4,6},{6,4},{5,7},{7,5},{8,10},{10,8},{9,1... | collective-permute-start | bytes 1572872 | tf_op jit(solution)/shard_map/ppermute | solution.py:367
  120.8 16.0 %collective-permute-start.23 = (bf16[128,896]{1,0:T(8,128)(2,1)S(1)}, bf16[128,896]{1,0:T(8,128)(2,1)S(1)}, u32[]{:S(2)}, u32[]{:S(2)}) collective-permute-start(bf16[128,896]{1,0:T(8,128)(2,1)S(1)} %get-tuple-element.23), channel_id=1, source_target_pairs={{0,8},{4,12},{8,0},{12,4},{1,9},{5,13},{9,1},{13,5},{2,10},{6,14},... | collective-permute-start | bytes 688136 | tf_op jit(solution)/shard_map/ppermute | solution.py:367
  123.1 13.7 %collective-permute-start.24 = (bf16[128,896]{1,0:T(8,128)(2,1)S(1)}, bf16[128,896]{1,0:T(8,128)(2,1)S(1)}, u32[]{:S(2)}, u32[]{:S(2)}) collective-permute-start(bf16[128,896]{1,0:T(8,128)(2,1)S(1)} %get-tuple-element.24), channel_id=1, source_target_pairs={{0,12},{4,0},{8,4},{12,8},{1,13},{5,1},{9,5},{13,9},{2,14},{6,2},{... | collective-permute-start | bytes 688136 | tf_op jit(solution)/shard_map/ppermute | solution.py:367
  126.0 14.5 %collective-permute-start.22 = (bf16[128,896]{1,0:T(8,128)(2,1)S(1)}, bf16[128,896]{1,0:T(8,128)(2,1)S(1)}, u32[]{:S(2)}, u32[]{:S(2)}) collective-permute-start(bf16[128,896]{1,0:T(8,128)(2,1)S(1)} %get-tuple-element.25.refs_0_), channel_id=1, source_target_pairs={{0,4},{4,8},{8,12},{12,0},{1,5},{5,9},{9,13},{13,1},{2,6},{6,10},{... | collective-permute-start | bytes 688136 | tf_op jit(solution)/shard_map/ppermute | solution.py:367
  126.0 15.2 %collective-permute-start.26 = (bf16[4,128,512]{2,1,0:T(8,128)(2,1)S(1)}, bf16[4,128,512]{2,1,0:T(8,128)(2,1)S(1)}, u32[]{:S(2)}, u32[]{:S(2)}) collective-permute-start(bf16[4,128,512]{2,1,0:T(8,128)(2,1)S(1)} %pad_maximum_fusion.2.a0), channel_id=1, source_target_pairs={{0,1},{1,0},{2,3},{3,2},{4,5},{5,4},{6,7},{7,6},{8,9},{9,8},{10,11... | collective-permute-start | bytes 1572872 | tf_op jit(solution)/shard_map/ppermute | solution.py:367
  141.2 2.0 %collective-permute-start.27 = (bf16[4,128,512]{2,1,0:T(8,128)(2,1)S(1)}, bf16[4,128,512]{2,1,0:T(8,128)(2,1)S(1)}, u32[]{:S(2)}, u32[]{:S(2)}) collective-permute-start(bf16[4,128,512]{2,1,0:T(8,128)(2,1)S(1)} %hold.9.a1), channel_id=1, source_target_pairs={{0,1},{1,0},{2,3},{3,2},{4,5},{5,4},{6,7},{7,6},{8,9},{9,8},{10,11... | collective-permute-start | bytes 1572872 | tf_op jit(solution)/shard_map/ppermute | solution.py:367
  (3 other events, 2.8 us)

commit v4 on v3

--- a/solution.py
+++ b/solution.py
@@ -11,7 +11,7 @@
 SEQS = 2
 F32 = jnp.float32
 BF16 = jnp.bfloat16
-VMEM_LIMIT = 52 * 1024 * 1024
+MIB = 1024 * 1024
 
 
 def plain(activations, out_grad, loss_mask, w_gate, w_down, basis_a, basis_g):
@@ -66,7 +66,7 @@
     return pl.BlockSpec(shape, lambda i, s: (0,) * len(shape))
 
 
-def call(kernel, place, operands, in_specs, outs, out_specs, scratch, flops, moved, name, after=(), through=()):
+def call(kernel, place, operands, in_specs, outs, out_specs, scratch, flops, moved, name, after=(), through=(), limit=52):
     n_in, n_out, n_after, n_through = len(operands), len(outs), len(after), len(through)
     skip = n_in + n_after + n_through
 
@@ -85,14 +85,22 @@
         ),
         out_shape=list(outs) + [jax.ShapeDtypeStruct(t.shape, t.dtype) for t in through],
         input_output_aliases={1 + n_in + n_after + i: n_out + i for i in range(n_through)},
-        compiler_params=pltpu.CompilerParams(vmem_limit_bytes=VMEM_LIMIT),
+        compiler_params=pltpu.CompilerParams(vmem_limit_bytes=limit * MIB),
         cost_estimate=pl.CostEstimate(flops=flops, transcendentals=0, bytes_accessed=moved),
         name=name,
     )(place, *operands, *after, *through)
 
 
-def hold(place, value, *after):
-    return call(lambda place: None, place, (), [], [], [], [], 0, 0, "hold", after, (value,))[0]
+def hold(value, *after):
+    return pl.pallas_call(
+        lambda *refs: None,
+        in_specs=[anywhere()] * (1 + len(after)),
+        out_specs=anywhere(),
+        out_shape=jax.ShapeDtypeStruct(value.shape, value.dtype),
+        input_output_aliases={0: 0},
+        compiler_params=pltpu.CompilerParams(vmem_limit_bytes=MIB),
+        name="hold",
+    )(value, *after)
 
 
 def row_copies(place, pieces, start_column, columns, whole, sems):
@@ -148,14 +156,14 @@
     out[...] = (total * (pre / (1.0 + jnp.exp(-pre)))).astype(out.dtype)
 
 
-def down_product(place, pieces, weight, gate, after, through, steps=8):
+def down_product(place, pieces, weight, gate, after, through, steps=4):
     rows, depth = pieces[0].shape
     width = weight.shape[0]
     return call(
         functools.partial(down_kernel, steps),
         place,
         (*pieces, weight, gate),
-        [in_hbm()] * 5 + [same((4 * rows, width))],
+        [in_hbm()] * 5 + [pl.BlockSpec(memory_space=pltpu.VMEM)],
         [jax.ShapeDtypeStruct((4 * rows, width), BF16)],
         [same((4 * rows, width))],
         [
@@ -268,7 +276,7 @@
         functools.partial(share_g_kernel, block),
         place,
         (up, basis),
-        [same((tokens, depth)), in_hbm()],
+        [pl.BlockSpec(memory_space=pltpu.VMEM), in_hbm()],
         [jax.ShapeDtypeStruct(shape, BF16), jax.ShapeDtypeStruct(shape, F32)],
         [same(shape), same(shape)],
         [pltpu.VMEM((chips, depth, block), BF16)] * 2 + [pltpu.SemaphoreType.DMA((2, chips))],
@@ -277,23 +285,17 @@
         "share_g",
         after=after,
         through=through,
+        limit=40,
     )
 
 
 SLOTS = 8
 
 
-def final_kernel(layers, first, place, a0, a1, a2, a3, g, out, pair, left, stage, sems, in_sems):
-    pieces = (a0, a1, a2, a3)
+def final_kernel(layers, place, a0, a1, a2, a3, g, out, pair, stage, sems):
     tokens, width = g.shape
     seq = tokens // SEQS
     block = stage.shape[1]
-    loads = [
-        pltpu.make_async_copy(pieces[which].at[z], left.at[which * layers + z], in_sems.at[which * layers + z])
-        for which in range(4)
-        for z in range(layers)
-    ]
-    start_all(loads)
     pair[...] = jnp.zeros_like(pair)
     for s in range(SEQS):
         rows = slice(s * seq, (s + 1) * seq)
@@ -304,11 +306,13 @@
         core = (place[2] + which // 2) % 2
         y = (place[1] + which) % 2
         slot = step % SLOTS
-        loads[step].wait()
         if step >= SLOTS:
             copies[step - SLOTS].wait()
         product = lax.dot_general(
-            left[step], pair[...], (((0,), (0,)), ((), ())), preferred_element_type=F32
+            (a0, a1, a2, a3)[which][z],
+            pair[...],
+            (((0,), (0,)), ((), ())),
+            preferred_element_type=F32,
         )
         total = None
         for s in range(SEQS):
@@ -317,50 +321,32 @@
         stage[slot] = total * (1.0 / tokens)
         start = pl.multiple_of(((z * 2 + y) * 2 + core) * block, block)
         copies.append(
-            pltpu.make_async_copy(
-                stage.at[slot],
-                out.at[pl.ds(start, block), pl.ds(first, width)],
-                sems.at[slot],
-            )
+            pltpu.make_async_copy(stage.at[slot], out.at[pl.ds(start, block)], sems.at[slot])
         )
         copies[step].start()
     wait_all(copies[-SLOTS:])
 
 
-def final_product(place, pieces, g, first, columns, before):
+def final_product(place, pieces, g):
     layers, tokens, block = pieces[0].shape
     width = g.shape[1]
-    shape = jax.ShapeDtypeStruct((4 * layers * block, columns), F32)
-
-    def kernel(place, a0, a1, a2, a3, g, *rest):
-        final_kernel(layers, first, place, a0, a1, a2, a3, g, *rest[-6:])
-
-    filled = () if before is None else (before,)
-    return pl.pallas_call(
-        kernel,
-        grid_spec=pltpu.PrefetchScalarGridSpec(
-            num_scalar_prefetch=1,
-            grid=(1,),
-            in_specs=[in_hbm()] * 4 + [same((tokens, width))] + [in_hbm()] * len(filled),
-            out_specs=in_hbm(),
-            scratch_shapes=[
-                pltpu.VMEM((tokens, SEQS * width), BF16),
-                pltpu.VMEM((4 * layers, tokens, block), BF16),
-                pltpu.VMEM((SLOTS, block, width), F32),
-                pltpu.SemaphoreType.DMA((SLOTS,)),
-                pltpu.SemaphoreType.DMA((4 * layers,)),
-            ],
-        ),
-        out_shape=shape,
-        input_output_aliases={6: 0} if filled else {},
-        compiler_params=pltpu.CompilerParams(vmem_limit_bytes=VMEM_LIMIT),
-        cost_estimate=pl.CostEstimate(
-            flops=8 * layers * block * width * tokens,
-            transcendentals=0,
-            bytes_accessed=16 * layers * block * width,
-        ),
-        name="final",
-    )(place, *pieces, g, *filled)
+    return call(
+        functools.partial(final_kernel, layers),
+        place,
+        (*pieces, g),
+        [pl.BlockSpec(memory_space=pltpu.VMEM)] * 5,
+        [jax.ShapeDtypeStruct((4 * layers * block, width), F32)],
+        [in_hbm()],
+        [
+            pltpu.VMEM((tokens, SEQS * width), BF16),
+            pltpu.VMEM((SLOTS, block, width), F32),
+            pltpu.SemaphoreType.DMA((SLOTS,)),
+        ],
+        8 * layers * block * width * tokens,
+        16 * layers * block * width,
+        "final",
+        limit=24,
+    )[0]
 
 
 def turn(value, axis, size, by):
@@ -426,24 +412,24 @@
     act = flat(over_chip(act_z))
     across = turn(grad_z, "y", 2, 1)
     gate, send_a, keep_a = front(place, act, w_gate, basis_a, chips, (grad_z,))
-    across = hold(place, across, gate)
-    send_a = hold(place, send_a, across)
+    across = hold(across, gate)
+    send_a = hold(send_a, across)
     grad = flat((grad_z, across, turn(grad_z, "core", 2, 1), turn(across, "core", 2, 1)))
     send_a, keep_a = for_y(keep_a, turn(send_a, "core", 2, 1), y, layers)
     up, keep_a = down_product(place, grad, w_down, gate, (send_a,), (keep_a,))
     sends_a, own_a = for_z(keep_a, turn(send_a, "y", 2, 1), z, layers)
     send_g, keep_g, own_a = share_g(place, up, basis_g, chips, (sends_a[0],), (own_a,))
     own_a = summed(own_a, from_others(sends_a, layers))
-    send_g = hold(place, send_g, own_a)
+    send_g = hold(send_g, own_a)
     send_g, keep_g = for_y(keep_g, turn(send_g, "core", 2, 1), y, layers)
     pieces_a = from_z(own_a, layers)
     sends_g, own_g = for_z(keep_g, turn(send_g, "y", 2, 1), z, layers)
     own_g = summed(own_g, from_others(sends_g, layers))
-    pieces_a[0] = hold(place, own_a, sends_g[0])
+    pieces_a[0] = hold(own_a, sends_g[0])
     mine = in_order(pieces_a, z)
-    across = hold(place, turn(mine, "y", 2, 1), own_g)
+    across = hold(turn(mine, "y", 2, 1), own_g)
     proj_a = mine, across, turn(mine, "core", 2, 1), turn(across, "core", 2, 1)
-    return final_product(place, proj_a, own_g, 0, own_g.shape[1], None)
+    return final_product(place, proj_a, own_g)
 
 
 def solution(mesh):

time: 161 us -> 150 us (0.932)
  Pallas kernels: 54.7 us -> 45 us
  local copies, waits for them, and re-layouts: 3.9 us -> 2.15 us
    pallas_call x1 -> x5, Pallas kernels: 15.8 us -> 0.01 us  [hold(): pl.pallas_call(lambda *refs: None, in_specs=[anywhere()] * (1 + len(after...]
    pallas_call x8 -> x4, Pallas kernels: 38.9 us -> 45 us  [call(): pl.pallas_call(body, grid_spec=pltpu.PrefetchScalarGridSpec(num_scalar_pr...]
    unnamed x14 -> x8, local copies, waits for them, and re-layouts: 3.73 us -> 1.98 us
  transfers between devices with their start and end apart: 28 -> 28, of which waited for: 9 -> 9; matrix products, arithmetic and copies ran while one was open for 5% -> 5% of each run, Pallas kernels for 23% -> 22%
where the time goes in v4:
time: 150 us; the launch traced here: 149 us
  waiting for transfers between devices  48.9 us (33%)
  Pallas kernels  45 us (30%)
  starting transfers between devices  43.5 us (29%)
  other arithmetic  9.12 us (6%)
  local copies, waits for them, and re-layouts  2.15 us (1%)
    ppermute x28, waiting for transfers between devices, turn(): lax.ppermute(value, axis, [(i, (i + by) % size) for i in range(size)])  48.9 us
    pallas_call x4, Pallas kernels, call(): pl.pallas_call(body, grid_spec=pltpu.PrefetchScalarGridSpec(num_scalar_pr...  45 us
    ppermute x28, starting transfers between devices, turn(): lax.ppermute(value, axis, [(i, (i + by) % size) for i in range(size)])  43.5 us
    add x1, other arithmetic, total(): lax.dynamic_index_in_dim(keep, which, 1, keepdims=False)  3.2 us
  transfers between devices with their start and end apart: 28, of which 9 were waited for; matrix products, arithmetic and copies ran while one was open for 5% of the time, Pallas kernels for 22%

profile of v4, /device:TPU:0, one launch (start us, length us, event | category | flops | bytes accessed | tf_op | source)
XLA Modules:
  0.0 149.2 jit_solution(735281080926358780)
XLA Ops:
  0.0 3.0 %collective-permute-start.4 = (bf16[8,8192]{1,0:T(8,128)(2,1)}, bf16[8,8192]{1,0:T(8,128)(2,1)S(1)}, u32[]{:S(2)}, u32[]{:S(2)}) collective-permute-start(bf16[8,8192]{1,0:T(8,128)(2,1)} %param.7), channel_id=1, source_target_pairs={{0,4},{4,8},{8,12},{12,0},{1,5},{5,9},{9,13},{13,1},{2,6},{6,10},{... | collective-permute-start | bytes 393224 | tf_op jit(solution)/shard_map/ppermute | solution.py:353
  3.0 2.6 %collective-permute-start.5 = (bf16[8,8192]{1,0:T(8,128)(2,1)}, bf16[8,8192]{1,0:T(8,128)(2,1)S(1)}, u32[]{:S(2)}, u32[]{:S(2)}) collective-permute-start(bf16[8,8192]{1,0:T(8,128)(2,1)} %param.7), channel_id=1, source_target_pairs={{0,8},{4,12},{8,0},{12,4},{1,9},{5,13},{9,1},{13,5},{2,10},{6,14},... | collective-permute-start | bytes 393224 | tf_op jit(solution)/shard_map/ppermute | solution.py:353
  5.6 1.3 collective-permute-start.6
  7.6 1.0 broadcast_multiply_fusion
  8.9 2.9 %collective-permute-start.2 = (bf16[8,8192]{1,0:T(8,128)(2,1)S(1)}, bf16[8,8192]{1,0:T(8,128)(2,1)S(1)}, u32[]{:S(2)}, u32[]{:S(2)}) collective-permute-start(bf16[8,8192]{1,0:T(8,128)(2,1)S(1)} %broadcast_multiply_fusion), channel_id=1, source_target_pairs={{0,12},{4,0},{8,4},{12,8},{1,13},{5,1},{9,5},{13,9},{2,14},{6,2},{... | collective-permute-start | bytes 393224 | tf_op jit(solution)/shard_map/ppermute | solution.py:353
  11.7 8.1 %collective-permute-start = (bf16[8,8192]{1,0:T(8,128)(2,1)S(1)}, bf16[8,8192]{1,0:T(8,128)(2,1)S(1)}, u32[]{:S(2)}, u32[]{:S(2)}) collective-permute-start(bf16[8,8192]{1,0:T(8,128)(2,1)S(1)} %broadcast_multiply_fusion), channel_id=1, source_target_pairs={{0,4},{4,8},{8,12},{12,0},{1,5},{5,9},{9,13},{13,1},{2,6},{6,10},{... | collective-permute-start | bytes 393224 | tf_op jit(solution)/shard_map/ppermute | solution.py:353
  19.8 1.0 select_bitcast_fusion.7
  20.9 1.6 %collective-permute-start.7 = (bf16[4,8,8192]{2,1,0:T(8,128)(2,1)S(1)}, bf16[4,8,8192]{2,1,0:T(8,128)(2,1)S(1)}, u32[]{:S(2)}, u32[]{:S(2)}) collective-permute-start(bf16[4,8,8192]{2,1,0:T(8,128)(2,1)S(1)} %get-tuple-element.33), channel_id=1, source_target_pairs={{0,2},{2,0},{1,3},{3,1},{4,6},{6,4},{5,7},{7,5},{8,10},{10,8},{9,1... | collective-permute-start | bytes 1572872 | tf_op jit(solution)/shard_map/ppermute | solution.py:353
  22.5 3.3 %collective-permute-done.1 = bf16[8,8192]{1,0:T(8,128)(2,1)S(1)} collective-permute-done((bf16[8,8192]{1,0:T(8,128)(2,1)S(1)}, bf16[8,8192]{1,0:T(8,128)(2,1)S(1)}, u32[]{:S(2)}, u32[]{:S(2)}) %collective-permute-start.1) | collective-permute-done | bytes 131104 | tf_op jit(solution)/shard_map/ppermute | solution.py:353
  25.9 4.3 %collective-permute-done.7 = bf16[4,8,8192]{2,1,0:T(8,128)(2,1)S(1)} collective-permute-done((bf16[4,8,8192]{2,1,0:T(8,128)(2,1)S(1)}, bf16[4,8,8192]{2,1,0:T(8,128)(2,1)S(1)}, u32[]{:S(2)}, u32[]{:S(2)}) %collective-permute-start.7) | collective-permute-done | bytes 524320 | tf_op jit(solution)/shard_map/ppermute | solution.py:353
  31.0 1.7 %collective-permute-start.3 = (bf16[4,8,8192]{2,1,0:T(8,128)(2,1)}, bf16[4,8,8192]{2,1,0:T(8,128)(2,1)S(1)}, u32[]{:S(2)}, u32[]{:S(2)}) collective-permute-start(bf16[4,8,8192]{2,1,0:T(8,128)(2,1)} %get-tuple-element.39.refs_6_), channel_id=1, source_target_pairs={{0,2},{2,0},{1,3},{3,1},{4,6},{6,4},{5,7},{7,5},{8,10},{10,8},{9,1... | collective-permute-start | bytes 1572872 | tf_op jit(solution)/shard_map/ppermute | solution.py:353
  32.8 13.1 %front.1 = (f32[128,896]{1,0:T(8,128)S(1)}, bf16[8,128,512]{2,1,0:T(8,128)(2,1)}, f32[8,128,512]{2,1,0:T(8,128)}) custom-call(s32[4]{0:T(128)S(1)} %pad_add_fusion.place, bf16[32,8192]{1,0:T(8,128)(2,1)S(1)} %get-tuple-element.34.refs_0_, bf16[32,8192]{1,0:T(8,128)(2,1)S(1)} %bitcast.107, bf16[32,8192]{1,0:T(8,128)(2,1)} %bitcast.15.refs_2_, ...), custom_call_target="tpu_custom_call" | custom-call | flops 2952790016 | bytes 23068672 | tf_op jit(solution)/shard_map/front/pallas_call | solution.py:77
  45.9 1.2 copy-done
  47.8 2.1 %collective-permute-done.12 = bf16[8,128,512]{2,1,0:T(8,128)(2,1)} collective-permute-done((bf16[8,128,512]{2,1,0:T(8,128)(2,1)S(1)}, bf16[8,128,512]{2,1,0:T(8,128)(2,1)}, u32[]{:S(2)}, u32[]{:S(2)}) %collective-permute-start.12) | collective-permute-done | bytes 1048608 | tf_op jit(solution)/shard_map/ppermute | solution.py:353
  49.9 3.2 %fusion.3 = (f32[4,128,512]{2,1,0:T(8,128)}, bf16[4,128,512]{2,1,0:T(8,128)(2,1)S(1)}) fusion(f32[4,2,128,512]{3,2,1,0:T(8,128)} %bitcast.108, s32[]{:T(128)S(6)} %select_n.394, bf16[4,2,128,512]{3,2,1,0:T(8,128)(2,1)} %bitcast.21, s32[]{:T(128)S(6)} %select_n.393), kind=kLoop, calls=%fused_computation.6 | loop fusion | flops 1310720 | bytes 4718600 | tf_op jit(solution)/shard_map/add | solution.py:379
  53.1 1.2 collective-permute-start.13
  55.1 10.5 %down.1 = (bf16[128,896]{1,0:T(8,128)(2,1)S(1)}, f32[4,128,512]{2,1,0:T(8,128)}) custom-call(s32[4]{0:T(128)S(1)} %pad_add_fusion.place, bf16[32,8192]{1,0:T(8,128)(2,1)S(1)} %get-tuple-element.40.refs_0_, bf16[32,8192]{1,0:T(8,128)(2,1)S(1)} %bitcast.104, bf16[32,8192]{1,0:T(8,128)(2,1)} %bitcast.111, ...), custom_call_target="tpu_custom_call", output_to_operand_aliasing={{1}: (8, {})} | custom-call | flops 1879048192 | bytes 14680064 | tf_op jit(solution)/shard_map/down/pallas_call | solution.py:77
  65.6 1.5 %collective-permute-done.13 = bf16[4,128,512]{2,1,0:T(8,128)(2,1)S(1)} collective-permute-done((bf16[4,128,512]{2,1,0:T(8,128)(2,1)S(1)}, bf16[4,128,512]{2,1,0:T(8,128)(2,1)S(1)}, u32[]{:S(2)}, u32[]{:S(2)}) %collective-permute-start.13) | collective-permute-done | bytes 524320 | tf_op jit(solution)/shard_map/ppermute | solution.py:353
  67.1 1.4 convert_add_fusion
  68.6 8.1 %collective-permute-start.16 = (bf16[128,512]{1,0:T(8,128)(2,1)S(1)}, bf16[128,512]{1,0:T(8,128)(2,1)S(1)}, u32[]{:S(2)}, u32[]{:S(2)}) collective-permute-start(bf16[128,512]{1,0:T(8,128)(2,1)S(1)} %get-tuple-element.27), channel_id=1, source_target_pairs={{0,12},{4,0},{8,4},{12,8},{1,13},{5,1},{9,5},{13,9},{2,14},{6,2},{... | collective-permute-start | bytes 393224 | tf_op jit(solution)/shard_map/ppermute | solution.py:353
  77.4 9.6 %share_g.1 = (bf16[8,128,896]{2,1,0:T(8,128)(2,1)S(1)}, f32[8,128,896]{2,1,0:T(8,128)S(1)}, f32[128,512]{1,0:T(8,128)S(1)}) custom-call(s32[4]{0:T(128)S(1)} %pad_add_fusion.place, bf16[128,896]{1,0:T(8,128)(2,1)S(1)} %get-tuple-element.16.refs_0_, bf16[896,14336]{1,0:T(8,128)(2,1)} %refs_1_.1, ...), custom_call_target="tpu_custom_call", output_to_operand_aliasing={{2}: (4, {})} | custom-call | flops 3288334336 | bytes 25690112 | tf_op jit(solution)/shard_map/share_g/pallas_call | solution.py:77
  87.9 3.8 %collective-permute-done.17 = bf16[8,128,896]{2,1,0:T(8,128)(2,1)S(1)} collective-permute-done((bf16[8,128,896]{2,1,0:T(8,128)(2,1)S(1)}, bf16[8,128,896]{2,1,0:T(8,128)(2,1)S(1)}, u32[]{:S(2)}, u32[]{:S(2)}) %collective-permute-start.17) | collective-permute-done | bytes 1835040 | tf_op jit(solution)/shard_map/ppermute | solution.py:353
  91.8 1.2 collective-permute-start.18
  93.0 2.5 %collective-permute-start.21 = (bf16[128,512]{1,0:T(8,128)(2,1)S(1)}, bf16[128,512]{1,0:T(8,128)(2,1)S(1)}, u32[]{:S(2)}, u32[]{:S(2)}) collective-permute-start(bf16[128,512]{1,0:T(8,128)(2,1)S(1)} %add_convert_fusion.refs_1_.refs_0_), channel_id=1, source_target_pairs={{0,12},{4,0},{8,4},{12,8},{1,13},{5,1},{9,5},{13,9},{2,14},{6,2},{... | collective-permute-start | bytes 393224 | tf_op jit(solution)/shard_map/ppermute | solution.py:353
  95.5 1.1 collective-permute-start.20
  97.3 17.0 %collective-permute-done.18 = bf16[4,128,896]{2,1,0:T(8,128)(2,1)S(1)} collective-permute-done((bf16[4,128,896]{2,1,0:T(8,128)(2,1)S(1)}, bf16[4,128,896]{2,1,0:T(8,128)(2,1)S(1)}, u32[]{:S(2)}, u32[]{:S(2)}) %collective-permute-start.18) | collective-permute-done | bytes 917536 | tf_op jit(solution)/shard_map/ppermute | solution.py:353
  114.8 1.2 collective-permute-start.22
  116.0 2.3 %collective-permute-start.24 = (bf16[128,896]{1,0:T(8,128)(2,1)S(1)}, bf16[128,896]{1,0:T(8,128)(2,1)S(1)}, u32[]{:S(2)}, u32[]{:S(2)}) collective-permute-start(bf16[128,896]{1,0:T(8,128)(2,1)S(1)} %get-tuple-element.23), channel_id=1, source_target_pairs={{0,8},{4,12},{8,0},{12,4},{1,9},{5,13},{9,1},{13,5},{2,10},{6,14},... | collective-permute-start | bytes 688136 | tf_op jit(solution)/shard_map/ppermute | solution.py:353
  118.3 2.3 %collective-permute-start.25 = (bf16[128,896]{1,0:T(8,128)(2,1)S(1)}, bf16[128,896]{1,0:T(8,128)(2,1)S(1)}, u32[]{:S(2)}, u32[]{:S(2)}) collective-permute-start(bf16[128,896]{1,0:T(8,128)(2,1)S(1)} %get-tuple-element.24), channel_id=1, source_target_pairs={{0,12},{4,0},{8,4},{12,8},{1,13},{5,1},{9,5},{13,9},{2,14},{6,2},{... | collective-permute-start | bytes 688136 | tf_op jit(solution)/shard_map/ppermute | solution.py:353
  120.6 14.5 %collective-permute-done.24 = bf16[128,896]{1,0:T(8,128)(2,1)S(1)} collective-permute-done((bf16[128,896]{1,0:T(8,128)(2,1)S(1)}, bf16[128,896]{1,0:T(8,128)(2,1)S(1)}, u32[]{:S(2)}, u32[]{:S(2)}) %collective-permute-start.24) | collective-permute-done | bytes 229408 | tf_op jit(solution)/shard_map/ppermute | solution.py:353
  135.3 1.9 %collective-permute-done.27.refs_3_ = bf16[4,128,512]{2,1,0:T(8,128)(2,1)S(1)} collective-permute-done((bf16[4,128,512]{2,1,0:T(8,128)(2,1)S(1)}, bf16[4,128,512]{2,1,0:T(8,128)(2,1)S(1)}, u32[]{:S(2)}, u32[]{:S(2)}) %collective-permute-start.27) | collective-permute-done | bytes 524320 | tf_op jit(solution)/shard_map/ppermute | solution.py:353
  137.2 11.8 %final.1 = f32[8192,896]{1,0:T(8,128)} custom-call(s32[4]{0:T(128)S(1)} %pad_add_fusion.place, bf16[4,128,512]{2,1,0:T(8,128)(2,1)S(1)} %pad_maximum_fusion.2.refs_0_, bf16[4,128,512]{2,1,0:T(8,128)(2,1)S(1)} %hold.9.refs_1_, bf16[4,128,512]{2,1,0:T(8,128)(2,1)S(1)} %collective-permute-done.26.refs_2_, ...), custom_call_target="tpu_custom_call" | custom-call | flops 1879048192 | bytes 29360128 | tf_op jit(solution)/shard_map/final/pallas_call | solution.py:77
  (59 shorter events, 6.6 us)
Async XLA Ops:
  0.0 25.8 %copy-start.3 = (bf16[8,8192]{1,0:T(8,128)(2,1)S(1)}, bf16[8,8192]{1,0:T(8,128)(2,1)}, u32[]{:S(2)}) copy-start(bf16[8,8192]{1,0:T(8,128)(2,1)} %param.8) | copy-start | bytes 393220
  0.0 11.7 %collective-permute-start.4 = (bf16[8,8192]{1,0:T(8,128)(2,1)}, bf16[8,8192]{1,0:T(8,128)(2,1)S(1)}, u32[]{:S(2)}, u32[]{:S(2)}) collective-permute-start(bf16[8,8192]{1,0:T(8,128)(2,1)} %param.7), channel_id=1, source_target_pairs={{0,4},{4,8},{8,12},{12,0},{1,5},{5,9},{9,13},{13,1},{2,6},{6,10},{... | collective-permute-start | bytes 393224 | tf_op jit(solution)/shard_map/ppermute | solution.py:353
  3.0 16.8 %collective-permute-start.5 = (bf16[8,8192]{1,0:T(8,128)(2,1)}, bf16[8,8192]{1,0:T(8,128)(2,1)S(1)}, u32[]{:S(2)}, u32[]{:S(2)}) collective-permute-start(bf16[8,8192]{1,0:T(8,128)(2,1)} %param.7), channel_id=1, source_target_pairs={{0,8},{4,12},{8,0},{12,4},{1,9},{5,13},{9,1},{13,5},{2,10},{6,14},... | collective-permute-start | bytes 393224 | tf_op jit(solution)/shard_map/ppermute | solution.py:353
  5.6 14.2 %collective-permute-start.6 = (bf16[8,8192]{1,0:T(8,128)(2,1)}, bf16[8,8192]{1,0:T(8,128)(2,1)S(1)}, u32[]{:S(2)}, u32[]{:S(2)}) collective-permute-start(bf16[8,8192]{1,0:T(8,128)(2,1)} %param.7), channel_id=1, source_target_pairs={{0,12},{4,0},{8,4},{12,8},{1,13},{5,1},{9,5},{13,9},{2,14},{6,2},{... | collective-permute-start | bytes 393224 | tf_op jit(solution)/shard_map/ppermute | solution.py:353
  8.6 17.1 %collective-permute-start.1 = (bf16[8,8192]{1,0:T(8,128)(2,1)S(1)}, bf16[8,8192]{1,0:T(8,128)(2,1)S(1)}, u32[]{:S(2)}, u32[]{:S(2)}) collective-permute-start(bf16[8,8192]{1,0:T(8,128)(2,1)S(1)} %broadcast_multiply_fusion), channel_id=1, source_target_pairs={{0,8},{4,12},{8,0},{12,4},{1,9},{5,13},{9,1},{13,5},{2,10},{6,14},... | collective-permute-start | bytes 393224 | tf_op jit(solution)/shard_map/ppermute | solution.py:353
  8.9 16.9 %collective-permute-start.2 = (bf16[8,8192]{1,0:T(8,128)(2,1)S(1)}, bf16[8,8192]{1,0:T(8,128)(2,1)S(1)}, u32[]{:S(2)}, u32[]{:S(2)}) collective-permute-start(bf16[8,8192]{1,0:T(8,128)(2,1)S(1)} %broadcast_multiply_fusion), channel_id=1, source_target_pairs={{0,12},{4,0},{8,4},{12,8},{1,13},{5,1},{9,5},{13,9},{2,14},{6,2},{... | collective-permute-start | bytes 393224 | tf_op jit(solution)/shard_map/ppermute | solution.py:353
  11.7 14.0 %collective-permute-start = (bf16[8,8192]{1,0:T(8,128)(2,1)S(1)}, bf16[8,8192]{1,0:T(8,128)(2,1)S(1)}, u32[]{:S(2)}, u32[]{:S(2)}) collective-permute-start(bf16[8,8192]{1,0:T(8,128)(2,1)S(1)} %broadcast_multiply_fusion), channel_id=1, source_target_pairs={{0,4},{4,8},{8,12},{12,0},{1,5},{5,9},{9,13},{13,1},{2,6},{6,10},{... | collective-permute-start | bytes 393224 | tf_op jit(solution)/shard_map/ppermute | solution.py:353
  20.9 9.2 %collective-permute-start.7 = (bf16[4,8,8192]{2,1,0:T(8,128)(2,1)S(1)}, bf16[4,8,8192]{2,1,0:T(8,128)(2,1)S(1)}, u32[]{:S(2)}, u32[]{:S(2)}) collective-permute-start(bf16[4,8,8192]{2,1,0:T(8,128)(2,1)S(1)} %get-tuple-element.33), channel_id=1, source_target_pairs={{0,2},{2,0},{1,3},{3,1},{4,6},{6,4},{5,7},{7,5},{8,10},{10,8},{9,1... | collective-permute-start | bytes 1572872 | tf_op jit(solution)/shard_map/ppermute | solution.py:353
  22.5 10.3 %collective-permute-start.8 = (bf16[4,8,8192]{2,1,0:T(8,128)(2,1)S(1)}, bf16[4,8,8192]{2,1,0:T(8,128)(2,1)}, u32[]{:S(2)}, u32[]{:S(2)}) collective-permute-start(bf16[4,8,8192]{2,1,0:T(8,128)(2,1)S(1)} %get-tuple-element.33), channel_id=1, source_target_pairs={{0,1},{1,0},{2,3},{3,2},{4,5},{5,4},{6,7},{7,6},{8,9},{9,8},{10,11... | collective-permute-start | bytes 1572872 | tf_op jit(solution)/shard_map/ppermute | solution.py:353
  30.1 2.6 %collective-permute-start.9 = (bf16[4,8,8192]{2,1,0:T(8,128)(2,1)S(1)}, bf16[4,8,8192]{2,1,0:T(8,128)(2,1)}, u32[]{:S(2)}, u32[]{:S(2)}) collective-permute-start(bf16[4,8,8192]{2,1,0:T(8,128)(2,1)S(1)} %collective-permute-done.7), channel_id=1, source_target_pairs={{0,1},{1,0},{2,3},{3,2},{4,5},{5,4},{6,7},{7,6},{8,9},{9,8},{10,11... | collective-permute-start | bytes 1572872 | tf_op jit(solution)/shard_map/ppermute | solution.py:353
  31.0 14.8 %collective-permute-start.3 = (bf16[4,8,8192]{2,1,0:T(8,128)(2,1)}, bf16[4,8,8192]{2,1,0:T(8,128)(2,1)S(1)}, u32[]{:S(2)}, u32[]{:S(2)}) collective-permute-start(bf16[4,8,8192]{2,1,0:T(8,128)(2,1)} %get-tuple-element.39.refs_6_), channel_id=1, source_target_pairs={{0,2},{2,0},{1,3},{3,1},{4,6},{6,4},{5,7},{7,5},{8,10},{10,8},{9,1... | collective-permute-start | bytes 1572872 | tf_op jit(solution)/shard_map/ppermute | solution.py:353
  45.9 1.2 copy-start
  47.1 2.8 %collective-permute-start.12 = (bf16[8,128,512]{2,1,0:T(8,128)(2,1)S(1)}, bf16[8,128,512]{2,1,0:T(8,128)(2,1)}, u32[]{:S(2)}, u32[]{:S(2)}) collective-permute-start(bf16[8,128,512]{2,1,0:T(8,128)(2,1)S(1)} %hold.6), channel_id=1, source_target_pairs={{0,1},{1,0},{2,3},{3,2},{4,5},{5,4},{6,7},{7,6},{8,9},{9,8},{10,11... | collective-permute-start | bytes 3145736 | tf_op jit(solution)/shard_map/ppermute | solution.py:353
  47.3 7.0 %collective-permute-start.10 = (bf16[4,8,8192]{2,1,0:T(8,128)(2,1)}, bf16[4,8,8192]{2,1,0:T(8,128)(2,1)S(1)}, u32[]{:S(2)}, u32[]{:S(2)}) collective-permute-start(bf16[4,8,8192]{2,1,0:T(8,128)(2,1)} %get-tuple-element.39.refs_6_), channel_id=1, source_target_pairs={{0,1},{1,0},{2,3},{3,2},{4,5},{5,4},{6,7},{7,6},{8,9},{9,8},{10,11... | collective-permute-start | bytes 1572872 | tf_op jit(solution)/shard_map/ppermute | solution.py:353
  47.6 6.7 %collective-permute-start.11 = (bf16[4,8,8192]{2,1,0:T(8,128)(2,1)S(1)}, bf16[4,8,8192]{2,1,0:T(8,128)(2,1)}, u32[]{:S(2)}, u32[]{:S(2)}) collective-permute-start(bf16[4,8,8192]{2,1,0:T(8,128)(2,1)S(1)} %hold.5.refs_1_), channel_id=1, source_target_pairs={{0,1},{1,0},{2,3},{3,2},{4,5},{5,4},{6,7},{7,6},{8,9},{9,8},{10,11... | collective-permute-start | bytes 1572872 | tf_op jit(solution)/shard_map/ppermute | solution.py:353
  53.1 1.2 copy-start.1
  53.1 14.1 %collective-permute-start.13 = (bf16[4,128,512]{2,1,0:T(8,128)(2,1)S(1)}, bf16[4,128,512]{2,1,0:T(8,128)(2,1)S(1)}, u32[]{:S(2)}, u32[]{:S(2)}) collective-permute-start(bf16[4,128,512]{2,1,0:T(8,128)(2,1)S(1)} %get-tuple-element.22.refs_6_), channel_id=1, source_target_pairs={{0,2},{2,0},{1,3},{3,1},{4,6},{6,4},{5,7},{7,5},{8,10},{10,8},{9,1... | collective-permute-start | bytes 1572872 | tf_op jit(solution)/shard_map/ppermute | solution.py:353
  54.3 0.8 copy-start.2
  68.6 18.4 %collective-permute-start.16 = (bf16[128,512]{1,0:T(8,128)(2,1)S(1)}, bf16[128,512]{1,0:T(8,128)(2,1)S(1)}, u32[]{:S(2)}, u32[]{:S(2)}) collective-permute-start(bf16[128,512]{1,0:T(8,128)(2,1)S(1)} %get-tuple-element.27), channel_id=1, source_target_pairs={{0,12},{4,0},{8,4},{12,8},{1,13},{5,1},{9,5},{13,9},{2,14},{6,2},{... | collective-permute-start | bytes 393224 | tf_op jit(solution)/shard_map/ppermute | solution.py:353
  76.8 10.9 %collective-permute-start.15 = (bf16[128,512]{1,0:T(8,128)(2,1)S(1)}, bf16[128,512]{1,0:T(8,128)(2,1)S(1)}, u32[]{:S(2)}, u32[]{:S(2)}) collective-permute-start(bf16[128,512]{1,0:T(8,128)(2,1)S(1)} %get-tuple-element.28), channel_id=1, source_target_pairs={{0,8},{4,12},{8,0},{12,4},{1,9},{5,13},{9,1},{13,5},{2,10},{6,14},... | collective-permute-start | bytes 393224 | tf_op jit(solution)/shard_map/ppermute | solution.py:353
  76.8 10.9 %collective-permute-start.14 = (bf16[128,512]{1,0:T(8,128)(2,1)S(1)}, bf16[128,512]{1,0:T(8,128)(2,1)S(1)}, u32[]{:S(2)}, u32[]{:S(2)}) collective-permute-start(bf16[128,512]{1,0:T(8,128)(2,1)S(1)} %get-tuple-element.26.refs_2_), channel_id=1, source_target_pairs={{0,4},{4,8},{8,12},{12,0},{1,5},{5,9},{9,13},{13,1},{2,6},{6,10},{... | collective-permute-start | bytes 393224 | tf_op jit(solution)/shard_map/ppermute | solution.py:353
  87.8 3.9 %collective-permute-start.17 = (bf16[8,128,896]{2,1,0:T(8,128)(2,1)S(1)}, bf16[8,128,896]{2,1,0:T(8,128)(2,1)S(1)}, u32[]{:S(2)}, u32[]{:S(2)}) collective-permute-start(bf16[8,128,896]{2,1,0:T(8,128)(2,1)S(1)} %hold.7), channel_id=1, source_target_pairs={{0,1},{1,0},{2,3},{3,2},{4,5},{5,4},{6,7},{7,6},{8,9},{9,8},{10,11... | collective-permute-start | bytes 5505032 | tf_op jit(solution)/shard_map/ppermute | solution.py:353
  91.8 22.5 %collective-permute-start.18 = (bf16[4,128,896]{2,1,0:T(8,128)(2,1)S(1)}, bf16[4,128,896]{2,1,0:T(8,128)(2,1)S(1)}, u32[]{:S(2)}, u32[]{:S(2)}) collective-permute-start(bf16[4,128,896]{2,1,0:T(8,128)(2,1)S(1)} %fusion.5), channel_id=1, source_target_pairs={{0,2},{2,0},{1,3},{3,1},{4,6},{6,4},{5,7},{7,5},{8,10},{10,8},{9,1... | collective-permute-start | bytes 2752520 | tf_op jit(solution)/shard_map/ppermute | solution.py:353
  93.0 21.6 %collective-permute-start.21 = (bf16[128,512]{1,0:T(8,128)(2,1)S(1)}, bf16[128,512]{1,0:T(8,128)(2,1)S(1)}, u32[]{:S(2)}, u32[]{:S(2)}) collective-permute-start(bf16[128,512]{1,0:T(8,128)(2,1)S(1)} %add_convert_fusion.refs_1_.refs_0_), channel_id=1, source_target_pairs={{0,12},{4,0},{8,4},{12,8},{1,13},{5,1},{9,5},{13,9},{2,14},{6,2},{... | collective-permute-start | bytes 393224 | tf_op jit(solution)/shard_map/ppermute | solution.py:353
  95.5 19.1 %collective-permute-start.20 = (bf16[128,512]{1,0:T(8,128)(2,1)S(1)}, bf16[128,512]{1,0:T(8,128)(2,1)S(1)}, u32[]{:S(2)}, u32[]{:S(2)}) collective-permute-start(bf16[128,512]{1,0:T(8,128)(2,1)S(1)} %add_convert_fusion.refs_1_.refs_0_), channel_id=1, source_target_pairs={{0,8},{4,12},{8,0},{12,4},{1,9},{5,13},{9,1},{13,5},{2,10},{6,14},... | collective-permute-start | bytes 393224 | tf_op jit(solution)/shard_map/ppermute | solution.py:353
  96.7 18.0 %collective-permute-start.19 = (bf16[128,512]{1,0:T(8,128)(2,1)S(1)}, bf16[128,512]{1,0:T(8,128)(2,1)S(1)}, u32[]{:S(2)}, u32[]{:S(2)}) collective-permute-start(bf16[128,512]{1,0:T(8,128)(2,1)S(1)} %add_convert_fusion.refs_1_.refs_0_), channel_id=1, source_target_pairs={{0,4},{4,8},{8,12},{12,0},{1,5},{5,9},{9,13},{13,1},{2,6},{6,10},{... | collective-permute-start | bytes 393224 | tf_op jit(solution)/shard_map/ppermute | solution.py:353
  114.8 20.4 %collective-permute-start.22 = (bf16[4,128,512]{2,1,0:T(8,128)(2,1)S(1)}, bf16[4,128,512]{2,1,0:T(8,128)(2,1)S(1)}, u32[]{:S(2)}, u32[]{:S(2)}) collective-permute-start(bf16[4,128,512]{2,1,0:T(8,128)(2,1)S(1)} %pad_maximum_fusion.2.refs_0_), channel_id=1, source_target_pairs={{0,2},{2,0},{1,3},{3,1},{4,6},{6,4},{5,7},{7,5},{8,10},{10,8},{9,1... | collective-permute-start | bytes 1572872 | tf_op jit(solution)/shard_map/ppermute | solution.py:353
  116.0 19.1 %collective-permute-start.24 = (bf16[128,896]{1,0:T(8,128)(2,1)S(1)}, bf16[128,896]{1,0:T(8,128)(2,1)S(1)}, u32[]{:S(2)}, u32[]{:S(2)}) collective-permute-start(bf16[128,896]{1,0:T(8,128)(2,1)S(1)} %get-tuple-element.23), channel_id=1, source_target_pairs={{0,8},{4,12},{8,0},{12,4},{1,9},{5,13},{9,1},{13,5},{2,10},{6,14},... | collective-permute-start | bytes 688136 | tf_op jit(solution)/shard_map/ppermute | solution.py:353
  118.3 16.8 %collective-permute-start.25 = (bf16[128,896]{1,0:T(8,128)(2,1)S(1)}, bf16[128,896]{1,0:T(8,128)(2,1)S(1)}, u32[]{:S(2)}, u32[]{:S(2)}) collective-permute-start(bf16[128,896]{1,0:T(8,128)(2,1)S(1)} %get-tuple-element.24), channel_id=1, source_target_pairs={{0,12},{4,0},{8,4},{12,8},{1,13},{5,1},{9,5},{13,9},{2,14},{6,2},{... | collective-permute-start | bytes 688136 | tf_op jit(solution)/shard_map/ppermute | solution.py:353
  120.6 14.5 %collective-permute-start.23 = (bf16[128,896]{1,0:T(8,128)(2,1)S(1)}, bf16[128,896]{1,0:T(8,128)(2,1)S(1)}, u32[]{:S(2)}, u32[]{:S(2)}) collective-permute-start(bf16[128,896]{1,0:T(8,128)(2,1)S(1)} %get-tuple-element.25.refs_1_), channel_id=1, source_target_pairs={{0,4},{4,8},{8,12},{12,0},{1,5},{5,9},{9,13},{13,1},{2,6},{6,10},{... | collective-permute-start | bytes 688136 | tf_op jit(solution)/shard_map/ppermute | solution.py:353
  120.6 14.7 %collective-permute-start.26 = (bf16[4,128,512]{2,1,0:T(8,128)(2,1)S(1)}, bf16[4,128,512]{2,1,0:T(8,128)(2,1)S(1)}, u32[]{:S(2)}, u32[]{:S(2)}) collective-permute-start(bf16[4,128,512]{2,1,0:T(8,128)(2,1)S(1)} %pad_maximum_fusion.2.refs_0_), channel_id=1, source_target_pairs={{0,1},{1,0},{2,3},{3,2},{4,5},{5,4},{6,7},{7,6},{8,9},{9,8},{10,11... | collective-permute-start | bytes 1572872 | tf_op jit(solution)/shard_map/ppermute | solution.py:353
  135.2 2.0 %collective-permute-start.27 = (bf16[4,128,512]{2,1,0:T(8,128)(2,1)S(1)}, bf16[4,128,512]{2,1,0:T(8,128)(2,1)S(1)}, u32[]{:S(2)}, u32[]{:S(2)}) collective-permute-start(bf16[4,128,512]{2,1,0:T(8,128)(2,1)S(1)} %hold.9.refs_1_), channel_id=1, source_target_pairs={{0,1},{1,0},{2,3},{3,2},{4,5},{5,4},{6,7},{7,6},{8,9},{9,8},{10,11... | collective-permute-start | bytes 1572872 | tf_op jit(solution)/shard_map/ppermute | solution.py:353

commit v5 on v4

--- a/solution.py
+++ b/solution.py
@@ -134,22 +134,16 @@
         copy.wait()
 
 
-def down_kernel(steps, place, p0, p1, p2, p3, weight, gate, out, whole, buffer, sems, row_sems):
+def down_kernel(steps, place, p0, p1, p2, p3, weight, gate, out, whole, row_sems):
     rows_in = row_copies(place, (p0, p1, p2, p3), 0, whole.shape[1], whole, row_sems)
     start_all(rows_in)
+    wait_all(rows_in)
     depth = weight.shape[1] // steps
-    copies = []
-    for i in range(steps):
-        columns = pl.ds(i * depth, depth)
-        copies.append(pltpu.make_async_copy(weight.at[:, columns], buffer.at[:, columns], sems.at[i]))
-    start_all(copies)
-    wait_all(rows_in)
     total = None
     for i in range(steps):
-        copies[i].wait()
         part = slice(i * depth, (i + 1) * depth)
         product = lax.dot_general(
-            whole[:, part], buffer[:, part], (((1,), (1,)), ((), ())), preferred_element_type=F32
+            whole[:, part], weight[:, part], (((1,), (1,)), ((), ())), preferred_element_type=F32
         )
         total = product if total is None else total + product
     pre = gate[...]
@@ -163,20 +157,16 @@
         functools.partial(down_kernel, steps),
         place,
         (*pieces, weight, gate),
-        [in_hbm()] * 5 + [pl.BlockSpec(memory_space=pltpu.VMEM)],
+        [in_hbm()] * 4 + [pl.BlockSpec(memory_space=pltpu.VMEM)] * 2,
         [jax.ShapeDtypeStruct((4 * rows, width), BF16)],
         [same((4 * rows, width))],
-        [
-            pltpu.VMEM((4 * rows, depth), BF16),
-            pltpu.VMEM((width, depth), BF16),
-            pltpu.SemaphoreType.DMA((steps,)),
-            pltpu.SemaphoreType.DMA((4 * SEQS,)),
-        ],
+        [pltpu.VMEM((4 * rows, depth), BF16), pltpu.SemaphoreType.DMA((4 * SEQS,))],
         8 * rows * depth * width,
-        2 * depth * width,
+        2 * rows * depth,
         "down",
         after=after,
         through=through,
+        limit=16,
     )
 
 
@@ -407,6 +397,7 @@
     def flat(stacks):
         return [s.reshape(-1, s.shape[-1]) for s in stacks]
 
+    w_down = pltpu.with_memory_space_constraint(w_down, pltpu.VMEM)
     act_z = in_order(from_z(activations, layers), z)
     grad_z = in_order(from_z(masked, layers), z)
     act = flat(over_chip(act_z))

time: 150 us -> 149 us (level)
  local copies, waits for them, and re-layouts: 2.15 us -> 6.54 us
  Pallas kernels: 45 us -> 41.1 us
    unnamed x8 -> x6, local copies, waits for them, and re-layouts: 1.98 us -> 6.37 us
    pallas_call x4, Pallas kernels: 45 us -> 41 us  [call(): pl.pallas_call(body, grid_spec=pltpu.PrefetchScalarGridSpec(num_scalar_pr...]
  transfers between devices with their start and end apart: 28 -> 28, of which waited for: 9 -> 9; matrix products, arithmetic and copies ran while one was open for 5% -> 4% of each run, Pallas kernels for 22% -> 20%
where the time goes in v5:
time: 149 us; the launch traced here: 148 us
  waiting for transfers between devices  48.6 us (33%)
  starting transfers between devices  43.6 us (29%)
  Pallas kernels  41.1 us (28%)
  other arithmetic  7.9 us (5%)
  local copies, waits for them, and re-layouts  6.54 us (4%)
    ppermute x28, waiting for transfers between devices, turn(): lax.ppermute(value, axis, [(i, (i + by) % size) for i in range(size)])  48.6 us
    ppermute x28, starting transfers between devices, turn(): lax.ppermute(value, axis, [(i, (i + by) % size) for i in range(size)])  43.6 us
    pallas_call x4, Pallas kernels, call(): pl.pallas_call(body, grid_spec=pltpu.PrefetchScalarGridSpec(num_scalar_pr...  41 us
    unnamed x6, local copies, waits for them, and re-layouts  6.37 us
  transfers between devices with their start and end apart: 28, of which 9 were waited for; matrix products, arithmetic and copies ran while one was open for 4% of the time, Pallas kernels for 20%

profile of v5, /device:TPU:0, one launch (start us, length us, event | category | flops | bytes accessed | tf_op | source)
XLA Modules:
  0.0 148.1 jit_solution(9443991308940473155)
XLA Ops:
  0.0 3.0 %collective-permute-start.4 = (bf16[8,8192]{1,0:T(8,128)(2,1)}, bf16[8,8192]{1,0:T(8,128)(2,1)S(1)}, u32[]{:S(2)}, u32[]{:S(2)}) collective-permute-start(bf16[8,8192]{1,0:T(8,128)(2,1)} %param.7), channel_id=1, source_target_pairs={{0,4},{4,8},{8,12},{12,0},{1,5},{5,9},{9,13},{13,1},{2,6},{6,10},{... | collective-permute-start | bytes 393224 | tf_op jit(solution)/shard_map/ppermute | solution.py:343
  3.0 2.6 %collective-permute-start.5 = (bf16[8,8192]{1,0:T(8,128)(2,1)}, bf16[8,8192]{1,0:T(8,128)(2,1)S(1)}, u32[]{:S(2)}, u32[]{:S(2)}) collective-permute-start(bf16[8,8192]{1,0:T(8,128)(2,1)} %param.7), channel_id=1, source_target_pairs={{0,8},{4,12},{8,0},{12,4},{1,9},{5,13},{9,1},{13,5},{2,10},{6,14},... | collective-permute-start | bytes 393224 | tf_op jit(solution)/shard_map/ppermute | solution.py:343
  5.6 1.3 collective-permute-start.6
  7.6 1.0 broadcast_multiply_fusion
  8.9 2.9 %collective-permute-start.2 = (bf16[8,8192]{1,0:T(8,128)(2,1)S(1)}, bf16[8,8192]{1,0:T(8,128)(2,1)S(1)}, u32[]{:S(2)}, u32[]{:S(2)}) collective-permute-start(bf16[8,8192]{1,0:T(8,128)(2,1)S(1)} %broadcast_multiply_fusion), channel_id=1, source_target_pairs={{0,12},{4,0},{8,4},{12,8},{1,13},{5,1},{9,5},{13,9},{2,14},{6,2},{... | collective-permute-start | bytes 393224 | tf_op jit(solution)/shard_map/ppermute | solution.py:343
  11.7 8.1 %collective-permute-start = (bf16[8,8192]{1,0:T(8,128)(2,1)S(1)}, bf16[8,8192]{1,0:T(8,128)(2,1)S(1)}, u32[]{:S(2)}, u32[]{:S(2)}) collective-permute-start(bf16[8,8192]{1,0:T(8,128)(2,1)S(1)} %broadcast_multiply_fusion), channel_id=1, source_target_pairs={{0,4},{4,8},{8,12},{12,0},{1,5},{5,9},{9,13},{13,1},{2,6},{6,10},{... | collective-permute-start | bytes 393224 | tf_op jit(solution)/shard_map/ppermute | solution.py:343
  20.9 1.6 %collective-permute-start.7 = (bf16[4,8,8192]{2,1,0:T(8,128)(2,1)S(1)}, bf16[4,8,8192]{2,1,0:T(8,128)(2,1)S(1)}, u32[]{:S(2)}, u32[]{:S(2)}) collective-permute-start(bf16[4,8,8192]{2,1,0:T(8,128)(2,1)S(1)} %get-tuple-element.33), channel_id=1, source_target_pairs={{0,2},{2,0},{1,3},{3,1},{4,6},{6,4},{5,7},{7,5},{8,10},{10,8},{9,1... | collective-permute-start | bytes 1572872 | tf_op jit(solution)/shard_map/ppermute | solution.py:343
  22.5 3.3 %collective-permute-done.1 = bf16[8,8192]{1,0:T(8,128)(2,1)S(1)} collective-permute-done((bf16[8,8192]{1,0:T(8,128)(2,1)S(1)}, bf16[8,8192]{1,0:T(8,128)(2,1)S(1)}, u32[]{:S(2)}, u32[]{:S(2)}) %collective-permute-start.1) | collective-permute-done | bytes 131104 | tf_op jit(solution)/shard_map/ppermute | solution.py:343
  25.9 4.3 %collective-permute-done.7 = bf16[4,8,8192]{2,1,0:T(8,128)(2,1)S(1)} collective-permute-done((bf16[4,8,8192]{2,1,0:T(8,128)(2,1)S(1)}, bf16[4,8,8192]{2,1,0:T(8,128)(2,1)S(1)}, u32[]{:S(2)}, u32[]{:S(2)}) %collective-permute-start.7) | collective-permute-done | bytes 524320 | tf_op jit(solution)/shard_map/ppermute | solution.py:343
  31.0 1.7 %collective-permute-start.3 = (bf16[4,8,8192]{2,1,0:T(8,128)(2,1)}, bf16[4,8,8192]{2,1,0:T(8,128)(2,1)S(1)}, u32[]{:S(2)}, u32[]{:S(2)}) collective-permute-start(bf16[4,8,8192]{2,1,0:T(8,128)(2,1)} %get-tuple-element.39.refs_6_), channel_id=1, source_target_pairs={{0,2},{2,0},{1,3},{3,1},{4,6},{6,4},{5,7},{7,5},{8,10},{10,8},{9,1... | collective-permute-start | bytes 1572872 | tf_op jit(solution)/shard_map/ppermute | solution.py:343
  32.8 13.1 %front.1 = (f32[128,896]{1,0:T(8,128)S(1)}, bf16[8,128,512]{2,1,0:T(8,128)(2,1)}, f32[8,128,512]{2,1,0:T(8,128)}) custom-call(s32[4]{0:T(128)S(1)} %pad_add_fusion.place, bf16[32,8192]{1,0:T(8,128)(2,1)S(1)} %get-tuple-element.34.refs_0_, bf16[32,8192]{1,0:T(8,128)(2,1)S(1)} %bitcast.107, bf16[32,8192]{1,0:T(8,128)(2,1)} %bitcast.15.refs_2_, ...), custom_call_target="tpu_custom_call" | custom-call | flops 2952790016 | bytes 23068672 | tf_op jit(solution)/shard_map/front/pallas_call | solution.py:77
  45.9 1.2 copy-done.1
  47.8 2.1 %collective-permute-done.12 = bf16[8,128,512]{2,1,0:T(8,128)(2,1)} collective-permute-done((bf16[8,128,512]{2,1,0:T(8,128)(2,1)S(1)}, bf16[8,128,512]{2,1,0:T(8,128)(2,1)}, u32[]{:S(2)}, u32[]{:S(2)}) %collective-permute-start.12) | collective-permute-done | bytes 1048608 | tf_op jit(solution)/shard_map/ppermute | solution.py:343
  49.9 2.2 %fusion.3 = (f32[4,128,512]{2,1,0:T(8,128)S(1)}, bf16[4,128,512]{2,1,0:T(8,128)(2,1)S(1)}) fusion(f32[4,2,128,512]{3,2,1,0:T(8,128)} %bitcast.108, s32[]{:T(128)S(6)} %select_n.394, bf16[4,2,128,512]{3,2,1,0:T(8,128)(2,1)} %bitcast.21, s32[]{:T(128)S(6)} %select_n.393), kind=kLoop, calls=%fused_computation.6 | loop fusion | flops 1310720 | bytes 4718600 | tf_op jit(solution)/shard_map/add | solution.py:369
  52.0 1.3 collective-permute-start.13
  53.3 5.2 %copy-done = bf16[896,8192]{1,0:T(8,128)(2,1)S(1)} copy-done((bf16[896,8192]{1,0:T(8,128)(2,1)S(1)}, bf16[896,8192]{1,0:T(8,128)(2,1)}, u32[]{:S(2)}) %copy-start) | copy-done | bytes 14680088
  58.5 6.6 %down.1 = (bf16[128,896]{1,0:T(8,128)(2,1)S(1)}, f32[4,128,512]{2,1,0:T(8,128)S(1)}) custom-call(s32[4]{0:T(128)S(1)} %pad_add_fusion.place, bf16[32,8192]{1,0:T(8,128)(2,1)S(1)} %get-tuple-element.40.refs_0_, bf16[32,8192]{1,0:T(8,128)(2,1)S(1)} %bitcast.104, bf16[32,8192]{1,0:T(8,128)(2,1)} %bitcast.18.refs_2_, ...), custom_call_target="tpu_custom_call", output_to_operand_aliasing={{1}: (8, {})} | custom-call | flops 1879048192 | bytes 524288 | tf_op jit(solution)/shard_map/down/pallas_call | solution.py:77
  65.1 1.2 collective-permute-done.13
  66.3 1.2 convert_add_fusion
  67.6 8.1 %collective-permute-start.16 = (bf16[128,512]{1,0:T(8,128)(2,1)S(1)}, bf16[128,512]{1,0:T(8,128)(2,1)S(1)}, u32[]{:S(2)}, u32[]{:S(2)}) collective-permute-start(bf16[128,512]{1,0:T(8,128)(2,1)S(1)} %get-tuple-element.27), channel_id=1, source_target_pairs={{0,12},{4,0},{8,4},{12,8},{1,13},{5,1},{9,5},{13,9},{2,14},{6,2},{... | collective-permute-start | bytes 393224 | tf_op jit(solution)/shard_map/ppermute | solution.py:343
  76.4 9.6 %share_g.1 = (bf16[8,128,896]{2,1,0:T(8,128)(2,1)S(1)}, f32[8,128,896]{2,1,0:T(8,128)S(1)}, f32[128,512]{1,0:T(8,128)S(1)}) custom-call(s32[4]{0:T(128)S(1)} %pad_add_fusion.place, bf16[128,896]{1,0:T(8,128)(2,1)S(1)} %get-tuple-element.16.refs_0_, bf16[896,14336]{1,0:T(8,128)(2,1)} %refs_1_.1, ...), custom_call_target="tpu_custom_call", output_to_operand_aliasing={{2}: (4, {})} | custom-call | flops 3288334336 | bytes 25690112 | tf_op jit(solution)/shard_map/share_g/pallas_call | solution.py:77
  86.8 3.8 %collective-permute-done.17 = bf16[8,128,896]{2,1,0:T(8,128)(2,1)S(1)} collective-permute-done((bf16[8,128,896]{2,1,0:T(8,128)(2,1)S(1)}, bf16[8,128,896]{2,1,0:T(8,128)(2,1)S(1)}, u32[]{:S(2)}, u32[]{:S(2)}) %collective-permute-start.17) | collective-permute-done | bytes 1835040 | tf_op jit(solution)/shard_map/ppermute | solution.py:343
  90.8 1.2 collective-permute-start.18
  91.9 2.5 %collective-permute-start.21 = (bf16[128,512]{1,0:T(8,128)(2,1)S(1)}, bf16[128,512]{1,0:T(8,128)(2,1)S(1)}, u32[]{:S(2)}, u32[]{:S(2)}) collective-permute-start(bf16[128,512]{1,0:T(8,128)(2,1)S(1)} %add_convert_fusion.refs_1_.refs_0_), channel_id=1, source_target_pairs={{0,12},{4,0},{8,4},{12,8},{1,13},{5,1},{9,5},{13,9},{2,14},{6,2},{... | collective-permute-start | bytes 393224 | tf_op jit(solution)/shard_map/ppermute | solution.py:343
  94.5 1.1 collective-permute-start.20
  96.2 17.0 %collective-permute-done.18 = bf16[4,128,896]{2,1,0:T(8,128)(2,1)S(1)} collective-permute-done((bf16[4,128,896]{2,1,0:T(8,128)(2,1)S(1)}, bf16[4,128,896]{2,1,0:T(8,128)(2,1)S(1)}, u32[]{:S(2)}, u32[]{:S(2)}) %collective-permute-start.18) | collective-permute-done | bytes 917536 | tf_op jit(solution)/shard_map/ppermute | solution.py:343
  113.8 1.2 collective-permute-start.22
  114.9 2.3 %collective-permute-start.24 = (bf16[128,896]{1,0:T(8,128)(2,1)S(1)}, bf16[128,896]{1,0:T(8,128)(2,1)S(1)}, u32[]{:S(2)}, u32[]{:S(2)}) collective-permute-start(bf16[128,896]{1,0:T(8,128)(2,1)S(1)} %get-tuple-element.23), channel_id=1, source_target_pairs={{0,8},{4,12},{8,0},{12,4},{1,9},{5,13},{9,1},{13,5},{2,10},{6,14},... | collective-permute-start | bytes 688136 | tf_op jit(solution)/shard_map/ppermute | solution.py:343
  117.2 2.3 %collective-permute-start.25 = (bf16[128,896]{1,0:T(8,128)(2,1)S(1)}, bf16[128,896]{1,0:T(8,128)(2,1)S(1)}, u32[]{:S(2)}, u32[]{:S(2)}) collective-permute-start(bf16[128,896]{1,0:T(8,128)(2,1)S(1)} %get-tuple-element.24), channel_id=1, source_target_pairs={{0,12},{4,0},{8,4},{12,8},{1,13},{5,1},{9,5},{13,9},{2,14},{6,2},{... | collective-permute-start | bytes 688136 | tf_op jit(solution)/shard_map/ppermute | solution.py:343
  119.5 14.5 %collective-permute-done.24 = bf16[128,896]{1,0:T(8,128)(2,1)S(1)} collective-permute-done((bf16[128,896]{1,0:T(8,128)(2,1)S(1)}, bf16[128,896]{1,0:T(8,128)(2,1)S(1)}, u32[]{:S(2)}, u32[]{:S(2)}) %collective-permute-start.24) | collective-permute-done | bytes 229408 | tf_op jit(solution)/shard_map/ppermute | solution.py:343
  134.2 1.9 %collective-permute-done.27.refs_3_ = bf16[4,128,512]{2,1,0:T(8,128)(2,1)S(1)} collective-permute-done((bf16[4,128,512]{2,1,0:T(8,128)(2,1)S(1)}, bf16[4,128,512]{2,1,0:T(8,128)(2,1)S(1)}, u32[]{:S(2)}, u32[]{:S(2)}) %collective-permute-start.27) | collective-permute-done | bytes 524320 | tf_op jit(solution)/shard_map/ppermute | solution.py:343
  136.1 11.8 %final.1 = f32[8192,896]{1,0:T(8,128)} custom-call(s32[4]{0:T(128)S(1)} %pad_add_fusion.place, bf16[4,128,512]{2,1,0:T(8,128)(2,1)S(1)} %pad_maximum_fusion.2.refs_0_, bf16[4,128,512]{2,1,0:T(8,128)(2,1)S(1)} %hold.9.refs_1_, bf16[4,128,512]{2,1,0:T(8,128)(2,1)S(1)} %collective-permute-done.26.refs_2_, ...), custom_call_target="tpu_custom_call" | custom-call | flops 1879048192 | bytes 29360128 | tf_op jit(solution)/shard_map/final/pallas_call | solution.py:77
  (57 shorter events, 6.8 us)
Async XLA Ops:
  0.0 25.8 %copy-start.2 = (bf16[8,8192]{1,0:T(8,128)(2,1)S(1)}, bf16[8,8192]{1,0:T(8,128)(2,1)}, u32[]{:S(2)}) copy-start(bf16[8,8192]{1,0:T(8,128)(2,1)} %param.8) | copy-start | bytes 393220
  0.0 11.7 %collective-permute-start.4 = (bf16[8,8192]{1,0:T(8,128)(2,1)}, bf16[8,8192]{1,0:T(8,128)(2,1)S(1)}, u32[]{:S(2)}, u32[]{:S(2)}) collective-permute-start(bf16[8,8192]{1,0:T(8,128)(2,1)} %param.7), channel_id=1, source_target_pairs={{0,4},{4,8},{8,12},{12,0},{1,5},{5,9},{9,13},{13,1},{2,6},{6,10},{... | collective-permute-start | bytes 393224 | tf_op jit(solution)/shard_map/ppermute | solution.py:343
  3.0 16.8 %collective-permute-start.5 = (bf16[8,8192]{1,0:T(8,128)(2,1)}, bf16[8,8192]{1,0:T(8,128)(2,1)S(1)}, u32[]{:S(2)}, u32[]{:S(2)}) collective-permute-start(bf16[8,8192]{1,0:T(8,128)(2,1)} %param.7), channel_id=1, source_target_pairs={{0,8},{4,12},{8,0},{12,4},{1,9},{5,13},{9,1},{13,5},{2,10},{6,14},... | collective-permute-start | bytes 393224 | tf_op jit(solution)/shard_map/ppermute | solution.py:343
  5.6 14.2 %collective-permute-start.6 = (bf16[8,8192]{1,0:T(8,128)(2,1)}, bf16[8,8192]{1,0:T(8,128)(2,1)S(1)}, u32[]{:S(2)}, u32[]{:S(2)}) collective-permute-start(bf16[8,8192]{1,0:T(8,128)(2,1)} %param.7), channel_id=1, source_target_pairs={{0,12},{4,0},{8,4},{12,8},{1,13},{5,1},{9,5},{13,9},{2,14},{6,2},{... | collective-permute-start | bytes 393224 | tf_op jit(solution)/shard_map/ppermute | solution.py:343
  8.6 17.1 %collective-permute-start.1 = (bf16[8,8192]{1,0:T(8,128)(2,1)S(1)}, bf16[8,8192]{1,0:T(8,128)(2,1)S(1)}, u32[]{:S(2)}, u32[]{:S(2)}) collective-permute-start(bf16[8,8192]{1,0:T(8,128)(2,1)S(1)} %broadcast_multiply_fusion), channel_id=1, source_target_pairs={{0,8},{4,12},{8,0},{12,4},{1,9},{5,13},{9,1},{13,5},{2,10},{6,14},... | collective-permute-start | bytes 393224 | tf_op jit(solution)/shard_map/ppermute | solution.py:343
  8.9 16.9 %collective-permute-start.2 = (bf16[8,8192]{1,0:T(8,128)(2,1)S(1)}, bf16[8,8192]{1,0:T(8,128)(2,1)S(1)}, u32[]{:S(2)}, u32[]{:S(2)}) collective-permute-start(bf16[8,8192]{1,0:T(8,128)(2,1)S(1)} %broadcast_multiply_fusion), channel_id=1, source_target_pairs={{0,12},{4,0},{8,4},{12,8},{1,13},{5,1},{9,5},{13,9},{2,14},{6,2},{... | collective-permute-start | bytes 393224 | tf_op jit(solution)/shard_map/ppermute | solution.py:343
  11.7 14.0 %collective-permute-start = (bf16[8,8192]{1,0:T(8,128)(2,1)S(1)}, bf16[8,8192]{1,0:T(8,128)(2,1)S(1)}, u32[]{:S(2)}, u32[]{:S(2)}) collective-permute-start(bf16[8,8192]{1,0:T(8,128)(2,1)S(1)} %broadcast_multiply_fusion), channel_id=1, source_target_pairs={{0,4},{4,8},{8,12},{12,0},{1,5},{5,9},{9,13},{13,1},{2,6},{6,10},{... | collective-permute-start | bytes 393224 | tf_op jit(solution)/shard_map/ppermute | solution.py:343
  20.9 9.2 %collective-permute-start.7 = (bf16[4,8,8192]{2,1,0:T(8,128)(2,1)S(1)}, bf16[4,8,8192]{2,1,0:T(8,128)(2,1)S(1)}, u32[]{:S(2)}, u32[]{:S(2)}) collective-permute-start(bf16[4,8,8192]{2,1,0:T(8,128)(2,1)S(1)} %get-tuple-element.33), channel_id=1, source_target_pairs={{0,2},{2,0},{1,3},{3,1},{4,6},{6,4},{5,7},{7,5},{8,10},{10,8},{9,1... | collective-permute-start | bytes 1572872 | tf_op jit(solution)/shard_map/ppermute | solution.py:343
  22.5 10.3 %collective-permute-start.8 = (bf16[4,8,8192]{2,1,0:T(8,128)(2,1)S(1)}, bf16[4,8,8192]{2,1,0:T(8,128)(2,1)}, u32[]{:S(2)}, u32[]{:S(2)}) collective-permute-start(bf16[4,8,8192]{2,1,0:T(8,128)(2,1)S(1)} %get-tuple-element.33), channel_id=1, source_target_pairs={{0,1},{1,0},{2,3},{3,2},{4,5},{5,4},{6,7},{7,6},{8,9},{9,8},{10,11... | collective-permute-start | bytes 1572872 | tf_op jit(solution)/shard_map/ppermute | solution.py:343
  30.1 2.6 %collective-permute-start.9 = (bf16[4,8,8192]{2,1,0:T(8,128)(2,1)S(1)}, bf16[4,8,8192]{2,1,0:T(8,128)(2,1)}, u32[]{:S(2)}, u32[]{:S(2)}) collective-permute-start(bf16[4,8,8192]{2,1,0:T(8,128)(2,1)S(1)} %collective-permute-done.7), channel_id=1, source_target_pairs={{0,1},{1,0},{2,3},{3,2},{4,5},{5,4},{6,7},{7,6},{8,9},{9,8},{10,11... | collective-permute-start | bytes 1572872 | tf_op jit(solution)/shard_map/ppermute | solution.py:343
  31.0 14.8 %collective-permute-start.3 = (bf16[4,8,8192]{2,1,0:T(8,128)(2,1)}, bf16[4,8,8192]{2,1,0:T(8,128)(2,1)S(1)}, u32[]{:S(2)}, u32[]{:S(2)}) collective-permute-start(bf16[4,8,8192]{2,1,0:T(8,128)(2,1)} %get-tuple-element.39.refs_6_), channel_id=1, source_target_pairs={{0,2},{2,0},{1,3},{3,1},{4,6},{6,4},{5,7},{7,5},{8,10},{10,8},{9,1... | collective-permute-start | bytes 1572872 | tf_op jit(solution)/shard_map/ppermute | solution.py:343
  45.9 1.2 copy-start.1
  47.1 2.8 %collective-permute-start.12 = (bf16[8,128,512]{2,1,0:T(8,128)(2,1)S(1)}, bf16[8,128,512]{2,1,0:T(8,128)(2,1)}, u32[]{:S(2)}, u32[]{:S(2)}) collective-permute-start(bf16[8,128,512]{2,1,0:T(8,128)(2,1)S(1)} %hold.6), channel_id=1, source_target_pairs={{0,1},{1,0},{2,3},{3,2},{4,5},{5,4},{6,7},{7,6},{8,9},{9,8},{10,11... | collective-permute-start | bytes 3145736 | tf_op jit(solution)/shard_map/ppermute | solution.py:343
  47.3 6.0 %collective-permute-start.10 = (bf16[4,8,8192]{2,1,0:T(8,128)(2,1)}, bf16[4,8,8192]{2,1,0:T(8,128)(2,1)}, u32[]{:S(2)}, u32[]{:S(2)}) collective-permute-start(bf16[4,8,8192]{2,1,0:T(8,128)(2,1)} %get-tuple-element.39.refs_6_), channel_id=1, source_target_pairs={{0,1},{1,0},{2,3},{3,2},{4,5},{5,4},{6,7},{7,6},{8,9},{9,8},{10,11... | collective-permute-start | bytes 1572872 | tf_op jit(solution)/shard_map/ppermute | solution.py:343
  47.6 5.7 %collective-permute-start.11 = (bf16[4,8,8192]{2,1,0:T(8,128)(2,1)S(1)}, bf16[4,8,8192]{2,1,0:T(8,128)(2,1)}, u32[]{:S(2)}, u32[]{:S(2)}) collective-permute-start(bf16[4,8,8192]{2,1,0:T(8,128)(2,1)S(1)} %hold.5.refs_1_), channel_id=1, source_target_pairs={{0,1},{1,0},{2,3},{3,2},{4,5},{5,4},{6,7},{7,6},{8,9},{9,8},{10,11... | collective-permute-start | bytes 1572872 | tf_op jit(solution)/shard_map/ppermute | solution.py:343
  52.0 14.2 %collective-permute-start.13 = (bf16[4,128,512]{2,1,0:T(8,128)(2,1)S(1)}, bf16[4,128,512]{2,1,0:T(8,128)(2,1)}, u32[]{:S(2)}, u32[]{:S(2)}) collective-permute-start(bf16[4,128,512]{2,1,0:T(8,128)(2,1)S(1)} %get-tuple-element.22.refs_6_), channel_id=1, source_target_pairs={{0,2},{2,0},{1,3},{3,1},{4,6},{6,4},{5,7},{7,5},{8,10},{10,8},{9,1... | collective-permute-start | bytes 1572872 | tf_op jit(solution)/shard_map/ppermute | solution.py:343
  53.3 5.2 %copy-start = (bf16[896,8192]{1,0:T(8,128)(2,1)S(1)}, bf16[896,8192]{1,0:T(8,128)(2,1)}, u32[]{:S(2)}) copy-start(bf16[896,8192]{1,0:T(8,128)(2,1)} %refs_4_.3) | copy-start | bytes 44040196
  67.6 18.4 %collective-permute-start.16 = (bf16[128,512]{1,0:T(8,128)(2,1)S(1)}, bf16[128,512]{1,0:T(8,128)(2,1)S(1)}, u32[]{:S(2)}, u32[]{:S(2)}) collective-permute-start(bf16[128,512]{1,0:T(8,128)(2,1)S(1)} %get-tuple-element.27), channel_id=1, source_target_pairs={{0,12},{4,0},{8,4},{12,8},{1,13},{5,1},{9,5},{13,9},{2,14},{6,2},{... | collective-permute-start | bytes 393224 | tf_op jit(solution)/shard_map/ppermute | solution.py:343
  75.7 10.9 %collective-permute-start.15 = (bf16[128,512]{1,0:T(8,128)(2,1)S(1)}, bf16[128,512]{1,0:T(8,128)(2,1)S(1)}, u32[]{:S(2)}, u32[]{:S(2)}) collective-permute-start(bf16[128,512]{1,0:T(8,128)(2,1)S(1)} %get-tuple-element.28), channel_id=1, source_target_pairs={{0,8},{4,12},{8,0},{12,4},{1,9},{5,13},{9,1},{13,5},{2,10},{6,14},... | collective-permute-start | bytes 393224 | tf_op jit(solution)/shard_map/ppermute | solution.py:343
  75.7 10.9 %collective-permute-start.14 = (bf16[128,512]{1,0:T(8,128)(2,1)S(1)}, bf16[128,512]{1,0:T(8,128)(2,1)S(1)}, u32[]{:S(2)}, u32[]{:S(2)}) collective-permute-start(bf16[128,512]{1,0:T(8,128)(2,1)S(1)} %get-tuple-element.26.refs_2_), channel_id=1, source_target_pairs={{0,4},{4,8},{8,12},{12,0},{1,5},{5,9},{9,13},{13,1},{2,6},{6,10},{... | collective-permute-start | bytes 393224 | tf_op jit(solution)/shard_map/ppermute | solution.py:343
  86.7 3.9 %collective-permute-start.17 = (bf16[8,128,896]{2,1,0:T(8,128)(2,1)S(1)}, bf16[8,128,896]{2,1,0:T(8,128)(2,1)S(1)}, u32[]{:S(2)}, u32[]{:S(2)}) collective-permute-start(bf16[8,128,896]{2,1,0:T(8,128)(2,1)S(1)} %hold.7), channel_id=1, source_target_pairs={{0,1},{1,0},{2,3},{3,2},{4,5},{5,4},{6,7},{7,6},{8,9},{9,8},{10,11... | collective-permute-start | bytes 5505032 | tf_op jit(solution)/shard_map/ppermute | solution.py:343
  90.8 22.5 %collective-permute-start.18 = (bf16[4,128,896]{2,1,0:T(8,128)(2,1)S(1)}, bf16[4,128,896]{2,1,0:T(8,128)(2,1)S(1)}, u32[]{:S(2)}, u32[]{:S(2)}) collective-permute-start(bf16[4,128,896]{2,1,0:T(8,128)(2,1)S(1)} %fusion.5), channel_id=1, source_target_pairs={{0,2},{2,0},{1,3},{3,1},{4,6},{6,4},{5,7},{7,5},{8,10},{10,8},{9,1... | collective-permute-start | bytes 2752520 | tf_op jit(solution)/shard_map/ppermute | solution.py:343
  91.9 21.6 %collective-permute-start.21 = (bf16[128,512]{1,0:T(8,128)(2,1)S(1)}, bf16[128,512]{1,0:T(8,128)(2,1)S(1)}, u32[]{:S(2)}, u32[]{:S(2)}) collective-permute-start(bf16[128,512]{1,0:T(8,128)(2,1)S(1)} %add_convert_fusion.refs_1_.refs_0_), channel_id=1, source_target_pairs={{0,12},{4,0},{8,4},{12,8},{1,13},{5,1},{9,5},{13,9},{2,14},{6,2},{... | collective-permute-start | bytes 393224 | tf_op jit(solution)/shard_map/ppermute | solution.py:343
  94.5 19.1 %collective-permute-start.20 = (bf16[128,512]{1,0:T(8,128)(2,1)S(1)}, bf16[128,512]{1,0:T(8,128)(2,1)S(1)}, u32[]{:S(2)}, u32[]{:S(2)}) collective-permute-start(bf16[128,512]{1,0:T(8,128)(2,1)S(1)} %add_convert_fusion.refs_1_.refs_0_), channel_id=1, source_target_pairs={{0,8},{4,12},{8,0},{12,4},{1,9},{5,13},{9,1},{13,5},{2,10},{6,14},... | collective-permute-start | bytes 393224 | tf_op jit(solution)/shard_map/ppermute | solution.py:343
  95.6 18.0 %collective-permute-start.19 = (bf16[128,512]{1,0:T(8,128)(2,1)S(1)}, bf16[128,512]{1,0:T(8,128)(2,1)S(1)}, u32[]{:S(2)}, u32[]{:S(2)}) collective-permute-start(bf16[128,512]{1,0:T(8,128)(2,1)S(1)} %add_convert_fusion.refs_1_.refs_0_), channel_id=1, source_target_pairs={{0,4},{4,8},{8,12},{12,0},{1,5},{5,9},{9,13},{13,1},{2,6},{6,10},{... | collective-permute-start | bytes 393224 | tf_op jit(solution)/shard_map/ppermute | solution.py:343
  113.8 20.4 %collective-permute-start.22 = (bf16[4,128,512]{2,1,0:T(8,128)(2,1)S(1)}, bf16[4,128,512]{2,1,0:T(8,128)(2,1)S(1)}, u32[]{:S(2)}, u32[]{:S(2)}) collective-permute-start(bf16[4,128,512]{2,1,0:T(8,128)(2,1)S(1)} %pad_maximum_fusion.2.refs_0_), channel_id=1, source_target_pairs={{0,2},{2,0},{1,3},{3,1},{4,6},{6,4},{5,7},{7,5},{8,10},{10,8},{9,1... | collective-permute-start | bytes 1572872 | tf_op jit(solution)/shard_map/ppermute | solution.py:343
  114.9 19.1 %collective-permute-start.24 = (bf16[128,896]{1,0:T(8,128)(2,1)S(1)}, bf16[128,896]{1,0:T(8,128)(2,1)S(1)}, u32[]{:S(2)}, u32[]{:S(2)}) collective-permute-start(bf16[128,896]{1,0:T(8,128)(2,1)S(1)} %get-tuple-element.23), channel_id=1, source_target_pairs={{0,8},{4,12},{8,0},{12,4},{1,9},{5,13},{9,1},{13,5},{2,10},{6,14},... | collective-permute-start | bytes 688136 | tf_op jit(solution)/shard_map/ppermute | solution.py:343
  117.2 16.8 %collective-permute-start.25 = (bf16[128,896]{1,0:T(8,128)(2,1)S(1)}, bf16[128,896]{1,0:T(8,128)(2,1)S(1)}, u32[]{:S(2)}, u32[]{:S(2)}) collective-permute-start(bf16[128,896]{1,0:T(8,128)(2,1)S(1)} %get-tuple-element.24), channel_id=1, source_target_pairs={{0,12},{4,0},{8,4},{12,8},{1,13},{5,1},{9,5},{13,9},{2,14},{6,2},{... | collective-permute-start | bytes 688136 | tf_op jit(solution)/shard_map/ppermute | solution.py:343
  119.5 14.5 %collective-permute-start.23 = (bf16[128,896]{1,0:T(8,128)(2,1)S(1)}, bf16[128,896]{1,0:T(8,128)(2,1)S(1)}, u32[]{:S(2)}, u32[]{:S(2)}) collective-permute-start(bf16[128,896]{1,0:T(8,128)(2,1)S(1)} %get-tuple-element.25.refs_1_), channel_id=1, source_target_pairs={{0,4},{4,8},{8,12},{12,0},{1,5},{5,9},{9,13},{13,1},{2,6},{6,10},{... | collective-permute-start | bytes 688136 | tf_op jit(solution)/shard_map/ppermute | solution.py:343
  119.5 14.7 %collective-permute-start.26 = (bf16[4,128,512]{2,1,0:T(8,128)(2,1)S(1)}, bf16[4,128,512]{2,1,0:T(8,128)(2,1)S(1)}, u32[]{:S(2)}, u32[]{:S(2)}) collective-permute-start(bf16[4,128,512]{2,1,0:T(8,128)(2,1)S(1)} %pad_maximum_fusion.2.refs_0_), channel_id=1, source_target_pairs={{0,1},{1,0},{2,3},{3,2},{4,5},{5,4},{6,7},{7,6},{8,9},{9,8},{10,11... | collective-permute-start | bytes 1572872 | tf_op jit(solution)/shard_map/ppermute | solution.py:343
  134.1 2.0 %collective-permute-start.27 = (bf16[4,128,512]{2,1,0:T(8,128)(2,1)S(1)}, bf16[4,128,512]{2,1,0:T(8,128)(2,1)S(1)}, u32[]{:S(2)}, u32[]{:S(2)}) collective-permute-start(bf16[4,128,512]{2,1,0:T(8,128)(2,1)S(1)} %hold.9.refs_1_), channel_id=1, source_target_pairs={{0,1},{1,0},{2,3},{3,2},{4,5},{5,4},{6,7},{7,6},{8,9},{9,8},{10,11... | collective-permute-start | bytes 1572872 | tf_op jit(solution)/shard_map/ppermute | solution.py:343
